TPU v7x, 128 devices: a whole 4x4x4 slice. The times are simulated.
128 devices in a mesh: dom: 128 (over x, z, y, core).
Axes of the slice: x: 4, y: 4, z: 4, core: 2. Of those that a mesh axis runs over, the one named last changes fastest.
Arguments:
- feats: bfloat16 [262144, 256], P('dom'), may hold values from -6 to 6
- hub_feat: bfloat16 [16384, 256], P('dom'), may hold values from -6 to 6
- weight: bfloat16 [512, 256], replicated, may hold values from -0.25 to 0.25
- bias: float32 [256], replicated, may hold values from -4 to 4
- loc_nbr: int32 [262144, 16], P('dom'), may hold values from 0 to 2047
- loc_len: int32 [262144], P('dom'), may hold values from 1 to 16
- hub_nbr: int32 [262144, 8], P('dom'), may hold values from 0 to 16383
- hub_len: int32 [262144], P('dom'), may hold values from 0 to 8
- send_list: int32 [16384, 64], P('dom'), may hold values from 0 to 2047
- halo_nbr: int32 [262144, 8], P('dom'), may hold values from 0 to 8191
- halo_len: int32 [262144], P('dom'), may hold values from 0 to 8
Outputs:
- layer_out: bfloat16 [262144, 256], P('dom')
All inputs are finite; a program needn't handle non-finite values.
Results may differ from a plain program's by a relative error of at most 0.0016.
Values may be sent and summed in bfloat16 or wider, within the bound.
No kernel may reach another device: no remote copies, remote signals or barrier semaphores. Data moves between devices by JAX's collectives and lax.ppermute only.
A program may use at most 128 MiB of HBM per device.

v0:
```python
import jax
import jax.numpy as jnp
from jax import lax
from jax.sharding import PartitionSpec as P


def masked_sum(rows, length):
    mask = jnp.arange(rows.shape[1], dtype=jnp.int32)[None, :] < length[:, None]
    return jnp.sum(rows.astype(jnp.float32) * mask[:, :, None].astype(jnp.float32), axis=1)


def per_device(
    feats, hub_feat, weight, bias, loc_nbr, loc_len, hub_nbr, hub_len, send_list, halo_nbr, halo_len
):
    rows_here, width = feats.shape
    peers = lax.axis_size("dom")
    slots = send_list.shape[1]
    outgoing = feats[send_list]
    arrived = lax.all_to_all(outgoing, "dom", split_axis=0, concat_axis=0, tiled=True)
    arrived = arrived.reshape(peers * slots, width)
    loc_sum = masked_sum(feats[loc_nbr], loc_len)
    halo_sum = masked_sum(arrived[halo_nbr], halo_len)
    whole_hubs = lax.all_gather(hub_feat, "dom", axis=0, tiled=True)
    hub_sum = masked_sum(whole_hubs[hub_nbr], hub_len)
    degree = (loc_len + hub_len + halo_len).astype(jnp.float32)
    agg = ((loc_sum + hub_sum + halo_sum) / degree[:, None]).astype(jnp.bfloat16)
    joined = jnp.concatenate([feats, agg], axis=1)
    result = jnp.dot(joined, weight, preferred_element_type=jnp.float32) + bias
    return jnp.maximum(result, 0.0).astype(jnp.bfloat16)


def solution(mesh):
    placed = (
        P("dom", None),
        P("dom", None),
        P(),
        P(),
        P("dom", None),
        P("dom"),
        P("dom", None),
        P("dom"),
        P("dom", None),
        P("dom", None),
        P("dom"),
    )
    return jax.shard_map(
        per_device, mesh=mesh, in_specs=placed, out_specs=P("dom", None), check_vma=False
    )
```

profile of v0, /device:TPU:1, one launch (start us, length us, event | category | flops | bytes accessed | tf_op | source)
XLA Modules:
  0.0 367.2 jit_solution(3301954519009317720)
XLA Ops:
  6.5 0.0 copy-start
  6.5 0.0 all-gather.2.cloned.1.call-start
  6.5 0.7 all-gather.2.cloned.1.call-update
  7.3 0.8 compare_select_fusion.3
  8.0 0.1 copy.14
  8.1 0.1 reshape.93
  8.2 32.5 %gather_fusion.2 = bf16[8192,256]{1,0:T(8,128)(2,1)} fusion(bf16[2048,256]{1,0:T(8,128)(2,1)} %param.11, s32[8192]{0:T(1024)S(1)} %broadcast_clamp_fusion.3), kind=kCustom, calls=%fused_computation.2 | custom fusion | bytes 8421376 | tf_op jit(solution)/shard_map/gather | solution.py:18
  40.7 0.0 copy-start.3
  40.7 0.0 copy-start.1
  40.7 12.0 %all-to-all-start = ((bf16[128,64,256]{2,1,0:T(8,128)(2,1)}), bf16[128,64,256]{2,1,0:T(8,128)(2,1)}, u32[]{:S(2)}, u32[]{:S(2)}) async-start(bf16[128,64,256]{2,1,0:T(8,128)(2,1)} %bitcast.12), calls=%async_computation | async-start | bytes 8388608 | tf_op jit(solution)/shard_map/all_to_all | solution.py:19
  52.6 0.0 copy-done.3
  52.7 0.3 copy.12
  53.0 0.3 reshape.77
  53.3 0.0 copy-done.1
  53.4 0.0 copy-start.4
  53.4 0.0 copy-start.5
  53.4 129.4 %gather_fusion = bf16[32768,256]{1,0:T(8,128)(2,1)} fusion(bf16[2048,256]{1,0:T(8,128)(2,1)S(1)} %copy-done.1, s32[32768]{0:T(1024)S(1)} %broadcast_clamp_fusion), kind=kCustom, calls=%fused_computation | custom fusion | bytes 33685504 | tf_op jit(solution)/shard_map/gather | solution.py:21
  182.8 0.0 copy-done.4
  182.8 0.0 copy-start.6
  182.8 0.0 copy-start.7
  182.8 0.0 copy-start.8
  182.8 0.3 copy.15
  183.2 0.5 reshape.101
  183.7 0.0 copy-done.5
  183.7 0.3 copy.13
  184.0 0.5 reshape.85
  184.5 0.0 copy-done.6
  184.5 0.0 copy-done.7
  184.6 0.0 copy-done.8
  184.6 0.3 fusion.8
  185.0 1.3 fusion.10
  186.3 1.3 fusion.9
  187.6 13.6 %fusion = f32[2048,256]{1,0:T(8,128)S(1)} fusion(f32[2048,16]{1,0:T(8,128)S(1)} %fusion.8, bf16[32768,256]{1,0:T(8,128)(2,1)} %gather_fusion), kind=kLoop, calls=%fused_computation.5 | loop fusion | flops 24641536 | bytes 19005440 | tf_op jit(solution)/shard_map/reduce_sum | solution.py:9
  201.2 0.0 all-to-all-done
  201.2 63.9 %gather_fusion.3 = bf16[16384,256]{1,0:T(8,128)(2,1)} fusion(bf16[8192,256]{1,0:T(8,128)(2,1)} %bitcast.3, s32[16384]{0:T(1024)S(1)} %broadcast_clamp_fusion.1), kind=kCustom, calls=%fused_computation.3 | custom fusion | bytes 16842752 | tf_op jit(solution)/shard_map/gather | solution.py:22
  265.1 14.1 %fusion.1 = f32[2048,256]{1,0:T(8,128)} fusion(bf16[16384,256]{1,0:T(8,128)(2,1)} %gather_fusion.3, f32[2048,8]{1,0:T(8,128)} %fusion.10), kind=kLoop, calls=%fused_computation.7 | loop fusion | flops 12058624 | bytes 10551296 | tf_op jit(solution)/shard_map/reduce_sum | solution.py:9
  279.3 0.0 all-gather.2.cloned.1.call-done
  279.3 65.6 %gather_fusion.1 = bf16[16384,256]{1,0:T(8,128)(2,1)} fusion(bf16[16384,256]{1,0:T(8,128)(2,1)} %all-gather.2.cloned.1.call-done, s32[16384]{0:T(1024)S(1)} %broadcast_clamp_fusion.2), kind=kCustom, calls=%fused_computation.1 | custom fusion | bytes 16842752 | tf_op jit(solution)/shard_map/gather | solution.py:24
  344.9 0.0 copy-start.2
  344.9 13.1 %fusion.2 = f32[2048,256]{1,0:T(8,128)S(1)} fusion(bf16[16384,256]{1,0:T(8,128)(2,1)} %gather_fusion.1, f32[2048,8]{1,0:T(8,128)} %fusion.9), kind=kLoop, calls=%fused_computation.9 | loop fusion | flops 12058624 | bytes 10551296 | tf_op jit(solution)/shard_map/reduce_sum | solution.py:9
  358.0 0.0 copy-done.2
  358.0 0.0 copy-start.9
  358.0 0.4 divide_convert_fusion
  358.5 0.0 copy-done
  358.5 0.2 copy-done.9
  358.7 1.7 fusion.4
  (8 shorter events, 0.1 us)
Async XLA Ops:
  6.5 351.9 %copy-start = (bf16[512,256]{1,0:T(8,128)(2,1)S(1)}, bf16[512,256]{1,0:T(8,128)(2,1)}, u32[]{:S(2)}) copy-start(bf16[512,256]{1,0:T(8,128)(2,1)} %param.13) | copy-start | bytes 786436
  6.5 272.7 %all-gather.2.cloned.1.call-start = ((), (), s32[]{:S(2)}) async-start(), calls=%async_computation.1 | async-start | bytes 8454144 | tf_op jit(solution)/shard_map/all_gather | solution.py:23
  40.7 12.0 %copy-start.3 = (s32[2048,16]{0,1:T(8,128)S(1)}, s32[2048,16]{0,1:T(8,128)}, u32[]{:S(2)}) copy-start(s32[2048,16]{0,1:T(8,128)} %param.15) | copy-start | bytes 393220
  40.7 12.7 %copy-start.1 = (bf16[2048,256]{1,0:T(8,128)(2,1)S(1)}, bf16[2048,256]{1,0:T(8,128)(2,1)}, u32[]{:S(2)}) copy-start(bf16[2048,256]{1,0:T(8,128)(2,1)} %param.11) | copy-start | bytes 3145732
  40.7 160.6 %all-to-all-start = ((bf16[128,64,256]{2,1,0:T(8,128)(2,1)}), bf16[128,64,256]{2,1,0:T(8,128)(2,1)}, u32[]{:S(2)}, u32[]{:S(2)}) async-start(bf16[128,64,256]{2,1,0:T(8,128)(2,1)} %bitcast.12), calls=%async_computation | async-start | bytes 8388608 | tf_op jit(solution)/shard_map/all_to_all | solution.py:19
  53.4 129.4 %copy-start.4 = (s32[2048,8]{0,1:T(8,128)S(1)}, s32[2048,8]{0,1:T(8,128)}, u32[]{:S(2)}) copy-start(s32[2048,8]{0,1:T(8,128)} %param.20) | copy-start | bytes 196612
  53.4 130.3 %copy-start.5 = (s32[2048,8]{0,1:T(8,128)S(1)}, s32[2048,8]{0,1:T(8,128)}, u32[]{:S(2)}) copy-start(s32[2048,8]{0,1:T(8,128)} %param.17) | copy-start | bytes 196612
  182.8 1.7 copy-start.6
  182.8 1.7 copy-start.7
  182.8 1.7 copy-start.8
  344.9 13.1 %copy-start.2 = (f32[2048,256]{1,0:T(8,128)S(1)}, f32[2048,256]{1,0:T(8,128)}, u32[]{:S(2)}) copy-start(f32[2048,256]{1,0:T(8,128)} %fusion.1) | copy-start | bytes 6291460
  358.0 0.7 copy-start.9
Sparse Core Ops, SparseCore 0:
  10.3 107.3 all-gather.1
where the time goes:
time: 368 us; the launch traced here: 367 us
  local copies, waits for them, and re-layouts  294 us (80%)
  other arithmetic  45.1 us (12%)
  between operations  13.6 us (4%)
  starting transfers between devices  12 us (3%)
    gather x1, local copies, waits for them, and re-layouts, per_device(): loc_sum = masked_sum(feats[loc_nbr], loc_len)  129 us
    gather x1, local copies, waits for them, and re-layouts, per_device(): hub_sum = masked_sum(whole_hubs[hub_nbr], hub_len)  65.6 us
    gather x1, local copies, waits for them, and re-layouts, per_device(): halo_sum = masked_sum(arrived[halo_nbr], halo_len)  63.9 us
    reduce_sum x3, other arithmetic, masked_sum(): jnp.sum(rows.astype(jnp.float32) * mask[:, :, None].astype(jnp.float32),...  40.9 us
    gather x1, local copies, waits for them, and re-layouts, per_device(): outgoing = feats[send_list]  32.5 us
    all_to_all x1, starting transfers between devices, per_device(): lax.all_to_all(outgoing, 'dom', split_axis=0, concat_axis=0, tiled=True)  12 us
  transfers between devices with their start and end apart: 2, of which 0 were waited for; matrix products, arithmetic and copies ran while one was open for 71% of the time, Pallas kernels for 0%

commit v1 on v0

v1 whole, which is shorter than its diff:
```python
import jax
import jax.numpy as jnp
from jax import lax
from jax.experimental import pallas as pl
from jax.experimental.pallas import tpu as pltpu
from jax.sharding import PartitionSpec as P

LANES = 128
VMEM_LIMIT = 48 * 2**20


def one_hot(mask):
    return jnp.where(mask, 1.0, 0.0).astype(jnp.bfloat16)


def send_body(list_ref, feats_ref, out_ref, hot_ref):
    columns = list_ref[...].T
    rows = feats_ref.shape[0]
    lane = lax.broadcasted_iota(jnp.int32, (LANES, LANES), 1)
    for j in range(columns.shape[1]):
        wanted = jnp.broadcast_to(columns[:, j : j + 1], (LANES, LANES))
        for t in range(rows // LANES):
            hot_ref[j * LANES : (j + 1) * LANES, t * LANES : (t + 1) * LANES] = one_hot(
                wanted == lane + t * LANES
            )
    out_ref[...] = jnp.dot(
        hot_ref[...], feats_ref[...], preferred_element_type=jnp.float32
    ).astype(out_ref.dtype)


def gather_to_send(feats, send_list):
    rows, width = feats.shape
    count = send_list.size
    group = 8 * LANES
    return pl.pallas_call(
        send_body,
        grid=(count // group,),
        in_specs=[
            pl.BlockSpec((8, LANES), lambda i: (i, 0)),
            pl.BlockSpec((rows, width), lambda i: (0, 0)),
        ],
        out_specs=pl.BlockSpec((group, width), lambda i: (i, 0)),
        out_shape=jax.ShapeDtypeStruct((count, width), feats.dtype),
        scratch_shapes=[pltpu.VMEM((group, rows), jnp.bfloat16)],
        compiler_params=pltpu.CompilerParams(vmem_limit_bytes=VMEM_LIMIT),
        cost_estimate=pl.CostEstimate(
            flops=2 * count * rows * width, bytes_accessed=2 * count * width, transcendentals=0
        ),
        name="gather_to_send",
    )(send_list.reshape(count // LANES, LANES), feats)


def local_body(part, high_ref, low_ref, feats_ref, out_ref, count_ref):
    rows = feats_ref.shape[0]
    blocks = rows // LANES
    groups, contract = high_ref.shape
    tall = lax.broadcasted_iota(jnp.int32, (blocks * part, contract), 0)
    short = lax.broadcasted_iota(jnp.int32, (LANES, contract), 0)
    for g in range(groups):
        left = one_hot(tall == high_ref[g : g + 1, :])
        right = one_hot(short == low_ref[g : g + 1, :])
        counts = lax.dot_general(
            left, right, (((1,), (1,)), ((), ())), preferred_element_type=jnp.float32
        ).astype(jnp.bfloat16)
        for b in range(blocks):
            count_ref[g * part : (g + 1) * part, b * LANES : (b + 1) * LANES] = counts[
                b * part : (b + 1) * part, :
            ]
    out_ref[...] = jnp.dot(count_ref[...], feats_ref[...], preferred_element_type=jnp.float32)


def local_sums(feats, neighbours, length):
    rows, width = feats.shape
    slots = neighbours.shape[1]
    part = 2 * LANES // slots
    used = jnp.arange(slots, dtype=jnp.int32)[None, :] < length[:, None]
    place = (jnp.arange(rows, dtype=jnp.int32) % part)[:, None]
    high = jnp.where(used, (neighbours // LANES) * part + place, -1).reshape(-1, part * slots)
    low = (neighbours % LANES).reshape(-1, part * slots)
    groups = 16
    return pl.pallas_call(
        lambda *refs: local_body(part, *refs),
        grid=(rows // (groups * part),),
        in_specs=[
            pl.BlockSpec((groups, part * slots), lambda i: (i, 0)),
            pl.BlockSpec((groups, part * slots), lambda i: (i, 0)),
            pl.BlockSpec((rows, width), lambda i: (0, 0)),
        ],
        out_specs=pl.BlockSpec((groups * part, width), lambda i: (i, 0)),
        out_shape=jax.ShapeDtypeStruct((rows, width), jnp.float32),
        scratch_shapes=[pltpu.VMEM((groups * part, rows), jnp.bfloat16)],
        compiler_params=pltpu.CompilerParams(vmem_limit_bytes=VMEM_LIMIT),
        cost_estimate=pl.CostEstimate(
            flops=4 * rows * rows * width, bytes_accessed=4 * rows * width, transcendentals=0
        ),
        name="local_sums",
    )(high, low, feats)


def load_table(source, stage, table, sem):
    count = source.shape[0]
    size = stage.shape[0] // stage_chunks(count)
    chunks = stage_chunks(count)

    def copy(c):
        span = pl.ds(c * size, size)
        return pltpu.make_async_copy(source.at[span], stage.at[span], sem.at[c])

    for c in range(chunks):
        copy(c).start()
    table[2 * count : 2 * count + 8, :] = jnp.zeros((8, LANES), jnp.float32)
    for c in range(chunks):
        copy(c).wait()

        def widen(i, carry, c=c):
            start = c * size + i * 256
            block = stage[pl.ds(pl.multiple_of(start, 256), 256), :].astype(jnp.float32)
            table[pl.ds(2 * start, 256, stride=2), :] = block[:, :LANES]
            table[pl.ds(2 * start + 1, 256, stride=2), :] = block[:, LANES:]
            return carry

        lax.fori_loop(0, size // 256, widen, 0)


def stage_chunks(count):
    return 4


def add_rows(index_ref, table, out_ref, slots, unroll):
    def step(i, carry):
        for u in range(unroll):
            v = i * unroll + u
            total = None
            for k in range(slots):
                row = table[pl.ds(pl.multiple_of(index_ref[v * slots + k], 2), 2), :]
                total = row if total is None else total + row
            out_ref[pl.ds(pl.multiple_of(2 * v, 2), 2), :] = total
        return carry

    lax.fori_loop(0, out_ref.shape[0] // (2 * unroll), step, 0)


def hub_body(slots, index_ref, source, out_ref, stage, table, sem):
    load_table(source, stage, table, sem)
    add_rows(index_ref, table, out_ref, slots, 16)


def row_index(neighbours, length, count):
    used = jnp.arange(neighbours.shape[1], dtype=jnp.int32)[None, :] < length[:, None]
    return jnp.where(used, neighbours * 2, 2 * count).reshape(-1)


def hub_sums(index, slots, source):
    count, width = source.shape
    rows = index.shape[0] // slots
    return pl.pallas_call(
        lambda *refs: hub_body(slots, *refs),
        in_specs=[
            pl.BlockSpec(memory_space=pltpu.SMEM),
            pl.BlockSpec(memory_space=pl.ANY),
        ],
        out_specs=pl.BlockSpec(memory_space=pltpu.VMEM),
        out_shape=jax.ShapeDtypeStruct((2 * rows, LANES), jnp.float32),
        scratch_shapes=[
            pltpu.VMEM((count, width), source.dtype),
            pltpu.VMEM((2 * count + 8, LANES), jnp.float32),
            pltpu.SemaphoreType.DMA((stage_chunks(count),)),
        ],
        compiler_params=pltpu.CompilerParams(vmem_limit_bytes=VMEM_LIMIT),
        cost_estimate=pl.CostEstimate(
            flops=40_000_000_000, bytes_accessed=2 * count * width, transcendentals=0
        ),
        name="hub_sums",
    )(index, source)


def layer_body(
    slots, index_ref, source, hub_ref, loc_ref, degree_ref, feats_ref, weight_ref, bias_ref,
    out_ref, stage, table, halo, sem,
):
    load_table(source, stage, table, sem)
    add_rows(index_ref, table, halo, slots, 16)
    rows, width = feats_ref.shape
    tile = 256

    def finish(i, carry):
        start = pl.multiple_of(i * tile, tile)
        span = pl.ds(start, tile)
        degree = degree_ref[span, :]
        halves = []
        for h in range(2):
            pick = pl.ds(2 * start + h, tile, stride=2)
            total = loc_ref[span, h * LANES : (h + 1) * LANES] + hub_ref[pick, :] + halo[pick, :]
            halves.append((total / degree).astype(jnp.bfloat16))
        agg = jnp.concatenate(halves, axis=1)
        result = jnp.dot(
            feats_ref[span, :], weight_ref[:width, :], preferred_element_type=jnp.float32
        )
        result += jnp.dot(agg, weight_ref[width:, :], preferred_element_type=jnp.float32)
        result += bias_ref[...]
        out_ref[span, :] = jnp.maximum(result, 0.0).astype(out_ref.dtype)
        return carry

    lax.fori_loop(0, rows // tile, finish, 0)


def layer(index, slots, source, hub, loc, degree, feats, weight, bias):
    count, width = source.shape
    rows = feats.shape[0]
    vmem = pl.BlockSpec(memory_space=pltpu.VMEM)
    return pl.pallas_call(
        lambda *refs: layer_body(slots, *refs),
        in_specs=[
            pl.BlockSpec(memory_space=pltpu.SMEM),
            pl.BlockSpec(memory_space=pl.ANY),
            vmem, vmem, vmem, vmem, vmem, vmem,
        ],
        out_specs=vmem,
        out_shape=jax.ShapeDtypeStruct((rows, width), feats.dtype),
        scratch_shapes=[
            pltpu.VMEM((count, width), source.dtype),
            pltpu.VMEM((2 * count + 8, LANES), jnp.float32),
            pltpu.VMEM((2 * rows, LANES), jnp.float32),
            pltpu.SemaphoreType.DMA((stage_chunks(count),)),
        ],
        compiler_params=pltpu.CompilerParams(vmem_limit_bytes=VMEM_LIMIT),
        cost_estimate=pl.CostEstimate(
            flops=40_000_000_000, bytes_accessed=2 * count * width, transcendentals=0
        ),
        name="layer",
    )(index, source, hub, loc, degree, feats, weight, bias)


def per_device(
    feats, hub_feat, weight, bias, loc_nbr, loc_len, hub_nbr, hub_len, send_list, halo_nbr, halo_len
):
    rows, width = feats.shape
    peers, slots = send_list.shape
    whole_hubs = lax.all_gather(hub_feat, "dom", axis=0, tiled=True)
    outgoing = gather_to_send(feats, send_list)
    arrived = lax.all_to_all(
        outgoing.reshape(peers, slots, width), "dom", split_axis=0, concat_axis=0, tiled=True
    ).reshape(peers * slots, width)
    loc = local_sums(feats, loc_nbr, loc_len)
    hub = hub_sums(row_index(hub_nbr, hub_len, whole_hubs.shape[0]), hub_nbr.shape[1], whole_hubs)
    degree = jnp.broadcast_to(
        (loc_len + hub_len + halo_len).astype(jnp.float32)[:, None], (rows, LANES)
    )
    return layer(
        row_index(halo_nbr, halo_len, peers * slots),
        halo_nbr.shape[1],
        arrived,
        hub,
        loc,
        degree,
        feats,
        weight,
        bias[None, :],
    )


def solution(mesh):
    placed = (
        P("dom", None),
        P("dom", None),
        P(),
        P(),
        P("dom", None),
        P("dom"),
        P("dom", None),
        P("dom"),
        P("dom", None),
        P("dom", None),
        P("dom"),
    )
    return jax.shard_map(
        per_device, mesh=mesh, in_specs=placed, out_specs=P("dom", None), check_vma=False
    )
```

time: 368 us -> 165 us (0.45)
  local copies, waits for them, and re-layouts: 294 us -> 8.97 us
  Pallas kernels: 0 us -> 65.6 us
  waiting for transfers between devices: 0.71 us -> 64.6 us
  other arithmetic: 45.1 us -> 0.17 us
    gather x4 -> x0, local copies, waits for them, and re-layouts: 291 us -> none  [the longest x1 129 us: per_device(): loc_sum = masked_sum(feats[loc_nbr], loc_len)]
    pallas_call x0 -> x4, Pallas kernels: none -> 65.6 us  [the longest x1 20.9 us: layer(): pl.pallas_call(lambda *refs: layer_body(slots, *refs), in_specs=[pl.Block...]
    all_gather x1, waiting for transfers between devices: 0.01 us -> 63.9 us  [per_device(): whole_hubs = lax.all_gather(hub_feat, 'dom', axis=0, tiled=True)]
    reduce_sum x3 -> x0, other arithmetic: 40.9 us -> none  [masked_sum(): jnp.sum(rows.astype(jnp.float32) * mask[:, :, None].astype(jnp.float32),...]
    unnamed x20 -> x25, local copies, waits for them, and re-layouts: 0.27 us -> 5.38 us
  transfers between devices with their start and end apart: 2 -> 2, of which waited for: 0 -> 1; matrix products, arithmetic and copies ran while one was open for 71% -> 3% of each run, Pallas kernels for 0% -> 27%
where the time goes in v1:
time: 165 us
  Pallas kernels  65.6 us (40%)
  waiting for transfers between devices  64.6 us (39%)
  between operations  13.6 us (8%)
  starting transfers between devices  12 us (7%)
  local copies, waits for them, and re-layouts  8.97 us (5%)
    all_gather x1, waiting for transfers between devices, per_device(): whole_hubs = lax.all_gather(hub_feat, 'dom', axis=0, tiled=True)  63.9 us
    pallas_call x1, Pallas kernels, layer(): pl.pallas_call(lambda *refs: layer_body(slots, *refs), in_specs=[pl.Block...  20.9 us
    pallas_call x1, Pallas kernels, hub_sums(): pl.pallas_call(lambda *refs: hub_body(slots, *refs), in_specs=[pl.BlockSp...  19.3 us
    pallas_call x1, Pallas kernels, gather_to_send(): pl.pallas_call(send_body, grid=(count // group,), in_specs=[pl.BlockSpec(...  13.1 us
    pallas_call x1, Pallas kernels, local_sums(): pl.pallas_call(lambda *refs: local_body(part, *refs), grid=(rows // (grou...  12.4 us
    all_to_all x1, starting transfers between devices, per_device(): lax.all_to_all(outgoing.reshape(peers, slots, width), 'dom', split_axis=0...  12 us
    unnamed x25, local copies, waits for them, and re-layouts  5.38 us
  transfers between devices with their start and end apart: 2, of which 1 were waited for; matrix products, arithmetic and copies ran while one was open for 3% of the time, Pallas kernels for 27%

profile of v1, /device:TPU:1, one launch (start us, length us, event | category | flops | bytes accessed | tf_op | source)
XLA Modules:
  0.0 165.0 jit_solution(2826188428365938594)
XLA Ops:
  6.5 0.0 all-gather.2.cloned.1.call-start
  6.5 0.7 all-gather.2.cloned.1.call-update
  7.3 0.8 copy.16
  8.1 0.1 reshape.35.list_ref
  8.2 0.0 copy-start.1
  8.2 1.2 copy-done.1
  9.4 13.1 %gather_to_send.1 = bf16[8192,256]{1,0:T(8,128)(2,1)S(1)} custom-call(s32[64,128]{1,0:T(8,128)S(1)} %reshape.35.list_ref, bf16[2048,256]{1,0:T(8,128)(2,1)S(1)} %copy-done.1), custom_call_target="tpu_custom_call" | custom-call | flops 8589934592 | bytes 4194304 | tf_op jit(solution)/shard_map/gather_to_send/pallas_call | solution.py:35
  22.5 0.0 copy-start
  22.5 1.9 %copy-done = bf16[8192,256]{1,0:T(8,128)(2,1)} copy-done((bf16[8192,256]{1,0:T(8,128)(2,1)}, bf16[8192,256]{1,0:T(8,128)(2,1)S(1)}, u32[]{:S(2)}) %copy-start) | copy-done | bytes 4194328
  24.4 0.0 copy-start.7
  24.4 0.0 copy-start.10
  24.4 0.0 copy-start.8
  24.4 0.0 copy-start.9
  24.4 0.0 copy-start.6
  24.5 0.0 copy-start.11
  24.5 12.0 %all-to-all-start = ((bf16[128,64,256]{2,1,0:T(8,128)(2,1)}), bf16[128,64,256]{2,1,0:T(8,128)(2,1)}, u32[]{:S(2)}, u32[]{:S(2)}) async-start(bf16[128,64,256]{2,1,0:T(8,128)(2,1)} %bitcast.3), calls=%async_computation | async-start | bytes 8388608 | tf_op jit(solution)/shard_map/all_to_all | solution.py:241
  36.4 0.0 copy-done.7
  36.5 0.0 copy-done.10
  36.5 0.0 copy-done.8
  36.5 0.0 copy-done.9
  36.5 0.0 copy-done.6
  36.5 0.0 copy-done.11
  36.5 0.1 add_select_fusion
  36.7 0.3 copy.19
  37.0 0.0 copy-start.2
  37.0 0.4 reshape.40.refs_1_
  37.5 0.3 copy.15
  37.8 0.5 reshape.34.refs_0_
  38.3 0.3 copy.17
  38.7 0.5 reshape.38.refs_0_
  39.2 0.3 copy.18
  39.5 0.4 reshape.39.refs_0_
  39.9 0.0 copy-done.2
  40.0 12.4 %local_sums.1.refs_3_ = f32[2048,256]{1,0:T(8,128)S(1)} custom-call(s32[128,256]{1,0:T(8,128)S(1)} %reshape.39.refs_0_, s32[128,256]{1,0:T(8,128)S(1)} %reshape.40.refs_1_, bf16[2048,256]{1,0:T(8,128)(2,1)S(1)} %copy-done.2), custom_call_target="tpu_custom_call" | custom-call | flops 4294967296 | bytes 2097152 | tf_op jit(solution)/shard_map/local_sums/pallas_call | solution.py:81
  52.4 0.0 copy-start.5
  52.4 1.3 copy-done.5
  53.7 0.0 copy-start.3
  53.7 0.0 copy-start.4
  53.7 63.9 %all-gather.2.cloned.1.call-done.refs_1_ = bf16[16384,256]{1,0:T(8,128)(2,1)} async-done(((bf16[128,256]{1,0:T(8,128)(2,1)}), bf16[16384,256]{1,0:T(8,128)(2,1)}) %all-gather.2.cloned.1.call-update) | async-done | bytes 8388624 | tf_op jit(solution)/shard_map/all_gather | solution.py:239
  117.6 19.3 %hub_sums.1.refs_2_ = f32[4096,128]{1,0:T(8,128)S(1)} custom-call(s32[16384]{0:T(1024)S(1)} %reshape.38.refs_0_, bf16[16384,256]{1,0:T(8,128)(2,1)} %all-gather.2.cloned.1.call-done.refs_1_), custom_call_target="tpu_custom_call" | custom-call | flops 40000000000 | bytes 8388608 | tf_op jit(solution)/shard_map/hub_sums/pallas_call | solution.py:156
  136.9 0.0 all-to-all-done
  136.9 0.3 broadcast_in_dim.15.refs_4_
  137.2 0.0 copy-done.3
  137.3 0.0 copy-done.4
  137.3 20.9 %layer.1 = bf16[2048,256]{1,0:T(8,128)(2,1)} custom-call(s32[16384]{0:T(1024)S(1)} %reshape.34.refs_0_, bf16[8192,256]{1,0:T(8,128)(2,1)} %bitcast.1.refs_1_, f32[4096,128]{1,0:T(8,128)S(1)} %hub_sums.1.refs_2_, f32[2048,256]{1,0:T(8,128)} %copy-done.5, f32[2048,128]{1,0:T(8,128)S(1)} %broadcast_in_dim.15.refs_4_, bf16[2048,256]{1,0:T(8,128)(2,1)S(1)} %copy-done.2, ...), custom_call_target="tpu_custom_call" | custom-call | flops 40000000000 | bytes 4194304 | tf_op jit(solution)/shard_map/layer/pallas_call | solution.py:211
  (4 shorter events, 0.0 us)
Async XLA Ops:
  6.5 111.1 %all-gather.2.cloned.1.call-start = ((), (), s32[]{:S(2)}) async-start(), calls=%async_computation.1 | async-start | bytes 8454144 | tf_op jit(solution)/shard_map/all_gather | solution.py:239
  8.2 1.2 copy-start.1
  22.5 1.9 %copy-start = (bf16[8192,256]{1,0:T(8,128)(2,1)}, bf16[8192,256]{1,0:T(8,128)(2,1)S(1)}, u32[]{:S(2)}) copy-start(bf16[8192,256]{1,0:T(8,128)(2,1)S(1)} %gather_to_send.1) | copy-start | bytes 12582916
  24.4 12.0 %copy-start.7 = (s32[2048,8]{0,1:T(8,128)S(1)}, s32[2048,8]{0,1:T(8,128)}, u32[]{:S(2)}) copy-start(s32[2048,8]{0,1:T(8,128)} %param.17) | copy-start | bytes 196612
  24.4 12.0 %copy-start.10 = (s32[2048]{0:T(1024)S(1)}, s32[2048]{0:T(1024)}, u32[]{:S(2)}) copy-start(s32[2048]{0:T(1024)} %param.18) | copy-start | bytes 24580
  24.4 12.1 %copy-start.8 = (s32[2048,8]{0,1:T(8,128)S(1)}, s32[2048,8]{0,1:T(8,128)}, u32[]{:S(2)}) copy-start(s32[2048,8]{0,1:T(8,128)} %param.20) | copy-start | bytes 196612
  24.4 12.1 %copy-start.9 = (s32[2048]{0:T(1024)S(1)}, s32[2048]{0:T(1024)}, u32[]{:S(2)}) copy-start(s32[2048]{0:T(1024)} %param.21) | copy-start | bytes 24580
  24.4 12.1 %copy-start.6 = (s32[2048,16]{0,1:T(8,128)S(1)}, s32[2048,16]{0,1:T(8,128)}, u32[]{:S(2)}) copy-start(s32[2048,16]{0,1:T(8,128)} %param.15) | copy-start | bytes 393220
  24.5 12.1 %copy-start.11 = (s32[2048]{0:T(1024)S(1)}, s32[2048]{0:T(1024)}, u32[]{:S(2)}) copy-start(s32[2048]{0:T(1024)} %param.16) | copy-start | bytes 24580
  24.5 112.4 %all-to-all-start = ((bf16[128,64,256]{2,1,0:T(8,128)(2,1)}), bf16[128,64,256]{2,1,0:T(8,128)(2,1)}, u32[]{:S(2)}, u32[]{:S(2)}) async-start(bf16[128,64,256]{2,1,0:T(8,128)(2,1)} %bitcast.3), calls=%async_computation | async-start | bytes 8388608 | tf_op jit(solution)/shard_map/all_to_all | solution.py:241
  37.0 2.9 %copy-start.2 = (bf16[2048,256]{1,0:T(8,128)(2,1)S(1)}, bf16[2048,256]{1,0:T(8,128)(2,1)}, u32[]{:S(2)}) copy-start(bf16[2048,256]{1,0:T(8,128)(2,1)} %refs_5_.1) | copy-start | bytes 3145732
  52.4 1.3 copy-start.5
  53.7 83.5 %copy-start.3 = (bf16[512,256]{1,0:T(8,128)(2,1)S(1)}, bf16[512,256]{1,0:T(8,128)(2,1)}, u32[]{:S(2)}) copy-start(bf16[512,256]{1,0:T(8,128)(2,1)} %refs_6_.1) | copy-start | bytes 786436
  53.7 83.5 %copy-start.4 = (f32[256]{0:T(256)S(1)}, f32[256]{0:T(256)}, u32[]{:S(2)}) copy-start(f32[256]{0:T(256)} %param.14) | copy-start | bytes 3076
Sparse Core Ops, SparseCore 0:
  10.3 107.2 all-gather.1

commit v2 on v1

--- a/solution.py
+++ b/solution.py
@@ -7,6 +7,8 @@
 
 LANES = 128
 VMEM_LIMIT = 48 * 2**20
+CHUNK = 2048
+WIDEN = 256
 
 
 def one_hot(mask):
@@ -97,33 +99,42 @@
     )(high, low, feats)
 
 
-def load_table(source, stage, table, sem):
-    count = source.shape[0]
-    size = stage.shape[0] // stage_chunks(count)
-    chunks = stage_chunks(count)
-
-    def copy(c):
-        span = pl.ds(c * size, size)
-        return pltpu.make_async_copy(source.at[span], stage.at[span], sem.at[c])
-
-    for c in range(chunks):
-        copy(c).start()
-    table[2 * count : 2 * count + 8, :] = jnp.zeros((8, LANES), jnp.float32)
-    for c in range(chunks):
-        copy(c).wait()
-
-        def widen(i, carry, c=c):
-            start = c * size + i * 256
-            block = stage[pl.ds(pl.multiple_of(start, 256), 256), :].astype(jnp.float32)
-            table[pl.ds(2 * start, 256, stride=2), :] = block[:, :LANES]
-            table[pl.ds(2 * start + 1, 256, stride=2), :] = block[:, LANES:]
+def load_table(sources, stage, table, sem):
+    copies = []
+    start = 0
+    for source in sources:
+        count = source.shape[0]
+        size = min(count, CHUNK)
+        for first in range(0, count, size):
+            copies.append(
+                pltpu.make_async_copy(
+                    source.at[pl.ds(first, size)],
+                    stage.at[pl.ds(start, size)],
+                    sem.at[len(copies)],
+                )
+            )
+            start += size
+    for copy in copies:
+        copy.start()
+    table[2 * start : 2 * start + 8, :] = jnp.zeros((8, LANES), jnp.float32)
+    start = 0
+    for copy in copies:
+        copy.wait()
+        size = copy.dst_ref.shape[0]
+
+        def widen(i, carry, first=start):
+            at = first + i * WIDEN
+            block = stage[pl.ds(pl.multiple_of(at, WIDEN), WIDEN), :].astype(jnp.float32)
+            table[pl.ds(2 * at, WIDEN, stride=2), :] = block[:, :LANES]
+            table[pl.ds(2 * at + 1, WIDEN, stride=2), :] = block[:, LANES:]
             return carry
 
-        lax.fori_loop(0, size // 256, widen, 0)
-
-
-def stage_chunks(count):
-    return 4
+        lax.fori_loop(0, size // WIDEN, widen, 0)
+        start += size
+
+
+def chunk_count(sources):
+    return sum(-(-source.shape[0] // CHUNK) for source in sources)
 
 
 def add_rows(index_ref, table, out_ref, slots, unroll):
@@ -140,8 +151,9 @@
     lax.fori_loop(0, out_ref.shape[0] // (2 * unroll), step, 0)
 
 
-def hub_body(slots, index_ref, source, out_ref, stage, table, sem):
-    load_table(source, stage, table, sem)
+def hub_body(slots, pieces, index_ref, *refs):
+    sources, (out_ref, stage, table, sem) = refs[:pieces], refs[pieces:]
+    load_table(sources, stage, table, sem)
     add_rows(index_ref, table, out_ref, slots, 16)
 
 
@@ -150,35 +162,34 @@
     return jnp.where(used, neighbours * 2, 2 * count).reshape(-1)
 
 
-def hub_sums(index, slots, source):
-    count, width = source.shape
+def hub_sums(index, slots, sources):
+    width = sources[0].shape[1]
+    count = sum(source.shape[0] for source in sources)
     rows = index.shape[0] // slots
     return pl.pallas_call(
-        lambda *refs: hub_body(slots, *refs),
-        in_specs=[
-            pl.BlockSpec(memory_space=pltpu.SMEM),
-            pl.BlockSpec(memory_space=pl.ANY),
-        ],
+        lambda *refs: hub_body(slots, len(sources), *refs),
+        in_specs=[pl.BlockSpec(memory_space=pltpu.SMEM)]
+        + [pl.BlockSpec(memory_space=pl.ANY)] * len(sources),
         out_specs=pl.BlockSpec(memory_space=pltpu.VMEM),
         out_shape=jax.ShapeDtypeStruct((2 * rows, LANES), jnp.float32),
         scratch_shapes=[
-            pltpu.VMEM((count, width), source.dtype),
+            pltpu.VMEM((count, width), sources[0].dtype),
             pltpu.VMEM((2 * count + 8, LANES), jnp.float32),
-            pltpu.SemaphoreType.DMA((stage_chunks(count),)),
+            pltpu.SemaphoreType.DMA((chunk_count(sources),)),
         ],
         compiler_params=pltpu.CompilerParams(vmem_limit_bytes=VMEM_LIMIT),
         cost_estimate=pl.CostEstimate(
-            flops=40_000_000_000, bytes_accessed=2 * count * width, transcendentals=0
+            flops=20_000_000_000, bytes_accessed=2 * count * width, transcendentals=0
         ),
         name="hub_sums",
-    )(index, source)
+    )(index, *sources)
 
 
 def layer_body(
     slots, index_ref, source, hub_ref, loc_ref, degree_ref, feats_ref, weight_ref, bias_ref,
     out_ref, stage, table, halo, sem,
 ):
-    load_table(source, stage, table, sem)
+    load_table([source], stage, table, sem)
     add_rows(index_ref, table, halo, slots, 16)
     rows, width = feats_ref.shape
     tile = 256
@@ -221,7 +232,7 @@
             pltpu.VMEM((count, width), source.dtype),
             pltpu.VMEM((2 * count + 8, LANES), jnp.float32),
             pltpu.VMEM((2 * rows, LANES), jnp.float32),
-            pltpu.SemaphoreType.DMA((stage_chunks(count),)),
+            pltpu.SemaphoreType.DMA((chunk_count([source]),)),
         ],
         compiler_params=pltpu.CompilerParams(vmem_limit_bytes=VMEM_LIMIT),
         cost_estimate=pl.CostEstimate(
@@ -231,18 +242,71 @@
     )(index, source, hub, loc, degree, feats, weight, bias)
 
 
+RING = 4
+STRIDES = {"x": 32, "z": 8, "y": 2}
+ORDERS = (("y", "z", "x"), ("z", "x", "y"))
+
+
+def moved(stage, step):
+    pairs = []
+    for device in range(2 * RING**3):
+        stride = STRIDES[ORDERS[device % 2][stage]]
+        at = device // stride % RING
+        pairs.append((device, device + (step(at) - at) * stride))
+    return pairs
+
+
+def gather_hubs(own):
+    block = own
+    for stage in range(2):
+        for flip in (1, 3):
+            other = lax.ppermute(block, "dom", moved(stage, lambda i, flip=flip: i ^ flip))
+            block = jnp.concatenate([block, other], axis=0)
+    blocks = [block]
+    for shift in (1, 3, 2):
+        blocks.append(
+            lax.ppermute(block, "dom", moved(2, lambda i, shift=shift: (i - shift) % RING))
+        )
+    swap = [(device, device ^ 1) for device in range(2 * RING**3)]
+    return blocks + [lax.ppermute(part, "dom", swap) for part in blocks]
+
+
+def gray(value):
+    return value ^ (value >> 1)
+
+
+def hub_place(hub, rows_each):
+    me = lax.axis_index("dom")
+    device = hub // rows_each
+    apart = {
+        name: ((device // stride % RING), (me // stride % RING)) for name, stride in STRIDES.items()
+    }
+    near = {name: gray(theirs ^ mine) for name, (theirs, mine) in apart.items()}
+    far = {name: gray((theirs - mine) & (RING - 1)) for name, (theirs, mine) in apart.items()}
+    core = device & 1
+
+    def place(order):
+        return (far[order[2]] * RING + near[order[1]]) * RING + near[order[0]]
+
+    block = jnp.where(core == 0, place(ORDERS[0]), place(ORDERS[1]))
+    block += (core ^ (me & 1)) * RING**3
+    return block * rows_each + hub % rows_each
+
+
 def per_device(
     feats, hub_feat, weight, bias, loc_nbr, loc_len, hub_nbr, hub_len, send_list, halo_nbr, halo_len
 ):
     rows, width = feats.shape
     peers, slots = send_list.shape
-    whole_hubs = lax.all_gather(hub_feat, "dom", axis=0, tiled=True)
+    hubs = gather_hubs(hub_feat)
     outgoing = gather_to_send(feats, send_list)
     arrived = lax.all_to_all(
         outgoing.reshape(peers, slots, width), "dom", split_axis=0, concat_axis=0, tiled=True
     ).reshape(peers * slots, width)
     loc = local_sums(feats, loc_nbr, loc_len)
-    hub = hub_sums(row_index(hub_nbr, hub_len, whole_hubs.shape[0]), hub_nbr.shape[1], whole_hubs)
+    each = hub_feat.shape[0]
+    hub_index = row_index(hub_place(hub_nbr, each), hub_len, lax.axis_size("dom") * each)
+    hub = hub_sums(hub_index, hub_nbr.shape[1], hubs)
     degree = jnp.broadcast_to(
         (loc_len + hub_len + halo_len).astype(jnp.float32)[:, None], (rows, LANES)
     )

time: 165 us -> 183 us (1.11)
  starting transfers between devices: 12 us -> 26.9 us
  between operations: 13.6 us -> 0.23 us
  local copies, waits for them, and re-layouts: 8.97 us -> 19.4 us
  other arithmetic: 0.17 us -> 5.51 us
    all_gather x1 -> x0, waiting for transfers between devices: 63.9 us -> none  [per_device(): whole_hubs = lax.all_gather(hub_feat, 'dom', axis=0, tiled=True)]
    ppermute x0 -> x11, waiting for transfers between devices: none -> 63.3 us  [the longest x3 55.3 us: gather_hubs(): lax.ppermute(block, 'dom', moved(2, lambda i, shift=shift: (i - shift) %...]
    ppermute x0 -> x11, starting transfers between devices: none -> 16.1 us  [the longest x4 9.98 us: gather_hubs(): lax.ppermute(block, 'dom', moved(stage, lambda i, flip=flip: i ^ flip))]
    concatenate x0 -> x3, other arithmetic: none -> 2.58 us  [gather_hubs(): block = jnp.concatenate([block, other], axis=0)]
    reshape x2, local copies, waits for them, and re-layouts: 1 us -> 3.39 us  [row_index(): return jnp.where(used, neighbours * 2, 2 * count).reshape(-1)]
    select_n x2, local copies, waits for them, and re-layouts: 0.66 us -> 2.62 us  [row_index(): return jnp.where(used, neighbours * 2, 2 * count).reshape(-1)]
    unnamed x25 -> x29, local copies, waits for them, and re-layouts: 5.38 us -> 7.13 us
  transfers between devices with their start and end apart: 2 -> 12, of which waited for: 1 -> 6; matrix products, arithmetic and copies ran while one was open for 3% -> 9% of each run, Pallas kernels for 27% -> 25%
where the time goes in v2:
time: 183 us; the launch traced here: 182 us
  Pallas kernels  66.3 us (36%)
  waiting for transfers between devices  63.3 us (35%)
  starting transfers between devices  26.9 us (15%)
  local copies, waits for them, and re-layouts  19.4 us (11%)
  other arithmetic  5.51 us (3%)
    ppermute x3, waiting for transfers between devices, gather_hubs(): lax.ppermute(block, 'dom', moved(2, lambda i, shift=shift: (i - shift) %...  55.3 us
    pallas_call x1, Pallas kernels, layer(): pl.pallas_call(lambda *refs: layer_body(slots, *refs), in_specs=[pl.Block...  20.8 us
    pallas_call x1, Pallas kernels, hub_sums(): pl.pallas_call(lambda *refs: hub_body(slots, len(sources), *refs), in_spe...  20 us
    pallas_call x1, Pallas kernels, gather_to_send(): pl.pallas_call(send_body, grid=(count // group,), in_specs=[pl.BlockSpec(...  13.1 us
    pallas_call x1, Pallas kernels, local_sums(): pl.pallas_call(lambda *refs: local_body(part, *refs), grid=(rows // (grou...  12.4 us
    all_to_all x1, starting transfers between devices, per_device(): lax.all_to_all(outgoing.reshape(peers, slots, width), 'dom', split_axis=0...  10.8 us
    ppermute x4, starting transfers between devices, gather_hubs(): lax.ppermute(block, 'dom', moved(stage, lambda i, flip=flip: i ^ flip))  9.98 us
    ppermute x4, waiting for transfers between devices, gather_hubs(): lax.ppermute(block, 'dom', moved(stage, lambda i, flip=flip: i ^ flip))  7.9 us
  transfers between devices with their start and end apart: 12, of which 6 were waited for; matrix products, arithmetic and copies ran while one was open for 9% of the time, Pallas kernels for 25%

profile of v2, /device:TPU:1, one launch (start us, length us, event | category | flops | bytes accessed | tf_op | source)
XLA Modules:
  0.0 181.6 jit_solution(12083327071610982721)
XLA Ops:
  0.0 2.5 %collective-permute-start = (bf16[128,256]{1,0:T(8,128)(2,1)}, bf16[128,256]{1,0:T(8,128)(2,1)S(1)}, u32[]{:S(2)}, u32[]{:S(2)}) collective-permute-start(bf16[128,256]{1,0:T(8,128)(2,1)} %param.12), channel_id=1, source_target_pairs={{0,2},{1,9},{2,0},{3,11},{4,6},{5,13},{6,4},{7,15},{8,10},{9,1},{1... | collective-permute-start | bytes 196616 | tf_op jit(solution)/shard_map/ppermute | solution.py:263
  2.5 1.9 %collective-permute-done = bf16[128,256]{1,0:T(8,128)(2,1)S(1)} collective-permute-done((bf16[128,256]{1,0:T(8,128)(2,1)}, bf16[128,256]{1,0:T(8,128)(2,1)S(1)}, u32[]{:S(2)}, u32[]{:S(2)}) %collective-permute-start) | collective-permute-done | bytes 65568 | tf_op jit(solution)/shard_map/ppermute | solution.py:263
  4.3 0.8 pad_maximum_fusion.2
  5.2 3.7 %collective-permute-start.1 = (bf16[256,256]{1,0:T(8,128)(2,1)S(1)}, bf16[256,256]{1,0:T(8,128)(2,1)S(1)}, u32[]{:S(2)}, u32[]{:S(2)}) collective-permute-start(bf16[256,256]{1,0:T(8,128)(2,1)S(1)} %pad_maximum_fusion.2), channel_id=1, source_target_pairs={{0,6},{1,25},{2,4},{3,27},{4,2},{5,29},{6,0},{7,31},{8,14},{9,17},... | collective-permute-start | bytes 393224 | tf_op jit(solution)/shard_map/ppermute | solution.py:263
  8.8 2.7 %collective-permute-done.1 = bf16[256,256]{1,0:T(8,128)(2,1)S(1)} collective-permute-done((bf16[256,256]{1,0:T(8,128)(2,1)S(1)}, bf16[256,256]{1,0:T(8,128)(2,1)S(1)}, u32[]{:S(2)}, u32[]{:S(2)}) %collective-permute-start.1) | collective-permute-done | bytes 131104 | tf_op jit(solution)/shard_map/ppermute | solution.py:263
  11.5 0.9 pad_maximum_fusion.1
  12.4 1.3 collective-permute-start.2
  13.7 0.8 copy.16
  14.5 0.1 reshape.35.list_ref
  14.6 3.4 %collective-permute-done.2 = bf16[512,256]{1,0:T(8,128)(2,1)S(1)} collective-permute-done((bf16[512,256]{1,0:T(8,128)(2,1)S(1)}, bf16[512,256]{1,0:T(8,128)(2,1)S(1)}, u32[]{:S(2)}, u32[]{:S(2)}) %collective-permute-start.2) | collective-permute-done | bytes 262176 | tf_op jit(solution)/shard_map/ppermute | solution.py:263
  18.0 0.9 pad_maximum_fusion
  18.8 2.6 %collective-permute-start.3 = (bf16[1024,256]{1,0:T(8,128)(2,1)S(1)}, bf16[1024,256]{1,0:T(8,128)(2,1)S(1)}, u32[]{:S(2)}, u32[]{:S(2)}) collective-permute-start(bf16[1024,256]{1,0:T(8,128)(2,1)S(1)} %pad_maximum_fusion), channel_id=1, source_target_pairs={{0,24},{1,97},{2,26},{3,99},{4,28},{5,101},{6,30},{7,103},{8,16},{... | collective-permute-start | bytes 1572872 | tf_op jit(solution)/shard_map/ppermute | solution.py:263
  21.4 1.2 copy-done.1
  22.6 13.1 %gather_to_send.1 = bf16[8192,256]{1,0:T(8,128)(2,1)S(1)} custom-call(s32[64,128]{1,0:T(8,128)S(1)} %reshape.35.list_ref, bf16[2048,256]{1,0:T(8,128)(2,1)S(1)} %copy-done.1), custom_call_target="tpu_custom_call" | custom-call | flops 8589934592 | bytes 4194304 | tf_op jit(solution)/shard_map/gather_to_send/pallas_call | solution.py:37
  35.7 2.0 %copy-done = bf16[8192,256]{1,0:T(8,128)(2,1)} copy-done((bf16[8192,256]{1,0:T(8,128)(2,1)}, bf16[8192,256]{1,0:T(8,128)(2,1)S(1)}, u32[]{:S(2)}) %copy-start) | copy-done | bytes 4194328
  37.7 10.8 %all-to-all-start = ((bf16[128,64,256]{2,1,0:T(8,128)(2,1)}), bf16[128,64,256]{2,1,0:T(8,128)(2,1)}, u32[]{:S(2)}, u32[]{:S(2)}) async-start(bf16[128,64,256]{2,1,0:T(8,128)(2,1)} %bitcast.3), calls=%async_computation | async-start | bytes 8388608 | tf_op jit(solution)/shard_map/all_to_all | solution.py:303
  48.5 0.0 copy-start.11
  48.6 0.0 copy-start.9
  48.6 0.0 collective-permute-done.3
  48.7 3.0 %collective-permute-start.6 = (bf16[2048,256]{1,0:T(8,128)(2,1)S(1)}, bf16[2048,256]{1,0:T(8,128)(2,1)S(1)}, u32[]{:S(2)}, u32[]{:S(2)}) collective-permute-start(bf16[2048,256]{1,0:T(8,128)(2,1)S(1)} %constant_dynamic-update-slice_fusion.refs_1_), channel_id=1, source_target_pairs={{0,64},{1,5},{2,66},{3,7},{4,68},{5,1},{6,70},{7,3},{8,72},{9,13},... | collective-permute-start | bytes 3145736 | tf_op jit(solution)/shard_map/ppermute | solution.py:268
  51.7 0.9 collective-permute-start.4
  52.6 0.6 collective-permute-start.5
  53.1 0.3 fusion.16
  53.5 1.3 copy.17
  54.8 1.7 reshape.38.refs_0_
  56.5 1.0 add_select_fusion
  57.6 1.3 copy.18
  58.9 1.6 reshape.39.refs_0_
  60.5 1.3 copy.19
  61.8 1.6 reshape.40.refs_1_
  63.4 1.3 collective-permute-start.7
  64.7 43.4 %collective-permute-done.6.refs_4_ = bf16[2048,256]{1,0:T(8,128)(2,1)S(1)} collective-permute-done((bf16[2048,256]{1,0:T(8,128)(2,1)S(1)}, bf16[2048,256]{1,0:T(8,128)(2,1)S(1)}, u32[]{:S(2)}, u32[]{:S(2)}) %collective-permute-start.6) | collective-permute-done | bytes 1048608 | tf_op jit(solution)/shard_map/ppermute | solution.py:268
  108.1 0.1 collective-permute-start.10
  108.2 9.7 %collective-permute-done.4.refs_2_ = bf16[2048,256]{1,0:T(8,128)(2,1)} collective-permute-done((bf16[2048,256]{1,0:T(8,128)(2,1)S(1)}, bf16[2048,256]{1,0:T(8,128)(2,1)}, u32[]{:S(2)}, u32[]{:S(2)}) %collective-permute-start.4) | collective-permute-done | bytes 1048608 | tf_op jit(solution)/shard_map/ppermute | solution.py:268
  117.9 0.3 collective-permute-start.8
  118.2 2.2 %collective-permute-done.5.refs_3_ = bf16[2048,256]{1,0:T(8,128)(2,1)} collective-permute-done((bf16[2048,256]{1,0:T(8,128)(2,1)S(1)}, bf16[2048,256]{1,0:T(8,128)(2,1)}, u32[]{:S(2)}, u32[]{:S(2)}) %collective-permute-start.5) | collective-permute-done | bytes 1048608 | tf_op jit(solution)/shard_map/ppermute | solution.py:268
  120.4 0.0 collective-permute-start.9
  120.4 0.9 multiply_select_fusion
  121.3 1.3 copy.15
  122.6 1.6 reshape.34.refs_0_
  124.3 0.7 add_convert_fusion
  125.0 12.4 %local_sums.1.refs_3_ = f32[2048,256]{1,0:T(8,128)S(1)} custom-call(s32[128,256]{1,0:T(8,128)S(1)} %reshape.39.refs_0_, s32[128,256]{1,0:T(8,128)S(1)} %reshape.40.refs_1_, bf16[2048,256]{1,0:T(8,128)(2,1)S(1)} %copy-done.2), custom_call_target="tpu_custom_call" | custom-call | flops 4294967296 | bytes 2097152 | tf_op jit(solution)/shard_map/local_sums/pallas_call | solution.py:83
  137.4 1.4 copy-done.5
  138.8 0.0 collective-permute-done.8.refs_6_
  138.8 20.0 %hub_sums.1.refs_2_ = f32[4096,128]{1,0:T(8,128)} custom-call(s32[16384]{0:T(1024)S(1)} %reshape.38.refs_0_, bf16[2048,256]{1,0:T(8,128)(2,1)S(1)} %constant_dynamic-update-slice_fusion.refs_1_, bf16[2048,256]{1,0:T(8,128)(2,1)} %collective-permute-done.4.refs_2_, bf16[2048,256]{1,0:T(8,128)(2,1)} %collective-permute-done.5.refs_3_, ...), custom_call_target="tpu_custom_call" | custom-call | flops 20000000000 | bytes 8388608 | tf_op jit(solution)/shard_map/hub_sums/pallas_call | solution.py:169
  158.8 0.3 broadcast_in_dim.15.refs_4_
  159.2 1.6 copy-done.6
  160.8 20.8 %layer.1 = bf16[2048,256]{1,0:T(8,128)(2,1)} custom-call(s32[16384]{0:T(1024)S(1)} %reshape.34.refs_0_, bf16[8192,256]{1,0:T(8,128)(2,1)} %bitcast.1.refs_1_, f32[4096,128]{1,0:T(8,128)S(1)} %copy-done.6, f32[2048,256]{1,0:T(8,128)} %copy-done.5, f32[2048,128]{1,0:T(8,128)S(1)} %broadcast_in_dim.15.refs_4_, bf16[2048,256]{1,0:T(8,128)(2,1)S(1)} %copy-done.2, ...), custom_call_target="tpu_custom_call" | custom-call | flops 40000000000 | bytes 4194304 | tf_op jit(solution)/shard_map/layer/pallas_call | solution.py:222
  (28 shorter events, 0.1 us)
Async XLA Ops:
  0.0 4.3 %collective-permute-start = (bf16[128,256]{1,0:T(8,128)(2,1)}, bf16[128,256]{1,0:T(8,128)(2,1)S(1)}, u32[]{:S(2)}, u32[]{:S(2)}) collective-permute-start(bf16[128,256]{1,0:T(8,128)(2,1)} %param.12), channel_id=1, source_target_pairs={{0,2},{1,9},{2,0},{3,11},{4,6},{5,13},{6,4},{7,15},{8,10},{9,1},{1... | collective-permute-start | bytes 196616 | tf_op jit(solution)/shard_map/ppermute | solution.py:263
  5.2 6.3 %collective-permute-start.1 = (bf16[256,256]{1,0:T(8,128)(2,1)S(1)}, bf16[256,256]{1,0:T(8,128)(2,1)S(1)}, u32[]{:S(2)}, u32[]{:S(2)}) collective-permute-start(bf16[256,256]{1,0:T(8,128)(2,1)S(1)} %pad_maximum_fusion.2), channel_id=1, source_target_pairs={{0,6},{1,25},{2,4},{3,27},{4,2},{5,29},{6,0},{7,31},{8,14},{9,17},... | collective-permute-start | bytes 393224 | tf_op jit(solution)/shard_map/ppermute | solution.py:263
  12.4 5.6 %collective-permute-start.2 = (bf16[512,256]{1,0:T(8,128)(2,1)S(1)}, bf16[512,256]{1,0:T(8,128)(2,1)S(1)}, u32[]{:S(2)}, u32[]{:S(2)}) collective-permute-start(bf16[512,256]{1,0:T(8,128)(2,1)S(1)} %pad_maximum_fusion.1), channel_id=1, source_target_pairs={{0,8},{1,33},{2,10},{3,35},{4,12},{5,37},{6,14},{7,39},{8,0},{9,41... | collective-permute-start | bytes 786440 | tf_op jit(solution)/shard_map/ppermute | solution.py:263
  18.8 29.8 %collective-permute-start.3 = (bf16[1024,256]{1,0:T(8,128)(2,1)S(1)}, bf16[1024,256]{1,0:T(8,128)(2,1)S(1)}, u32[]{:S(2)}, u32[]{:S(2)}) collective-permute-start(bf16[1024,256]{1,0:T(8,128)(2,1)S(1)} %pad_maximum_fusion), channel_id=1, source_target_pairs={{0,24},{1,97},{2,26},{3,99},{4,28},{5,101},{6,30},{7,103},{8,16},{... | collective-permute-start | bytes 1572872 | tf_op jit(solution)/shard_map/ppermute | solution.py:263
  21.4 1.2 copy-start.1
  35.7 2.0 %copy-start = (bf16[8192,256]{1,0:T(8,128)(2,1)}, bf16[8192,256]{1,0:T(8,128)(2,1)S(1)}, u32[]{:S(2)}) copy-start(bf16[8192,256]{1,0:T(8,128)(2,1)S(1)} %gather_to_send.1) | copy-start | bytes 12582916
  37.7 10.8 %copy-start.7 = (bf16[128,256]{1,0:T(8,128)(2,1)S(1)}, bf16[128,256]{1,0:T(8,128)(2,1)}, u32[]{:S(2)}) copy-start(bf16[128,256]{1,0:T(8,128)(2,1)} %param.12) | copy-start | bytes 196612
  37.7 15.4 %copy-start.8 = (s32[2048,8]{0,1:T(8,128)S(1)}, s32[2048,8]{0,1:T(8,128)}, u32[]{:S(2)}) copy-start(s32[2048,8]{0,1:T(8,128)} %param.17) | copy-start | bytes 196612
  37.7 15.4 %copy-start.10 = (s32[2048]{0:T(1024)S(1)}, s32[2048]{0:T(1024)}, u32[]{:S(2)}) copy-start(s32[2048]{0:T(1024)} %param.18) | copy-start | bytes 24580
  37.7 121.1 %all-to-all-start = ((bf16[128,64,256]{2,1,0:T(8,128)(2,1)}), bf16[128,64,256]{2,1,0:T(8,128)(2,1)}, u32[]{:S(2)}, u32[]{:S(2)}) async-start(bf16[128,64,256]{2,1,0:T(8,128)(2,1)} %bitcast.3), calls=%async_computation | async-start | bytes 8388608 | tf_op jit(solution)/shard_map/all_to_all | solution.py:303
  48.5 8.0 %copy-start.11 = (s32[2048]{0:T(1024)S(1)}, s32[2048]{0:T(1024)}, u32[]{:S(2)}) copy-start(s32[2048]{0:T(1024)} %param.16) | copy-start | bytes 24580
  48.6 71.8 %copy-start.9 = (s32[2048]{0:T(1024)S(1)}, s32[2048]{0:T(1024)}, u32[]{:S(2)}) copy-start(s32[2048]{0:T(1024)} %param.21) | copy-start | bytes 24580
  48.7 59.4 %collective-permute-start.6 = (bf16[2048,256]{1,0:T(8,128)(2,1)S(1)}, bf16[2048,256]{1,0:T(8,128)(2,1)S(1)}, u32[]{:S(2)}, u32[]{:S(2)}) collective-permute-start(bf16[2048,256]{1,0:T(8,128)(2,1)S(1)} %constant_dynamic-update-slice_fusion.refs_1_), channel_id=1, source_target_pairs={{0,64},{1,5},{2,66},{3,7},{4,68},{5,1},{6,70},{7,3},{8,72},{9,13},... | collective-permute-start | bytes 3145736 | tf_op jit(solution)/shard_map/ppermute | solution.py:268
  51.7 66.2 %collective-permute-start.4 = (bf16[2048,256]{1,0:T(8,128)(2,1)S(1)}, bf16[2048,256]{1,0:T(8,128)(2,1)}, u32[]{:S(2)}, u32[]{:S(2)}) collective-permute-start(bf16[2048,256]{1,0:T(8,128)(2,1)S(1)} %constant_dynamic-update-slice_fusion.refs_1_), channel_id=1, source_target_pairs={{0,96},{1,7},{2,98},{3,1},{4,100},{5,3},{6,102},{7,5},{8,104},{9,1... | collective-permute-start | bytes 3145736 | tf_op jit(solution)/shard_map/ppermute | solution.py:268
  52.6 67.9 %collective-permute-start.5 = (bf16[2048,256]{1,0:T(8,128)(2,1)S(1)}, bf16[2048,256]{1,0:T(8,128)(2,1)}, u32[]{:S(2)}, u32[]{:S(2)}) collective-permute-start(bf16[2048,256]{1,0:T(8,128)(2,1)S(1)} %constant_dynamic-update-slice_fusion.refs_1_), channel_id=1, source_target_pairs={{0,32},{1,3},{2,34},{3,5},{4,36},{5,7},{6,38},{7,1},{8,40},{9,11},... | collective-permute-start | bytes 3145736 | tf_op jit(solution)/shard_map/ppermute | solution.py:268
  54.8 70.2 %copy-start.2 = (bf16[2048,256]{1,0:T(8,128)(2,1)S(1)}, bf16[2048,256]{1,0:T(8,128)(2,1)}, u32[]{:S(2)}) copy-start(bf16[2048,256]{1,0:T(8,128)(2,1)} %refs_5_.1) | copy-start | bytes 3145732
  63.4 75.4 %collective-permute-start.7 = (bf16[2048,256]{1,0:T(8,128)(2,1)S(1)}, bf16[2048,256]{1,0:T(8,128)(2,1)}, u32[]{:S(2)}, u32[]{:S(2)}) collective-permute-start(bf16[2048,256]{1,0:T(8,128)(2,1)S(1)} %constant_dynamic-update-slice_fusion.refs_1_), channel_id=1, source_target_pairs={{0,1},{1,0},{2,3},{3,2},{4,5},{5,4},{6,7},{7,6},{8,9},{9,8},{10,11... | collective-permute-start | bytes 3145736 | tf_op jit(solution)/shard_map/ppermute | solution.py:271
  108.1 30.7 %collective-permute-start.10 = (bf16[2048,256]{1,0:T(8,128)(2,1)S(1)}, bf16[2048,256]{1,0:T(8,128)(2,1)}, u32[]{:S(2)}, u32[]{:S(2)}) collective-permute-start(bf16[2048,256]{1,0:T(8,128)(2,1)S(1)} %collective-permute-done.6.refs_4_), channel_id=1, source_target_pairs={{0,1},{1,0},{2,3},{3,2},{4,5},{5,4},{6,7},{7,6},{8,9},{9,8},{10,11... | collective-permute-start | bytes 3145736 | tf_op jit(solution)/shard_map/ppermute | solution.py:271
  117.9 20.9 %collective-permute-start.8 = (bf16[2048,256]{1,0:T(8,128)(2,1)}, bf16[2048,256]{1,0:T(8,128)(2,1)}, u32[]{:S(2)}, u32[]{:S(2)}) collective-permute-start(bf16[2048,256]{1,0:T(8,128)(2,1)} %collective-permute-done.4.refs_2_), channel_id=1, source_target_pairs={{0,1},{1,0},{2,3},{3,2},{4,5},{5,4},{6,7},{7,6},{8,9},{9,8},{10,11... | collective-permute-start | bytes 3145736 | tf_op jit(solution)/shard_map/ppermute | solution.py:271
  120.4 18.4 %collective-permute-start.9 = (bf16[2048,256]{1,0:T(8,128)(2,1)}, bf16[2048,256]{1,0:T(8,128)(2,1)}, u32[]{:S(2)}, u32[]{:S(2)}) collective-permute-start(bf16[2048,256]{1,0:T(8,128)(2,1)} %collective-permute-done.5.refs_3_), channel_id=1, source_target_pairs={{0,1},{1,0},{2,3},{3,2},{4,5},{5,4},{6,7},{7,6},{8,9},{9,8},{10,11... | collective-permute-start | bytes 3145736 | tf_op jit(solution)/shard_map/ppermute | solution.py:271
  137.4 1.4 copy-start.5
  138.8 20.3 %copy-start.3 = (bf16[512,256]{1,0:T(8,128)(2,1)S(1)}, bf16[512,256]{1,0:T(8,128)(2,1)}, u32[]{:S(2)}) copy-start(bf16[512,256]{1,0:T(8,128)(2,1)} %refs_6_.1) | copy-start | bytes 786436
  138.8 20.4 %copy-start.4 = (f32[256]{0:T(256)S(1)}, f32[256]{0:T(256)}, u32[]{:S(2)}) copy-start(f32[256]{0:T(256)} %param.14) | copy-start | bytes 3076
  159.2 1.6 copy-start.6

commit v3 on v2

v3 whole, which is shorter than its diff:
```python
import jax
import jax.numpy as jnp
from jax import lax
from jax.experimental import pallas as pl
from jax.experimental.pallas import tpu as pltpu
from jax.sharding import PartitionSpec as P

LANES = 128
MIB = 2**20
CHUNK = 1024
WIDEN = 256
UNROLL = 32


def one_hot(mask):
    return jnp.where(mask, 1.0, 0.0).astype(jnp.bfloat16)


def send_body(list_ref, feats_ref, out_ref, hot_ref):
    columns = list_ref[...].T
    rows = feats_ref.shape[0]
    lane = lax.broadcasted_iota(jnp.int32, (LANES, LANES), 1)
    for j in range(columns.shape[1]):
        wanted = jnp.broadcast_to(columns[:, j : j + 1], (LANES, LANES))
        for t in range(rows // LANES):
            hot_ref[j * LANES : (j + 1) * LANES, t * LANES : (t + 1) * LANES] = one_hot(
                wanted == lane + t * LANES
            )
    out_ref[...] = jnp.dot(
        hot_ref[...], feats_ref[...], preferred_element_type=jnp.float32
    ).astype(out_ref.dtype)


def gather_to_send(feats, send_list, piece, pieces, so_far):
    rows, width = feats.shape
    count = send_list.size
    group = 8 * LANES
    steps = count // group // pieces
    first = piece * steps
    inputs = [send_list.reshape(count // LANES, LANES), feats]
    in_specs = [
        pl.BlockSpec((8, LANES), lambda i: (first + i, 0)),
        pl.BlockSpec((rows, width), lambda i: (0, 0)),
    ]
    aliases = {}
    if so_far is not None:
        inputs.append(so_far)
        in_specs.append(pl.BlockSpec(memory_space=pl.ANY))
        aliases = {2: 0}
    return pl.pallas_call(
        lambda list_ref, feats_ref, *refs: send_body(list_ref, feats_ref, refs[-2], refs[-1]),
        grid=(steps,),
        in_specs=in_specs,
        out_specs=pl.BlockSpec((group, width), lambda i: (first + i, 0)),
        out_shape=jax.ShapeDtypeStruct((count, width), feats.dtype),
        scratch_shapes=[pltpu.VMEM((group, rows), jnp.bfloat16)],
        input_output_aliases=aliases,
        compiler_params=pltpu.CompilerParams(vmem_limit_bytes=14 * MIB),
        cost_estimate=pl.CostEstimate(
            flops=4 * count * rows * width // pieces,
            bytes_accessed=2 * count * width // pieces,
            transcendentals=0,
        ),
        name="gather_to_send",
    )(*inputs)


def local_body(part, code_ref, feats_ref, out_ref, count_ref):
    rows = feats_ref.shape[0]
    blocks = rows // LANES
    groups, contract = code_ref.shape
    high = code_ref[...] >> 7
    low = code_ref[...] & (LANES - 1)
    tall = lax.broadcasted_iota(jnp.int32, (blocks * part, contract), 0)
    short = lax.broadcasted_iota(jnp.int32, (LANES, contract), 0)
    for g in range(groups):
        left = one_hot(tall == high[g : g + 1, :])
        right = one_hot(short == low[g : g + 1, :])
        counts = lax.dot_general(
            left, right, (((1,), (1,)), ((), ())), preferred_element_type=jnp.float32
        ).astype(jnp.bfloat16)
        for b in range(blocks):
            count_ref[g * part : (g + 1) * part, b * LANES : (b + 1) * LANES] = counts[
                b * part : (b + 1) * part, :
            ]
    out_ref[...] = jnp.dot(count_ref[...], feats_ref[...], preferred_element_type=jnp.float32)


def local_sums(feats, neighbours, length):
    rows, width = feats.shape
    slots = neighbours.shape[1]
    part = 2 * LANES // slots
    used = jnp.arange(slots, dtype=jnp.int32)[None, :] < length[:, None]
    place = (jnp.arange(rows, dtype=jnp.int32) % part)[:, None]
    high = (neighbours // LANES) * part + place
    code = jnp.where(used, high * LANES + neighbours % LANES, -1).reshape(-1, part * slots)
    groups = 16
    return pl.pallas_call(
        lambda *refs: local_body(part, *refs),
        grid=(rows // (groups * part),),
        in_specs=[
            pl.BlockSpec((groups, part * slots), lambda i: (i, 0)),
            pl.BlockSpec((rows, width), lambda i: (0, 0)),
        ],
        out_specs=pl.BlockSpec((groups * part, width), lambda i: (i, 0)),
        out_shape=jax.ShapeDtypeStruct((rows, width), jnp.float32),
        scratch_shapes=[pltpu.VMEM((groups * part, rows), jnp.bfloat16)],
        compiler_params=pltpu.CompilerParams(vmem_limit_bytes=14 * MIB),
        cost_estimate=pl.CostEstimate(
            flops=10 * rows * rows * width, bytes_accessed=4 * rows * width, transcendentals=0
        ),
        name="local_sums",
    )(code, feats)


def load_table(sources, stage, table, sem):
    copies = []
    start = 0
    for source in sources:
        count = source.shape[0]
        size = min(count, CHUNK)
        for first in range(0, count, size):
            copies.append(
                pltpu.make_async_copy(
                    source.at[pl.ds(first, size)],
                    stage.at[pl.ds(start, size)],
                    sem.at[len(copies)],
                )
            )
            start += size
    for copy in copies:
        copy.start()
    table[2 * start : 2 * start + 8, :] = jnp.zeros((8, LANES), jnp.float32)
    start = 0
    for copy in copies:
        copy.wait()
        size = copy.dst_ref.shape[0]

        def widen(i, carry, first=start):
            at = first + i * WIDEN
            block = stage[pl.ds(pl.multiple_of(at, WIDEN), WIDEN), :].astype(jnp.float32)
            table[pl.ds(2 * at, WIDEN, stride=2), :] = block[:, :LANES]
            table[pl.ds(2 * at + 1, WIDEN, stride=2), :] = block[:, LANES:]
            return carry

        lax.fori_loop(0, size // WIDEN, widen, 0)
        start += size


def chunk_count(sources):
    return sum(-(-source.shape[0] // CHUNK) for source in sources)


def add_rows(index_ref, table, out_ref, slots, unroll):
    def step(i, carry):
        base = (i * unroll // LANES) * (slots * LANES) + i * unroll % LANES
        for u in range(unroll):
            v = i * unroll + u
            total = None
            for k in range(slots):
                at = index_ref[base + k * LANES + u]
                row = table[pl.ds(pl.multiple_of(at, 2), 2), :]
                total = row if total is None else total + row
            out_ref[pl.ds(pl.multiple_of(2 * v, 2), 2), :] = total
        return carry

    lax.fori_loop(0, out_ref.shape[0] // (2 * unroll), step, 0)


def fetch(pairs, sem):
    copies = [
        pltpu.make_async_copy(source, target, sem.at[i]) for i, (source, target) in enumerate(pairs)
    ]
    for copy in copies:
        copy.start()
    return copies


def halves(ref, start, size):
    return [ref[pl.ds(2 * start + h, size, stride=2), :] for h in range(2)]


def list_body(slots, pieces, index_hbm, loc_hbm, *refs):
    sources, (out_ref, index, loc, stage, table, sem, extra) = refs[:pieces], refs[pieces:]
    ready, later = fetch([(index_hbm, index), (loc_hbm, loc)], extra)
    load_table(sources, stage, table, sem)
    ready.wait()
    add_rows(index, table, out_ref, slots, UNROLL)
    later.wait()

    def merge(i, carry):
        start = pl.multiple_of(i * WIDEN, WIDEN)
        for h, part in enumerate(halves(out_ref, start, WIDEN)):
            own = loc[pl.ds(start, WIDEN), h * LANES : (h + 1) * LANES]
            out_ref[pl.ds(2 * start + h, WIDEN, stride=2), :] = part + own
        return carry

    lax.fori_loop(0, loc.shape[0] // WIDEN, merge, 0)


def row_index(neighbours, length, count):
    used = jnp.arange(neighbours.shape[1], dtype=jnp.int32)[None, :] < length[:, None]
    rows, slots = neighbours.shape
    index = jnp.where(used, neighbours * 2, 2 * count).T.reshape(slots, rows // LANES, LANES)
    return index.transpose(1, 0, 2).reshape(-1)


def list_sums(index, slots, sources, loc):
    width = sources[0].shape[1]
    count = sum(source.shape[0] for source in sources)
    rows = index.shape[0] // slots
    return pl.pallas_call(
        lambda *refs: list_body(slots, len(sources), *refs),
        in_specs=[pl.BlockSpec(memory_space=pltpu.HBM)] * (2 + len(sources)),
        out_specs=pl.BlockSpec(memory_space=pltpu.VMEM),
        out_shape=pltpu.HBM((2 * rows, LANES), jnp.float32),
        scratch_shapes=[
            pltpu.SMEM(index.shape, index.dtype),
            pltpu.VMEM(loc.shape, loc.dtype),
            pltpu.VMEM((count, width), sources[0].dtype),
            pltpu.VMEM((2 * count + 8, LANES), jnp.float32),
            pltpu.SemaphoreType.DMA((chunk_count(sources),)),
            pltpu.SemaphoreType.DMA((2,)),
        ],
        compiler_params=pltpu.CompilerParams(vmem_limit_bytes=34 * MIB),
        cost_estimate=pl.CostEstimate(
            flops=20_000_000_000, bytes_accessed=2 * count * width, transcendentals=0
        ),
        name="list_sums",
    )(index, loc, *sources)


def layer_body(slots, pieces, index_hbm, *refs):
    sources, refs = refs[:pieces], refs[pieces:]
    outside, (bias_ref, out_ref), refs = refs[:4], refs[4:6], refs[6:]
    index, inside, (stage, table, last, sem, extra) = refs[0], refs[1:5], refs[5:]
    ready, *later = fetch([(index_hbm, index), *zip(outside, inside)], extra)
    load_table(sources, stage, table, sem)
    ready.wait()
    add_rows(index, table, last, slots, UNROLL)
    for copy in later:
        copy.wait()
    partial, degree, feats, weight = inside
    rows, width = feats.shape

    def finish(i, carry):
        start = pl.multiple_of(i * WIDEN, WIDEN)
        span = pl.ds(start, WIDEN)
        divisor = degree[span, :]
        means = [
            ((mine + theirs) / divisor).astype(jnp.bfloat16)
            for mine, theirs in zip(halves(partial, start, WIDEN), halves(last, start, WIDEN))
        ]
        result = jnp.dot(feats[span, :], weight[:width, :], preferred_element_type=jnp.float32)
        result += jnp.dot(
            jnp.concatenate(means, axis=1), weight[width:, :], preferred_element_type=jnp.float32
        )
        result += bias_ref[...]
        out_ref[span, :] = jnp.maximum(result, 0.0).astype(out_ref.dtype)
        return carry

    lax.fori_loop(0, rows // WIDEN, finish, 0)


def layer(index, slots, sources, partial, degree, feats, weight, bias):
    width = sources[0].shape[1]
    count = sum(source.shape[0] for source in sources)
    rows = feats.shape[0]
    outside = [partial, degree, feats, weight]
    vmem = pl.BlockSpec(memory_space=pltpu.VMEM)
    return pl.pallas_call(
        lambda *refs: layer_body(slots, len(sources), *refs),
        in_specs=[pl.BlockSpec(memory_space=pltpu.HBM)] * (1 + len(sources) + len(outside)) + [vmem],
        out_specs=vmem,
        out_shape=jax.ShapeDtypeStruct((rows, width), feats.dtype),
        scratch_shapes=[pltpu.SMEM(index.shape, index.dtype)]
        + [pltpu.VMEM(array.shape, array.dtype) for array in outside]
        + [
            pltpu.VMEM((count, width), feats.dtype),
            pltpu.VMEM((2 * count + 8, LANES), jnp.float32),
            pltpu.VMEM((2 * rows, LANES), jnp.float32),
            pltpu.SemaphoreType.DMA((chunk_count(sources),)),
            pltpu.SemaphoreType.DMA((1 + len(outside),)),
        ],
        compiler_params=pltpu.CompilerParams(vmem_limit_bytes=30 * MIB),
        cost_estimate=pl.CostEstimate(
            flops=20_000_000_000, bytes_accessed=2 * count * width, transcendentals=0
        ),
        name="layer",
    )(index, *sources, *outside, bias)


RING = 4
STRIDES = {"x": 32, "z": 8, "y": 2}
ORDERS = (("y", "z", "x"), ("z", "x", "y"))


def moved(stage, step):
    pairs = []
    for device in range(2 * RING**3):
        stride = STRIDES[ORDERS[device % 2][stage]]
        at = device // stride % RING
        pairs.append((device, device + (step(at) - at) * stride))
    return pairs


def swapped(block):
    return lax.ppermute(block, "dom", [(device, device ^ 1) for device in range(2 * RING**3)])


def gray(value):
    return value ^ (value >> 1)


def hub_place(hub, rows_each):
    me = lax.axis_index("dom")
    device = hub // rows_each
    apart = {
        name: ((device // stride % RING), (me // stride % RING)) for name, stride in STRIDES.items()
    }
    near = {name: gray(theirs ^ mine) for name, (theirs, mine) in apart.items()}
    far = {name: gray((theirs - mine) & (RING - 1)) for name, (theirs, mine) in apart.items()}
    core = device & 1

    def place(order):
        return (far[order[2]] * RING + near[order[1]]) * RING + near[order[0]]

    block = jnp.where(core == 0, place(ORDERS[0]), place(ORDERS[1]))
    block += (core ^ (me & 1)) * RING**3
    return block * rows_each + hub % rows_each


def per_device(
    feats, hub_feat, weight, bias, loc_nbr, loc_len, hub_nbr, hub_len, send_list, halo_nbr, halo_len
):
    rows, width = feats.shape
    peers, slots = send_list.shape
    each = hub_feat.shape[0]

    block, outgoing, piece = hub_feat, None, 0
    for stage in range(2):
        for flip in (1, 3):
            other = lax.ppermute(block, "dom", moved(stage, lambda i, flip=flip: i ^ flip))
            outgoing = gather_to_send(feats, send_list, piece, 4, outgoing)
            block = jnp.concatenate([block, other], axis=0)
            block, outgoing = lax.optimization_barrier((block, outgoing))
            piece += 1
    hubs = [block] + [
        lax.ppermute(block, "dom", moved(2, lambda i, shift=shift: (i - shift) % RING))
        for shift in (1, 3, 2)
    ]
    arrived = lax.all_to_all(
        outgoing.reshape(peers, slots, width), "dom", split_axis=0, concat_axis=0, tiled=True
    ).reshape(peers * slots, width)
    loc = local_sums(feats, loc_nbr, loc_len)
    hub_index = row_index(hub_place(hub_nbr, each), hub_len, peers * each)
    halo_index = row_index(halo_nbr, halo_len, peers * slots)
    hubs, loc, hub_index, halo_index = lax.optimization_barrier((hubs, loc, hub_index, halo_index))
    hubs = hubs + [swapped(part) for part in hubs]
    partial = list_sums(hub_index, hub_nbr.shape[1], hubs, loc)
    degree = jnp.broadcast_to(
        (loc_len + hub_len + halo_len).astype(jnp.float32)[:, None], (rows, LANES)
    )
    return layer(
        halo_index, halo_nbr.shape[1], [arrived], partial, degree, feats, weight, bias[None, :]
    )


def solution(mesh):
    placed = (
        P("dom", None),
        P("dom", None),
        P(),
        P(),
        P("dom", None),
        P("dom"),
        P("dom", None),
        P("dom"),
        P("dom", None),
        P("dom", None),
        P("dom"),
    )
    return jax.shard_map(
        per_device, mesh=mesh, in_specs=placed, out_specs=P("dom", None), check_vma=False
    )
```

time: 183 us -> 134 us (0.73)
  waiting for transfers between devices: 63.3 us -> 25 us
  local copies, waits for them, and re-layouts: 19.4 us -> 14 us
  other arithmetic: 5.51 us -> 1.44 us
  Pallas kernels: 66.3 us -> 63.2 us
  starting transfers between devices: 26.9 us -> 29 us
    ppermute x11, waiting for transfers between devices: 63.3 us -> 15.7 us  [the longest x3 9.14 us: per_device(): lax.ppermute(block, 'dom', moved(2, lambda i, shift=shift: (i - shift) %...]
    all_to_all x1, waiting for transfers between devices: 0.01 us -> 9.34 us  [per_device(): lax.all_to_all(outgoing.reshape(peers, slots, width), 'dom', split_axis=0...]
    reshape x5 -> x2, local copies, waits for them, and re-layouts: 6.68 us -> 1.68 us  [the longest x1 1.61 us: local_sums(): jnp.where(used, high * LANES + neighbours % LANES, -1)]
    select_n x4 -> x1, local copies, waits for them, and re-layouts: 5.24 us -> 1.31 us  [local_sums(): jnp.where(used, high * LANES + neighbours % LANES, -1)]
    unnamed x29, local copies, waits for them, and re-layouts: 7.13 us -> 10.7 us
    pallas_call x3 -> x6, Pallas kernels: 53.9 us -> 50.8 us  [the longest x1 19.4 us: layer(): pl.pallas_call(lambda *refs: layer_body(slots, len(sources), *refs), in_s...]
    concatenate x3 -> x4, other arithmetic: 2.58 us -> 0.13 us  [per_device(): block = jnp.concatenate([block, other], axis=0)]
    select_n x3 -> x1, other arithmetic: 2.2 us -> 0.14 us  [local_sums(): jnp.where(used, high * LANES + neighbours % LANES, -1)]
  transfers between devices with their start and end apart: 12 -> 12, of which waited for: 6 -> 7; matrix products, arithmetic and copies ran while one was open for 9% -> 4% of each run, Pallas kernels for 25% -> 33%
where the time goes in v3:
time: 134 us; the launch traced here: 133 us
  Pallas kernels  63.2 us (47%)
  starting transfers between devices  29 us (22%)
  waiting for transfers between devices  25 us (19%)
  local copies, waits for them, and re-layouts  14 us (10%)
  other arithmetic  1.44 us (1%)
    pallas_call x1, Pallas kernels, layer(): pl.pallas_call(lambda *refs: layer_body(slots, len(sources), *refs), in_s...  19.4 us
    pallas_call x1, Pallas kernels, list_sums(): pl.pallas_call(lambda *refs: list_body(slots, len(sources), *refs), in_sp...  18.3 us
    pallas_call x4, Pallas kernels, gather_to_send(): pl.pallas_call(lambda list_ref, feats_ref, *refs: send_body(list_ref, fea...  13.1 us
    pallas_call x1, Pallas kernels, local_sums(): pl.pallas_call(lambda *refs: local_body(part, *refs), grid=(rows // (grou...  12.4 us
    all_to_all x1, starting transfers between devices, per_device(): lax.all_to_all(outgoing.reshape(peers, slots, width), 'dom', split_axis=0...  10.9 us
    unnamed x29, local copies, waits for them, and re-layouts  10.7 us
    all_to_all x1, waiting for transfers between devices, per_device(): lax.all_to_all(outgoing.reshape(peers, slots, width), 'dom', split_axis=0...  9.34 us
    ppermute x3, waiting for transfers between devices, per_device(): lax.ppermute(block, 'dom', moved(2, lambda i, shift=shift: (i - shift) %...  9.14 us
  transfers between devices with their start and end apart: 12, of which 7 were waited for; matrix products, arithmetic and copies ran while one was open for 4% of the time, Pallas kernels for 33%

profile of v3, /device:TPU:1, one launch (start us, length us, event | category | flops | bytes accessed | tf_op | source)
XLA Modules:
  0.0 133.2 jit_solution(10476049618664085804)
XLA Ops:
  0.0 2.5 %collective-permute-start = (bf16[128,256]{1,0:T(8,128)(2,1)}, bf16[128,256]{1,0:T(8,128)(2,1)S(1)}, u32[]{:S(2)}, u32[]{:S(2)}) collective-permute-start(bf16[128,256]{1,0:T(8,128)(2,1)} %param.12), channel_id=1, source_target_pairs={{0,2},{1,9},{2,0},{3,11},{4,6},{5,13},{6,4},{7,15},{8,10},{9,1},{1... | collective-permute-start | bytes 196616 | tf_op jit(solution)/shard_map/ppermute | solution.py:343
  2.5 0.8 copy.17
  3.3 0.1 reshape.40.list_ref
  3.4 1.2 copy-done.3
  4.6 3.3 %gather_to_send.4.refs_0_ = bf16[8192,256]{1,0:T(8,128)(2,1)S(1)} custom-call(s32[64,128]{1,0:T(8,128)S(1)} %reshape.40.list_ref, bf16[2048,256]{1,0:T(8,128)(2,1)S(1)} %copy-done.3), custom_call_target="tpu_custom_call" | custom-call | flops 4294967296 | bytes 1048576 | tf_op jit(solution)/shard_map/gather_to_send/pallas_call | solution.py:50
  8.0 2.3 %collective-permute-start.1 = (bf16[256,256]{1,0:T(8,128)(2,1)S(1)}, bf16[256,256]{1,0:T(8,128)(2,1)S(1)}, u32[]{:S(2)}, u32[]{:S(2)}) collective-permute-start(bf16[256,256]{1,0:T(8,128)(2,1)S(1)} %pad_maximum_fusion.3), channel_id=1, source_target_pairs={{0,6},{1,25},{2,4},{3,27},{4,2},{5,29},{6,0},{7,31},{8,14},{9,17},... | collective-permute-start | bytes 393224 | tf_op jit(solution)/shard_map/ppermute | solution.py:343
  10.3 3.3 %gather_to_send.5.refs_0_ = bf16[8192,256]{1,0:T(8,128)(2,1)S(1)} custom-call(s32[64,128]{1,0:T(8,128)S(1)} %reshape.40.list_ref, bf16[2048,256]{1,0:T(8,128)(2,1)S(1)} %copy-done.3, bf16[8192,256]{1,0:T(8,128)(2,1)S(1)} %gather_to_send.4.refs_0_), custom_call_target="tpu_custom_call", output_to_operand_aliasing={{}: (2, {})} | custom-call | flops 4294967296 | bytes 1048576 | tf_op jit(solution)/shard_map/gather_to_send/pallas_call | solution.py:50
  13.6 0.0 collective-permute-done.1
  13.6 0.0 copy-start.8
  13.6 0.0 copy-start.13
  13.6 0.0 copy-start.4
  13.6 1.3 collective-permute-start.2
  14.9 3.3 %gather_to_send.6.refs_0_ = bf16[8192,256]{1,0:T(8,128)(2,1)S(1)} custom-call(s32[64,128]{1,0:T(8,128)S(1)} %reshape.40.list_ref, bf16[2048,256]{1,0:T(8,128)(2,1)S(1)} %copy-done.3, bf16[8192,256]{1,0:T(8,128)(2,1)S(1)} %gather_to_send.5.refs_0_), custom_call_target="tpu_custom_call", output_to_operand_aliasing={{}: (2, {})} | custom-call | flops 4294967296 | bytes 1048576 | tf_op jit(solution)/shard_map/gather_to_send/pallas_call | solution.py:50
  18.2 1.9 %copy-done = bf16[8192,256]{1,0:T(8,128)(2,1)} copy-done((bf16[8192,256]{1,0:T(8,128)(2,1)}, bf16[8192,256]{1,0:T(8,128)(2,1)S(1)}, u32[]{:S(2)}) %copy-start) | copy-done | bytes 4194328
  20.2 0.0 collective-permute-done.2
  20.2 1.9 %collective-permute-start.3 = (bf16[1024,256]{1,0:T(8,128)(2,1)S(1)}, bf16[1024,256]{1,0:T(8,128)(2,1)S(1)}, u32[]{:S(2)}, u32[]{:S(2)}) collective-permute-start(bf16[1024,256]{1,0:T(8,128)(2,1)S(1)} %pad_maximum_fusion.1), channel_id=1, source_target_pairs={{0,24},{1,97},{2,26},{3,99},{4,28},{5,101},{6,30},{7,103},{8,16},{... | collective-permute-start | bytes 1572872 | tf_op jit(solution)/shard_map/ppermute | solution.py:343
  22.1 0.1 fusion.4
  22.4 2.2 %copy-done.1 = bf16[8192,256]{1,0:T(8,128)(2,1)S(1)} copy-done((bf16[8192,256]{1,0:T(8,128)(2,1)S(1)}, bf16[8192,256]{1,0:T(8,128)(2,1)}, u32[]{:S(2)}) %copy-start.1) | copy-done | bytes 4194328
  24.5 3.3 %gather_to_send.7 = bf16[8192,256]{1,0:T(8,128)(2,1)S(1)} custom-call(s32[64,128]{1,0:T(8,128)S(1)} %reshape.40.list_ref, bf16[2048,256]{1,0:T(8,128)(2,1)S(1)} %copy-done.4, bf16[8192,256]{1,0:T(8,128)(2,1)S(1)} %copy-done.1), custom_call_target="tpu_custom_call", output_to_operand_aliasing={{}: (2, {})} | custom-call | flops 4294967296 | bytes 1048576 | tf_op jit(solution)/shard_map/gather_to_send/pallas_call | solution.py:50
  27.8 1.9 %copy-done.2 = bf16[8192,256]{1,0:T(8,128)(2,1)} copy-done((bf16[8192,256]{1,0:T(8,128)(2,1)}, bf16[8192,256]{1,0:T(8,128)(2,1)S(1)}, u32[]{:S(2)}) %copy-start.2) | copy-done | bytes 4194328
  29.8 0.1 collective-permute-done.3
  29.8 0.1 pad_maximum_fusion.refs_2_
  29.9 2.8 %collective-permute-start.4 = (bf16[2048,256]{1,0:T(8,128)(2,1)S(1)}, bf16[2048,256]{1,0:T(8,128)(2,1)S(1)}, u32[]{:S(2)}, u32[]{:S(2)}) collective-permute-start(bf16[2048,256]{1,0:T(8,128)(2,1)S(1)} %pad_maximum_fusion.refs_2_), channel_id=1, source_target_pairs={{0,96},{1,7},{2,98},{3,1},{4,100},{5,3},{6,102},{7,5},{8,104},{9,1... | collective-permute-start | bytes 3145736 | tf_op jit(solution)/shard_map/ppermute | solution.py:349
  32.7 0.0 collective-permute-start.5
  32.7 1.6 %collective-permute-start.6 = (bf16[2048,256]{1,0:T(8,128)(2,1)S(1)}, bf16[2048,256]{1,0:T(8,128)(2,1)}, u32[]{:S(2)}, u32[]{:S(2)}) collective-permute-start(bf16[2048,256]{1,0:T(8,128)(2,1)S(1)} %pad_maximum_fusion.refs_2_), channel_id=1, source_target_pairs={{0,64},{1,5},{2,66},{3,7},{4,68},{5,1},{6,70},{7,3},{8,72},{9,13},... | collective-permute-start | bytes 3145736 | tf_op jit(solution)/shard_map/ppermute | solution.py:349
  34.4 10.9 %all-to-all-start = ((bf16[128,64,256]{2,1,0:T(8,128)(2,1)}), bf16[128,64,256]{2,1,0:T(8,128)(2,1)}, u32[]{:S(2)}, u32[]{:S(2)}) async-start(bf16[128,64,256]{2,1,0:T(8,128)(2,1)} %bitcast.19), calls=%async_computation | async-start | bytes 8388608 | tf_op jit(solution)/shard_map/all_to_all | solution.py:352
  45.3 1.2 fusion.21
  46.5 1.3 copy.18
  47.8 1.6 %reshape.41.refs_0_ = s32[128,256]{1,0:T(8,128)S(1)} reshape(s32[2048,16]{1,0:T(8,128)} %copy.18) | data formatting | bytes 262144 | tf_op jit(solution)/shard_map/reshape | solution.py:96
  49.4 12.4 %local_sums.1.refs_1_ = f32[2048,256]{1,0:T(8,128)S(1)} custom-call(s32[128,256]{1,0:T(8,128)S(1)} %reshape.41.refs_0_, bf16[2048,256]{1,0:T(8,128)(2,1)S(1)} %copy-done.4), custom_call_target="tpu_custom_call" | custom-call | flops 10737418240 | bytes 2097152 | tf_op jit(solution)/shard_map/local_sums/pallas_call | solution.py:98
  61.8 0.0 collective-permute-done.4.refs_3_
  61.8 0.0 collective-permute-done.5.refs_4_
  61.8 9.1 %collective-permute-done.6.refs_5_ = bf16[2048,256]{1,0:T(8,128)(2,1)} collective-permute-done((bf16[2048,256]{1,0:T(8,128)(2,1)S(1)}, bf16[2048,256]{1,0:T(8,128)(2,1)}, u32[]{:S(2)}, u32[]{:S(2)}) %collective-permute-start.6) | collective-permute-done | bytes 1048608 | tf_op jit(solution)/shard_map/ppermute | solution.py:349
  71.0 5.1 %collective-permute-start.7 = (bf16[2048,256]{1,0:T(8,128)(2,1)S(1)}, bf16[2048,256]{1,0:T(8,128)(2,1)S(1)}, u32[]{:S(2)}, u32[]{:S(2)}) collective-permute-start(bf16[2048,256]{1,0:T(8,128)(2,1)S(1)} %pad_maximum_fusion.refs_2_), channel_id=1, source_target_pairs={{0,1},{1,0},{2,3},{3,2},{4,5},{5,4},{6,7},{7,6},{8,9},{9,8},{10,11... | collective-permute-start | bytes 3145736 | tf_op jit(solution)/shard_map/ppermute | solution.py:308
  76.1 0.0 collective-permute-start.8
  76.1 0.5 collective-permute-start.9
  76.6 0.0 collective-permute-start.10
  76.6 1.8 %collective-permute-done.7.refs_6_ = bf16[2048,256]{1,0:T(8,128)(2,1)S(1)} collective-permute-done((bf16[2048,256]{1,0:T(8,128)(2,1)S(1)}, bf16[2048,256]{1,0:T(8,128)(2,1)S(1)}, u32[]{:S(2)}, u32[]{:S(2)}) %collective-permute-start.7) | collective-permute-done | bytes 1048608 | tf_op jit(solution)/shard_map/ppermute | solution.py:308
  78.4 3.0 %collective-permute-done.8.refs_7_ = bf16[2048,256]{1,0:T(8,128)(2,1)S(1)} collective-permute-done((bf16[2048,256]{1,0:T(8,128)(2,1)S(1)}, bf16[2048,256]{1,0:T(8,128)(2,1)S(1)}, u32[]{:S(2)}, u32[]{:S(2)}) %collective-permute-start.8) | collective-permute-done | bytes 1048608 | tf_op jit(solution)/shard_map/ppermute | solution.py:308
  81.4 0.2 collective-permute-done.9.refs_8_
  81.6 1.5 %collective-permute-done.10.refs_9_ = bf16[2048,256]{1,0:T(8,128)(2,1)S(1)} collective-permute-done((bf16[2048,256]{1,0:T(8,128)(2,1)}, bf16[2048,256]{1,0:T(8,128)(2,1)S(1)}, u32[]{:S(2)}, u32[]{:S(2)}) %collective-permute-start.10) | collective-permute-done | bytes 1048608 | tf_op jit(solution)/shard_map/ppermute | solution.py:308
  83.1 18.3 %list_sums.1.refs_2_ = f32[4096,128]{1,0:T(8,128)} custom-call(s32[16384]{0:T(1024)S(1)} %get-tuple-element.29.refs_0_, f32[2048,256]{1,0:T(8,128)S(1)} %local_sums.1.refs_1_, bf16[2048,256]{1,0:T(8,128)(2,1)S(1)} %pad_maximum_fusion.refs_2_, bf16[2048,256]{1,0:T(8,128)(2,1)S(1)} %collective-permute-done.4.refs_3_, ...), custom_call_target="tpu_custom_call" | custom-call | flops 20000000000 | bytes 8388608 | tf_op jit(solution)/shard_map/list_sums/pallas_call | solution.py:212
  101.4 9.3 %all-to-all-done = bf16[128,64,256]{2,1,0:T(8,128)(2,1)} async-done(((bf16[128,64,256]{2,1,0:T(8,128)(2,1)}), bf16[128,64,256]{2,1,0:T(8,128)(2,1)}, u32[]{:S(2)}, u32[]{:S(2)}) %all-to-all-start) | async-done | bytes 4194336 | tf_op jit(solution)/shard_map/all_to_all | solution.py:352
  110.7 0.3 broadcast_in_dim.15.refs_3_
  111.1 0.0 copy-start.5
  111.1 0.9 copy-done.5
  112.0 1.6 %copy-done.7 = f32[4096,128]{1,0:T(8,128)S(1)} copy-done((f32[4096,128]{1,0:T(8,128)S(1)}, f32[4096,128]{1,0:T(8,128)}, u32[]{:S(2)}) %copy-start.7) | copy-done | bytes 2097176
  113.6 19.4 %layer.1 = bf16[2048,256]{1,0:T(8,128)(2,1)} custom-call(s32[16384]{0:T(1024)S(1)} %get-tuple-element.27.refs_0_, bf16[8192,256]{1,0:T(8,128)(2,1)} %bitcast.9.refs_1_, f32[4096,128]{1,0:T(8,128)S(1)} %copy-done.7, f32[2048,128]{1,0:T(8,128)S(1)} %broadcast_in_dim.15.refs_3_, bf16[2048,256]{1,0:T(8,128)(2,1)S(1)} %copy-done.4, ...), custom_call_target="tpu_custom_call" | custom-call | flops 20000000000 | bytes 4194304 | tf_op jit(solution)/shard_map/layer/pallas_call | solution.py:271
  (24 shorter events, 0.1 us)
Async XLA Ops:
  0.0 7.9 %collective-permute-start = (bf16[128,256]{1,0:T(8,128)(2,1)}, bf16[128,256]{1,0:T(8,128)(2,1)S(1)}, u32[]{:S(2)}, u32[]{:S(2)}) collective-permute-start(bf16[128,256]{1,0:T(8,128)(2,1)} %param.12), channel_id=1, source_target_pairs={{0,2},{1,9},{2,0},{3,11},{4,6},{5,13},{6,4},{7,15},{8,10},{9,1},{1... | collective-permute-start | bytes 196616 | tf_op jit(solution)/shard_map/ppermute | solution.py:343
  3.4 1.2 copy-start.3
  4.6 3.3 %copy-start.10 = (bf16[128,256]{1,0:T(8,128)(2,1)S(1)}, bf16[128,256]{1,0:T(8,128)(2,1)}, u32[]{:S(2)}) copy-start(bf16[128,256]{1,0:T(8,128)(2,1)} %param.12) | copy-start | bytes 196612
  8.0 5.6 %collective-permute-start.1 = (bf16[256,256]{1,0:T(8,128)(2,1)S(1)}, bf16[256,256]{1,0:T(8,128)(2,1)S(1)}, u32[]{:S(2)}, u32[]{:S(2)}) collective-permute-start(bf16[256,256]{1,0:T(8,128)(2,1)S(1)} %pad_maximum_fusion.3), channel_id=1, source_target_pairs={{0,6},{1,25},{2,4},{3,27},{4,2},{5,29},{6,0},{7,31},{8,14},{9,17},... | collective-permute-start | bytes 393224 | tf_op jit(solution)/shard_map/ppermute | solution.py:343
  13.6 8.5 %copy-start.8 = (s32[2048,16]{0,1:T(8,128)S(1)}, s32[2048,16]{0,1:T(8,128)}, u32[]{:S(2)}) copy-start(s32[2048,16]{0,1:T(8,128)} %param.15) | copy-start | bytes 393220
  13.6 8.5 %copy-start.13 = (s32[2048]{0:T(1024)S(1)}, s32[2048]{0:T(1024)}, u32[]{:S(2)}) copy-start(s32[2048]{0:T(1024)} %param.16) | copy-start | bytes 24580
  13.6 8.7 %copy-start.4 = (bf16[2048,256]{1,0:T(8,128)(2,1)S(1)}, bf16[2048,256]{1,0:T(8,128)(2,1)}, u32[]{:S(2)}) copy-start(bf16[2048,256]{1,0:T(8,128)(2,1)} %refs_4_.1) | copy-start | bytes 3145732
  13.6 6.5 %collective-permute-start.2 = (bf16[512,256]{1,0:T(8,128)(2,1)S(1)}, bf16[512,256]{1,0:T(8,128)(2,1)S(1)}, u32[]{:S(2)}, u32[]{:S(2)}) collective-permute-start(bf16[512,256]{1,0:T(8,128)(2,1)S(1)} %pad_maximum_fusion.2), channel_id=1, source_target_pairs={{0,8},{1,33},{2,10},{3,35},{4,12},{5,37},{6,14},{7,39},{8,0},{9,41... | collective-permute-start | bytes 786440 | tf_op jit(solution)/shard_map/ppermute | solution.py:343
  18.2 2.0 %copy-start = (bf16[8192,256]{1,0:T(8,128)(2,1)}, bf16[8192,256]{1,0:T(8,128)(2,1)S(1)}, u32[]{:S(2)}) copy-start(bf16[8192,256]{1,0:T(8,128)(2,1)S(1)} %gather_to_send.6.refs_0_) | copy-start | bytes 12582916
  20.2 9.6 %collective-permute-start.3 = (bf16[1024,256]{1,0:T(8,128)(2,1)S(1)}, bf16[1024,256]{1,0:T(8,128)(2,1)S(1)}, u32[]{:S(2)}, u32[]{:S(2)}) collective-permute-start(bf16[1024,256]{1,0:T(8,128)(2,1)S(1)} %pad_maximum_fusion.1), channel_id=1, source_target_pairs={{0,24},{1,97},{2,26},{3,99},{4,28},{5,101},{6,30},{7,103},{8,16},{... | collective-permute-start | bytes 1572872 | tf_op jit(solution)/shard_map/ppermute | solution.py:343
  22.3 2.2 %copy-start.1 = (bf16[8192,256]{1,0:T(8,128)(2,1)S(1)}, bf16[8192,256]{1,0:T(8,128)(2,1)}, u32[]{:S(2)}) copy-start(bf16[8192,256]{1,0:T(8,128)(2,1)} %copy-done) | copy-start | bytes 12582916
  27.8 2.0 %copy-start.2 = (bf16[8192,256]{1,0:T(8,128)(2,1)}, bf16[8192,256]{1,0:T(8,128)(2,1)S(1)}, u32[]{:S(2)}) copy-start(bf16[8192,256]{1,0:T(8,128)(2,1)S(1)} %gather_to_send.7) | copy-start | bytes 12582916
  29.9 31.9 %collective-permute-start.4 = (bf16[2048,256]{1,0:T(8,128)(2,1)S(1)}, bf16[2048,256]{1,0:T(8,128)(2,1)S(1)}, u32[]{:S(2)}, u32[]{:S(2)}) collective-permute-start(bf16[2048,256]{1,0:T(8,128)(2,1)S(1)} %pad_maximum_fusion.refs_2_), channel_id=1, source_target_pairs={{0,96},{1,7},{2,98},{3,1},{4,100},{5,3},{6,102},{7,5},{8,104},{9,1... | collective-permute-start | bytes 3145736 | tf_op jit(solution)/shard_map/ppermute | solution.py:349
  32.7 29.1 %collective-permute-start.5 = (bf16[2048,256]{1,0:T(8,128)(2,1)S(1)}, bf16[2048,256]{1,0:T(8,128)(2,1)}, u32[]{:S(2)}, u32[]{:S(2)}) collective-permute-start(bf16[2048,256]{1,0:T(8,128)(2,1)S(1)} %pad_maximum_fusion.refs_2_), channel_id=1, source_target_pairs={{0,32},{1,3},{2,34},{3,5},{4,36},{5,7},{6,38},{7,1},{8,40},{9,11},... | collective-permute-start | bytes 3145736 | tf_op jit(solution)/shard_map/ppermute | solution.py:349
  32.7 38.3 %collective-permute-start.6 = (bf16[2048,256]{1,0:T(8,128)(2,1)S(1)}, bf16[2048,256]{1,0:T(8,128)(2,1)}, u32[]{:S(2)}, u32[]{:S(2)}) collective-permute-start(bf16[2048,256]{1,0:T(8,128)(2,1)S(1)} %pad_maximum_fusion.refs_2_), channel_id=1, source_target_pairs={{0,64},{1,5},{2,66},{3,7},{4,68},{5,1},{6,70},{7,3},{8,72},{9,13},... | collective-permute-start | bytes 3145736 | tf_op jit(solution)/shard_map/ppermute | solution.py:349
  34.3 10.9 %copy-start.9 = (s32[2048,8]{0,1:T(8,128)S(1)}, s32[2048,8]{0,1:T(8,128)}, u32[]{:S(2)}) copy-start(s32[2048,8]{0,1:T(8,128)} %param.17) | copy-start | bytes 196612
  34.3 10.9 %copy-start.11 = (s32[2048]{0:T(1024)S(1)}, s32[2048]{0:T(1024)}, u32[]{:S(2)}) copy-start(s32[2048]{0:T(1024)} %param.18) | copy-start | bytes 24580
  34.4 10.9 %copy-start.12 = (s32[2048]{0:T(1024)S(1)}, s32[2048]{0:T(1024)}, u32[]{:S(2)}) copy-start(s32[2048]{0:T(1024)} %param.21) | copy-start | bytes 24580
  34.4 76.4 %all-to-all-start = ((bf16[128,64,256]{2,1,0:T(8,128)(2,1)}), bf16[128,64,256]{2,1,0:T(8,128)(2,1)}, u32[]{:S(2)}, u32[]{:S(2)}) async-start(bf16[128,64,256]{2,1,0:T(8,128)(2,1)} %bitcast.19), calls=%async_computation | async-start | bytes 8388608 | tf_op jit(solution)/shard_map/all_to_all | solution.py:352
  71.0 7.4 %collective-permute-start.7 = (bf16[2048,256]{1,0:T(8,128)(2,1)S(1)}, bf16[2048,256]{1,0:T(8,128)(2,1)S(1)}, u32[]{:S(2)}, u32[]{:S(2)}) collective-permute-start(bf16[2048,256]{1,0:T(8,128)(2,1)S(1)} %pad_maximum_fusion.refs_2_), channel_id=1, source_target_pairs={{0,1},{1,0},{2,3},{3,2},{4,5},{5,4},{6,7},{7,6},{8,9},{9,8},{10,11... | collective-permute-start | bytes 3145736 | tf_op jit(solution)/shard_map/ppermute | solution.py:308
  76.1 5.3 %collective-permute-start.8 = (bf16[2048,256]{1,0:T(8,128)(2,1)S(1)}, bf16[2048,256]{1,0:T(8,128)(2,1)S(1)}, u32[]{:S(2)}, u32[]{:S(2)}) collective-permute-start(bf16[2048,256]{1,0:T(8,128)(2,1)S(1)} %collective-permute-done.4.refs_3_), channel_id=1, source_target_pairs={{0,1},{1,0},{2,3},{3,2},{4,5},{5,4},{6,7},{7,6},{8,9},{9,8},{10,11... | collective-permute-start | bytes 3145736 | tf_op jit(solution)/shard_map/ppermute | solution.py:308
  76.1 5.5 %collective-permute-start.9 = (bf16[2048,256]{1,0:T(8,128)(2,1)}, bf16[2048,256]{1,0:T(8,128)(2,1)S(1)}, u32[]{:S(2)}, u32[]{:S(2)}) collective-permute-start(bf16[2048,256]{1,0:T(8,128)(2,1)} %collective-permute-done.5.refs_4_), channel_id=1, source_target_pairs={{0,1},{1,0},{2,3},{3,2},{4,5},{5,4},{6,7},{7,6},{8,9},{9,8},{10,11... | collective-permute-start | bytes 3145736 | tf_op jit(solution)/shard_map/ppermute | solution.py:308
  76.6 6.5 %collective-permute-start.10 = (bf16[2048,256]{1,0:T(8,128)(2,1)}, bf16[2048,256]{1,0:T(8,128)(2,1)S(1)}, u32[]{:S(2)}, u32[]{:S(2)}) collective-permute-start(bf16[2048,256]{1,0:T(8,128)(2,1)} %collective-permute-done.6.refs_5_), channel_id=1, source_target_pairs={{0,1},{1,0},{2,3},{3,2},{4,5},{5,4},{6,7},{7,6},{8,9},{9,8},{10,11... | collective-permute-start | bytes 3145736 | tf_op jit(solution)/shard_map/ppermute | solution.py:308
  76.6 34.5 %copy-start.6 = (f32[256]{0:T(256)S(1)}, f32[256]{0:T(256)}, u32[]{:S(2)}) copy-start(f32[256]{0:T(256)} %param.14) | copy-start | bytes 3076
  111.1 1.0 copy-start.5
  112.0 1.6 %copy-start.7 = (f32[4096,128]{1,0:T(8,128)S(1)}, f32[4096,128]{1,0:T(8,128)}, u32[]{:S(2)}) copy-start(f32[4096,128]{1,0:T(8,128)} %list_sums.1.refs_2_) | copy-start | bytes 6291460

commit v4 on v3

--- a/solution.py
+++ b/solution.py
@@ -10,55 +10,97 @@
 CHUNK = 1024
 WIDEN = 256
 UNROLL = 32
+SEND_PEERS = 16
+SEND_TURNS = ((0, 3), (3, 5))
 
 
 def one_hot(mask):
     return jnp.where(mask, 1.0, 0.0).astype(jnp.bfloat16)
 
 
-def send_body(list_ref, feats_ref, out_ref, hot_ref):
-    columns = list_ref[...].T
-    rows = feats_ref.shape[0]
-    lane = lax.broadcasted_iota(jnp.int32, (LANES, LANES), 1)
-    for j in range(columns.shape[1]):
-        wanted = jnp.broadcast_to(columns[:, j : j + 1], (LANES, LANES))
-        for t in range(rows // LANES):
-            hot_ref[j * LANES : (j + 1) * LANES, t * LANES : (t + 1) * LANES] = one_hot(
-                wanted == lane + t * LANES
-            )
-    out_ref[...] = jnp.dot(
-        hot_ref[...], feats_ref[...], preferred_element_type=jnp.float32
-    ).astype(out_ref.dtype)
-
-
-def gather_to_send(feats, send_list, piece, pieces, so_far):
+def widen_rows(source, first, table, start, size):
+    def step(i, carry):
+        at = start + i * WIDEN
+        block = source[pl.ds(pl.multiple_of(first + i * WIDEN, WIDEN), WIDEN), :]
+        block = block.astype(jnp.float32)
+        table[pl.ds(2 * at, WIDEN, stride=2), :] = block[:, :LANES]
+        table[pl.ds(2 * at + 1, WIDEN, stride=2), :] = block[:, LANES:]
+        return carry
+
+    lax.fori_loop(0, size // WIDEN, step, 0)
+
+
+def send_body(first, slots, index_hbm, feats_ref, out_ref, index, table, stage, sem):
+    step = pl.program_id(0)
+
+    @pl.when(step == 0)
+    def _():
+        copy = pltpu.make_async_copy(index_hbm, index, sem)
+        copy.start()
+        widen_rows(feats_ref, 0, table, 0, feats_ref.shape[0])
+        copy.wait()
+
+    here = out_ref.shape[0] // slots
+    peers = index.shape[0] // slots
+
+    def gather(buffer, peer):
+        at = first + step * here + peer
+        for s in range(slots):
+            row = table[pl.ds(pl.multiple_of(index[s * peers + at], 2), 2), :]
+            stage[pl.ds(2 * (buffer * slots + s), 2), :] = row
+
+    def pack(buffer, peer):
+        both = [stage[pl.ds(2 * buffer * slots + h, slots, stride=2), :] for h in range(2)]
+        rows = jnp.concatenate(both, axis=1).astype(out_ref.dtype)
+        out_ref[pl.ds(pl.multiple_of(peer * slots, slots), slots), :] = rows
+
+    gather(0, 0)
+
+    def pair(i, carry):
+        peer = 2 * i
+        pack(0, peer)
+        gather(1, peer + 1)
+        pack(1, peer + 1)
+        gather(0, jnp.minimum(peer + 2, here - 1))
+        return carry
+
+    lax.fori_loop(0, here // 2, pair, 0)
+
+
+def gather_to_send(feats, index, slots, part, so_far):
     rows, width = feats.shape
-    count = send_list.size
-    group = 8 * LANES
-    steps = count // group // pieces
-    first = piece * steps
-    inputs = [send_list.reshape(count // LANES, LANES), feats]
+    count = index.shape[0]
+    group = SEND_PEERS * slots
+    first, steps = part
+    inputs = [index, feats]
     in_specs = [
-        pl.BlockSpec((8, LANES), lambda i: (first + i, 0)),
+        pl.BlockSpec(memory_space=pl.ANY),
         pl.BlockSpec((rows, width), lambda i: (0, 0)),
     ]
     aliases = {}
     if so_far is not None:
         inputs.append(so_far)
-        in_specs.append(pl.BlockSpec(memory_space=pl.ANY))
+        in_specs.append(pl.BlockSpec(memory_space=pltpu.HBM))
         aliases = {2: 0}
     return pl.pallas_call(
-        lambda list_ref, feats_ref, *refs: send_body(list_ref, feats_ref, refs[-2], refs[-1]),
+        lambda index_hbm, feats_ref, *refs: send_body(
+            SEND_PEERS * first, slots, index_hbm, feats_ref, *refs[-5:]
+        ),
         grid=(steps,),
         in_specs=in_specs,
         out_specs=pl.BlockSpec((group, width), lambda i: (first + i, 0)),
-        out_shape=jax.ShapeDtypeStruct((count, width), feats.dtype),
-        scratch_shapes=[pltpu.VMEM((group, rows), jnp.bfloat16)],
+        out_shape=pltpu.HBM((count, width), feats.dtype),
+        scratch_shapes=[
+            pltpu.SMEM(index.shape, index.dtype),
+            pltpu.VMEM((2 * rows, LANES), jnp.float32),
+            pltpu.VMEM((4 * slots, LANES), jnp.float32),
+            pltpu.SemaphoreType.DMA,
+        ],
         input_output_aliases=aliases,
         compiler_params=pltpu.CompilerParams(vmem_limit_bytes=14 * MIB),
         cost_estimate=pl.CostEstimate(
-            flops=4 * count * rows * width // pieces,
-            bytes_accessed=2 * count * width // pieces,
+            flops=4 * group * steps * rows * width,
+            bytes_accessed=2 * group * steps * width,
             transcendentals=0,
         ),
         name="gather_to_send",
@@ -107,44 +149,33 @@
         scratch_shapes=[pltpu.VMEM((groups * part, rows), jnp.bfloat16)],
         compiler_params=pltpu.CompilerParams(vmem_limit_bytes=14 * MIB),
         cost_estimate=pl.CostEstimate(
-            flops=10 * rows * rows * width, bytes_accessed=4 * rows * width, transcendentals=0
+            flops=4 * rows * rows * width, bytes_accessed=4 * rows * width, transcendentals=0
         ),
         name="local_sums",
     )(code, feats)
 
 
-def load_table(sources, stage, table, sem):
+def start_table(sources, stage, sem):
     copies = []
     start = 0
     for source in sources:
-        count = source.shape[0]
-        size = min(count, CHUNK)
-        for first in range(0, count, size):
-            copies.append(
-                pltpu.make_async_copy(
-                    source.at[pl.ds(first, size)],
-                    stage.at[pl.ds(start, size)],
-                    sem.at[len(copies)],
-                )
+        size = min(source.shape[0], CHUNK)
+        for first in range(0, source.shape[0], size):
+            copy = pltpu.make_async_copy(
+                source.at[pl.ds(first, size)], stage.at[pl.ds(start, size)], sem.at[len(copies)]
             )
+            copy.start()
+            copies.append((copy, start, size))
             start += size
-    for copy in copies:
-        copy.start()
-    table[2 * start : 2 * start + 8, :] = jnp.zeros((8, LANES), jnp.float32)
-    start = 0
-    for copy in copies:
+    return copies
+
+
+def finish_table(copies, stage, table):
+    count = stage.shape[0]
+    table[2 * count : 2 * count + 8, :] = jnp.zeros((8, LANES), jnp.float32)
+    for copy, start, size in copies:
         copy.wait()
-        size = copy.dst_ref.shape[0]
-
-        def widen(i, carry, first=start):
-            at = first + i * WIDEN
-            block = stage[pl.ds(pl.multiple_of(at, WIDEN), WIDEN), :].astype(jnp.float32)
-            table[pl.ds(2 * at, WIDEN, stride=2), :] = block[:, :LANES]
-            table[pl.ds(2 * at + 1, WIDEN, stride=2), :] = block[:, LANES:]
-            return carry
-
-        lax.fori_loop(0, size // WIDEN, widen, 0)
-        start += size
+        widen_rows(stage, start, table, start, size)
 
 
 def chunk_count(sources):
@@ -182,8 +213,9 @@
 
 def list_body(slots, pieces, index_hbm, loc_hbm, *refs):
     sources, (out_ref, index, loc, stage, table, sem, extra) = refs[:pieces], refs[pieces:]
+    copies = start_table(sources, stage, sem)
     ready, later = fetch([(index_hbm, index), (loc_hbm, loc)], extra)
-    load_table(sources, stage, table, sem)
+    finish_table(copies, stage, table)
     ready.wait()
     add_rows(index, table, out_ref, slots, UNROLL)
     later.wait()
@@ -224,7 +256,7 @@
         ],
         compiler_params=pltpu.CompilerParams(vmem_limit_bytes=34 * MIB),
         cost_estimate=pl.CostEstimate(
-            flops=20_000_000_000, bytes_accessed=2 * count * width, transcendentals=0
+            flops=27_000_000_000, bytes_accessed=2 * count * width, transcendentals=0
         ),
         name="list_sums",
     )(index, loc, *sources)
@@ -234,8 +266,9 @@
     sources, refs = refs[:pieces], refs[pieces:]
     outside, (bias_ref, out_ref), refs = refs[:4], refs[4:6], refs[6:]
     index, inside, (stage, table, last, sem, extra) = refs[0], refs[1:5], refs[5:]
+    copies = start_table(sources, stage, sem)
     ready, *later = fetch([(index_hbm, index), *zip(outside, inside)], extra)
-    load_table(sources, stage, table, sem)
+    finish_table(copies, stage, table)
     ready.wait()
     add_rows(index, table, last, slots, UNROLL)
     for copy in later:
@@ -282,9 +315,9 @@
             pltpu.SemaphoreType.DMA((chunk_count(sources),)),
             pltpu.SemaphoreType.DMA((1 + len(outside),)),
         ],
-        compiler_params=pltpu.CompilerParams(vmem_limit_bytes=30 * MIB),
+        compiler_params=pltpu.CompilerParams(vmem_limit_bytes=62 * MIB),
         cost_estimate=pl.CostEstimate(
-            flops=20_000_000_000, bytes_accessed=2 * count * width, transcendentals=0
+            flops=27_000_000_000, bytes_accessed=2 * count * width, transcendentals=0
         ),
         name="layer",
     )(index, *sources, *outside, bias)
@@ -318,16 +351,22 @@
     apart = {
         name: ((device // stride % RING), (me // stride % RING)) for name, stride in STRIDES.items()
     }
-    near = {name: gray(theirs ^ mine) for name, (theirs, mine) in apart.items()}
-    far = {name: gray((theirs - mine) & (RING - 1)) for name, (theirs, mine) in apart.items()}
+    apart = {name: (theirs - mine) & (RING - 1) for name, (theirs, mine) in apart.items()}
     core = device & 1
 
     def place(order):
-        return (far[order[2]] * RING + near[order[1]]) * RING + near[order[0]]
+        return (gray(apart[order[2]]) * RING + apart[order[1]]) * RING + apart[order[0]]
 
     block = jnp.where(core == 0, place(ORDERS[0]), place(ORDERS[1]))
     block += (core ^ (me & 1)) * RING**3
     return block * rows_each + hub % rows_each
+
+
+def along(block, stage, shifts):
+    return [
+        lax.ppermute(block, "dom", moved(stage, lambda i, shift=shift: (i - shift) % RING))
+        for shift in shifts
+    ]
 
 
 def per_device(
@@ -337,30 +376,30 @@
     peers, slots = send_list.shape
     each = hub_feat.shape[0]
 
-    block, outgoing, piece = hub_feat, None, 0
-    for stage in range(2):
-        for flip in (1, 3):
-            other = lax.ppermute(block, "dom", moved(stage, lambda i, flip=flip: i ^ flip))
-            outgoing = gather_to_send(feats, send_list, piece, 4, outgoing)
-            block = jnp.concatenate([block, other], axis=0)
-            block, outgoing = lax.optimization_barrier((block, outgoing))
-            piece += 1
-    hubs = [block] + [
-        lax.ppermute(block, "dom", moved(2, lambda i, shift=shift: (i - shift) % RING))
-        for shift in (1, 3, 2)
-    ]
+    send_index = send_list.T.reshape(-1) * 2
+    block = jnp.concatenate([hub_feat] + along(hub_feat, 0, (1, 2, 3)), axis=0)
+    block, send_index = lax.optimization_barrier((block, send_index))
+    others = along(block, 1, (1, 2, 3))
+    outgoing = gather_to_send(feats, send_index, slots, SEND_TURNS[0], None)
+    block = jnp.concatenate([block] + others, axis=0)
+    block, outgoing = lax.optimization_barrier((block, outgoing))
+    hubs = [block] + along(block, 2, (1, 3, 2))
+    outgoing = gather_to_send(feats, send_index, slots, SEND_TURNS[1], outgoing)
+    outgoing, loc_nbr = lax.optimization_barrier((outgoing, loc_nbr))
     arrived = lax.all_to_all(
         outgoing.reshape(peers, slots, width), "dom", split_axis=0, concat_axis=0, tiled=True
     ).reshape(peers * slots, width)
     loc = local_sums(feats, loc_nbr, loc_len)
     hub_index = row_index(hub_place(hub_nbr, each), hub_len, peers * each)
     halo_index = row_index(halo_nbr, halo_len, peers * slots)
-    hubs, loc, hub_index, halo_index = lax.optimization_barrier((hubs, loc, hub_index, halo_index))
-    hubs = hubs + [swapped(part) for part in hubs]
-    partial = list_sums(hub_index, hub_nbr.shape[1], hubs, loc)
     degree = jnp.broadcast_to(
         (loc_len + hub_len + halo_len).astype(jnp.float32)[:, None], (rows, LANES)
     )
+    hubs, loc, hub_index, halo_index, degree = lax.optimization_barrier(
+        (hubs, loc, hub_index, halo_index, degree)
+    )
+    hubs = hubs + [swapped(part) for part in hubs]
+    partial = list_sums(hub_index, hub_nbr.shape[1], hubs, loc)
     return layer(
         halo_index, halo_nbr.shape[1], [arrived], partial, degree, feats, weight, bias[None, :]
     )

time: 134 us -> 120 us (0.90)
  waiting for transfers between devices: 25 us -> 10.7 us
  local copies, waits for them, and re-layouts: 14 us -> 3.31 us
  starting transfers between devices: 29 us -> 37.2 us
  other arithmetic: 1.44 us -> 4.34 us
    unnamed x29 -> x8, local copies, waits for them, and re-layouts: 10.7 us -> 1.24 us
    ppermute x7 -> x9, waiting for transfers between devices: 9.21 us -> 0.41 us  [along(): lax.ppermute(block, 'dom', moved(stage, lambda i, shift=shift: (i - shift...]
    ppermute x4, starting transfers between devices: 5.63 us -> 11.6 us  [swapped(): lax.ppermute(block, 'dom', [(device, device ^ 1) for device in range(2 *...]
    all_to_all x1, waiting for transfers between devices: 9.34 us -> 3.8 us  [per_device(): lax.all_to_all(outgoing.reshape(peers, slots, width), 'dom', split_axis=0...]
    ppermute x7 -> x9, starting transfers between devices: 12.4 us -> 16.4 us  [along(): lax.ppermute(block, 'dom', moved(stage, lambda i, shift=shift: (i - shift...]
    all_to_all x1, starting transfers between devices: 10.9 us -> 9.1 us  [per_device(): lax.all_to_all(outgoing.reshape(peers, slots, width), 'dom', split_axis=0...]
    pallas_call x1, Pallas kernels: 19.4 us -> 21 us  [layer(): pl.pallas_call(lambda *refs: layer_body(slots, len(sources), *refs), in_s...]
    pallas_call x4 -> x2, Pallas kernels: 13.1 us -> 12.2 us  [gather_to_send(): pl.pallas_call(lambda index_hbm, feats_ref, *refs: send_body(SEND_PEERS *...]
  transfers between devices with their start and end apart: 12 -> 14, of which waited for: 7 -> 7; matrix products, arithmetic and copies ran while one was open for 4% -> 5% of each run, Pallas kernels for 33% -> 36%
where the time goes in v4:
time: 120 us
  Pallas kernels  64 us (53%)
  starting transfers between devices  37.2 us (31%)
  waiting for transfers between devices  10.7 us (9%)
  other arithmetic  4.34 us (4%)
  local copies, waits for them, and re-layouts  3.31 us (3%)
    pallas_call x1, Pallas kernels, layer(): pl.pallas_call(lambda *refs: layer_body(slots, len(sources), *refs), in_s...  21 us
    pallas_call x1, Pallas kernels, list_sums(): pl.pallas_call(lambda *refs: list_body(slots, len(sources), *refs), in_sp...  18.4 us
    ppermute x9, starting transfers between devices, along(): lax.ppermute(block, 'dom', moved(stage, lambda i, shift=shift: (i - shift...  16.4 us
    pallas_call x1, Pallas kernels, local_sums(): pl.pallas_call(lambda *refs: local_body(part, *refs), grid=(rows // (grou...  12.4 us
    pallas_call x2, Pallas kernels, gather_to_send(): pl.pallas_call(lambda index_hbm, feats_ref, *refs: send_body(SEND_PEERS *...  12.2 us
    ppermute x4, starting transfers between devices, swapped(): lax.ppermute(block, 'dom', [(device, device ^ 1) for device in range(2 *...  11.6 us
    all_to_all x1, starting transfers between devices, per_device(): lax.all_to_all(outgoing.reshape(peers, slots, width), 'dom', split_axis=0...  9.1 us
    ppermute x4, waiting for transfers between devices, swapped(): lax.ppermute(block, 'dom', [(device, device ^ 1) for device in range(2 *...  6.48 us
  transfers between devices with their start and end apart: 14, of which 7 were waited for; matrix products, arithmetic and copies ran while one was open for 5% of the time, Pallas kernels for 36%

profile of v4, /device:TPU:1, one launch (start us, length us, event | category | flops | bytes accessed | tf_op | source)
XLA Modules:
  0.0 119.7 jit_solution(16602899102825748349)
XLA Ops:
  0.0 4.4 %collective-permute-start.1 = (bf16[128,256]{1,0:T(8,128)(2,1)}, bf16[128,256]{1,0:T(8,128)(2,1)S(1)}, u32[]{:S(2)}, u32[]{:S(2)}) collective-permute-start(bf16[128,256]{1,0:T(8,128)(2,1)} %param.12), channel_id=1, source_target_pairs={{0,4},{1,17},{2,6},{3,19},{4,0},{5,21},{6,2},{7,23},{8,12},{9,25},... | collective-permute-start | bytes 196616 | tf_op jit(solution)/shard_map/ppermute | solution.py:367
  4.4 0.4 collective-permute-start
  4.9 1.0 collective-permute-start.2
  5.9 0.8 multiply_bitcast_fusion.index_hbm
  6.7 0.7 add_convert_fusion
  7.4 1.8 %fusion.23 = (s32[16384]{0:T(1024)S(1)}, s32[16384]{0:T(1024)}) fusion(s32[2048,8]{0,1:T(8,128)} %param.17, s32[]{:T(128)S(6)} %and.118, s32[]{:T(128)S(6)} %select_n.108, s32[]{:T(128)S(6)} %select_n.104, s32[]{:T(128)S(6)} %select_n.100, s32[2048]{0:T(1024)} %param.18, s32[2048,8]{0,1:T(8,128)} %param.20, s32[2048]{0:T(1024)} %param.21), kind=kLoop, calls=%fused_computation.58 | loop fusion | flops 1949696 | bytes 278544 | tf_op jit(solution)/shard_map/reshape | solution.py:237
  9.2 0.0 collective-permute-done.1
  9.2 0.0 collective-permute-done
  9.2 0.2 collective-permute-done.2
  9.4 0.9 pad_maximum_fusion.1
  10.3 1.3 %collective-permute-start.5 = (bf16[512,256]{1,0:T(8,128)(2,1)S(1)}, bf16[512,256]{1,0:T(8,128)(2,1)S(1)}, u32[]{:S(2)}, u32[]{:S(2)}) collective-permute-start(bf16[512,256]{1,0:T(8,128)(2,1)S(1)} %pad_maximum_fusion.1), channel_id=1, source_target_pairs={{0,8},{1,33},{2,10},{3,35},{4,12},{5,37},{6,14},{7,39},{8,16},{9,4... | collective-permute-start | bytes 786440 | tf_op jit(solution)/shard_map/ppermute | solution.py:367
  11.5 2.5 %collective-permute-start.4 = (bf16[512,256]{1,0:T(8,128)(2,1)S(1)}, bf16[512,256]{1,0:T(8,128)(2,1)S(1)}, u32[]{:S(2)}, u32[]{:S(2)}) collective-permute-start(bf16[512,256]{1,0:T(8,128)(2,1)S(1)} %pad_maximum_fusion.1), channel_id=1, source_target_pairs={{0,16},{1,65},{2,18},{3,67},{4,20},{5,69},{6,22},{7,71},{8,24},{9,... | collective-permute-start | bytes 786440 | tf_op jit(solution)/shard_map/ppermute | solution.py:367
  14.0 1.2 collective-permute-start.3
  15.1 1.2 %copy-done = bf16[2048,256]{1,0:T(8,128)(2,1)S(1)} copy-done((bf16[2048,256]{1,0:T(8,128)(2,1)S(1)}, bf16[2048,256]{1,0:T(8,128)(2,1)}, u32[]{:S(2)}) %copy-start) | copy-done | bytes 1048600
  16.4 5.0 %gather_to_send.2.refs_0_ = bf16[8192,256]{1,0:T(8,128)(2,1)} custom-call(s32[8192]{0:T(1024)S(1)} %multiply_bitcast_fusion.index_hbm, bf16[2048,256]{1,0:T(8,128)(2,1)S(1)} %copy-done), custom_call_target="tpu_custom_call" | custom-call | flops 6442450944 | bytes 1572864 | tf_op jit(solution)/shard_map/gather_to_send/pallas_call | solution.py:85
  21.4 0.0 copy-start.1
  21.4 0.0 collective-permute-done.5
  21.4 0.0 collective-permute-done.4
  21.4 0.0 collective-permute-done.3
  21.5 0.1 pad_maximum_fusion.refs_2_
  21.5 3.0 %collective-permute-start.8 = (bf16[2048,256]{1,0:T(8,128)(2,1)S(1)}, bf16[2048,256]{1,0:T(8,128)(2,1)}, u32[]{:S(2)}, u32[]{:S(2)}) collective-permute-start(bf16[2048,256]{1,0:T(8,128)(2,1)S(1)} %pad_maximum_fusion.refs_2_), channel_id=1, source_target_pairs={{0,64},{1,5},{2,66},{3,7},{4,68},{5,1},{6,70},{7,3},{8,72},{9,13},... | collective-permute-start | bytes 3145736 | tf_op jit(solution)/shard_map/ppermute | solution.py:367
  24.5 0.4 collective-permute-start.7
  24.9 2.3 %collective-permute-start.6 = (bf16[2048,256]{1,0:T(8,128)(2,1)S(1)}, bf16[2048,256]{1,0:T(8,128)(2,1)}, u32[]{:S(2)}, u32[]{:S(2)}) collective-permute-start(bf16[2048,256]{1,0:T(8,128)(2,1)S(1)} %pad_maximum_fusion.refs_2_), channel_id=1, source_target_pairs={{0,96},{1,7},{2,98},{3,1},{4,100},{5,3},{6,102},{7,5},{8,104},{9,1... | collective-permute-start | bytes 3145736 | tf_op jit(solution)/shard_map/ppermute | solution.py:367
  27.2 0.0 copy-done.1
  27.2 7.1 %gather_to_send.3 = bf16[8192,256]{1,0:T(8,128)(2,1)} custom-call(s32[8192]{0:T(1024)S(1)} %multiply_bitcast_fusion.index_hbm, bf16[2048,256]{1,0:T(8,128)(2,1)S(1)} %copy-done.1, bf16[8192,256]{1,0:T(8,128)(2,1)} %gather_to_send.2.refs_0_), custom_call_target="tpu_custom_call", output_to_operand_aliasing={{}: (2, {})} | custom-call | flops 10737418240 | bytes 2621440 | tf_op jit(solution)/shard_map/gather_to_send/pallas_call | solution.py:85
  34.3 0.0 copy-start.2
  34.3 0.0 copy-start.3
  34.4 9.1 %all-to-all-start = ((bf16[128,64,256]{2,1,0:T(8,128)(2,1)}), bf16[128,64,256]{2,1,0:T(8,128)(2,1)}, u32[]{:S(2)}, u32[]{:S(2)}) async-start(bf16[128,64,256]{2,1,0:T(8,128)(2,1)} %bitcast.23), calls=%async_computation | async-start | bytes 8388608 | tf_op jit(solution)/shard_map/all_to_all | solution.py:389
  43.5 0.0 copy-done.2
  43.5 0.1 fusion.4
  43.6 0.3 copy.14
  44.0 0.4 reshape.37.refs_0_
  44.4 12.4 %local_sums.1.refs_1_ = f32[2048,256]{1,0:T(8,128)S(1)} custom-call(s32[128,256]{1,0:T(8,128)S(1)} %reshape.37.refs_0_, bf16[2048,256]{1,0:T(8,128)(2,1)S(1)} %copy-done.1), custom_call_target="tpu_custom_call" | custom-call | flops 4294967296 | bytes 2097152 | tf_op jit(solution)/shard_map/local_sums/pallas_call | solution.py:140
  56.8 0.0 collective-permute-done.8.refs_5_
  56.9 0.0 collective-permute-done.7.refs_4_
  56.9 0.2 collective-permute-done.6.refs_3_
  57.0 1.3 %broadcast_in_dim.15.refs_3_ = f32[2048,128]{1,0:T(8,128)} broadcast(f32[2048]{0:T(1024)S(1)} %add_convert_fusion), dimensions={0} | broadcast | bytes 1056768 | tf_op jit(solution)/shard_map/broadcast_in_dim | solution.py:395
  58.3 11.1 %collective-permute-start.9 = (bf16[2048,256]{1,0:T(8,128)(2,1)S(1)}, bf16[2048,256]{1,0:T(8,128)(2,1)S(1)}, u32[]{:S(2)}, u32[]{:S(2)}) collective-permute-start(bf16[2048,256]{1,0:T(8,128)(2,1)S(1)} %pad_maximum_fusion.refs_2_), channel_id=1, source_target_pairs={{0,1},{1,0},{2,3},{3,2},{4,5},{5,4},{6,7},{7,6},{8,9},{9,8},{10,11... | collective-permute-start | bytes 3145736 | tf_op jit(solution)/shard_map/ppermute | solution.py:341
  69.5 0.0 collective-permute-start.10
  69.5 0.5 collective-permute-start.11
  70.0 0.0 collective-permute-start.12
  70.0 3.2 %collective-permute-done.9.refs_6_ = bf16[2048,256]{1,0:T(8,128)(2,1)S(1)} collective-permute-done((bf16[2048,256]{1,0:T(8,128)(2,1)S(1)}, bf16[2048,256]{1,0:T(8,128)(2,1)S(1)}, u32[]{:S(2)}, u32[]{:S(2)}) %collective-permute-start.9) | collective-permute-done | bytes 1048608 | tf_op jit(solution)/shard_map/ppermute | solution.py:341
  73.2 0.2 collective-permute-done.10.refs_7_
  73.5 1.5 %collective-permute-done.11.refs_8_ = bf16[2048,256]{1,0:T(8,128)(2,1)S(1)} collective-permute-done((bf16[2048,256]{1,0:T(8,128)(2,1)}, bf16[2048,256]{1,0:T(8,128)(2,1)S(1)}, u32[]{:S(2)}, u32[]{:S(2)}) %collective-permute-start.11) | collective-permute-done | bytes 1048608 | tf_op jit(solution)/shard_map/ppermute | solution.py:341
  75.0 1.5 %collective-permute-done.12.refs_9_ = bf16[2048,256]{1,0:T(8,128)(2,1)S(1)} collective-permute-done((bf16[2048,256]{1,0:T(8,128)(2,1)}, bf16[2048,256]{1,0:T(8,128)(2,1)S(1)}, u32[]{:S(2)}, u32[]{:S(2)}) %collective-permute-start.12) | collective-permute-done | bytes 1048608 | tf_op jit(solution)/shard_map/ppermute | solution.py:341
  76.5 18.4 %list_sums.1.refs_2_ = f32[4096,128]{1,0:T(8,128)} custom-call(s32[16384]{0:T(1024)S(1)} %get-tuple-element.26.refs_0_, f32[2048,256]{1,0:T(8,128)S(1)} %local_sums.1.refs_1_, bf16[2048,256]{1,0:T(8,128)(2,1)S(1)} %pad_maximum_fusion.refs_2_, bf16[2048,256]{1,0:T(8,128)(2,1)} %collective-permute-done.6.refs_3_, ...), custom_call_target="tpu_custom_call" | custom-call | flops 27000000512 | bytes 8388608 | tf_op jit(solution)/shard_map/list_sums/pallas_call | solution.py:244
  94.9 3.8 %all-to-all-done = bf16[128,64,256]{2,1,0:T(8,128)(2,1)} async-done(((bf16[128,64,256]{2,1,0:T(8,128)(2,1)}), bf16[128,64,256]{2,1,0:T(8,128)(2,1)}, u32[]{:S(2)}, u32[]{:S(2)}) %all-to-all-start) | async-done | bytes 4194336 | tf_op jit(solution)/shard_map/all_to_all | solution.py:389
  98.7 21.0 %layer.1 = bf16[2048,256]{1,0:T(8,128)(2,1)} custom-call(s32[16384]{0:T(1024)} %get-tuple-element.24.refs_0_, bf16[8192,256]{1,0:T(8,128)(2,1)} %bitcast.11.refs_1_, f32[4096,128]{1,0:T(8,128)} %list_sums.1.refs_2_, f32[2048,128]{1,0:T(8,128)} %broadcast_in_dim.15.refs_3_, bf16[2048,256]{1,0:T(8,128)(2,1)} %refs_4_.1, bf16[512,256]{1,0:T(8,128)(2,1)} %refs_5_.1, ...), custom_call_target="tpu_custom_call" | custom-call | flops 27000000512 | bytes 4194304 | tf_op jit(solution)/shard_map/layer/pallas_call | solution.py:304
  (3 shorter events, 0.0 us)
Async XLA Ops:
  0.0 9.2 %collective-permute-start.1 = (bf16[128,256]{1,0:T(8,128)(2,1)}, bf16[128,256]{1,0:T(8,128)(2,1)S(1)}, u32[]{:S(2)}, u32[]{:S(2)}) collective-permute-start(bf16[128,256]{1,0:T(8,128)(2,1)} %param.12), channel_id=1, source_target_pairs={{0,4},{1,17},{2,6},{3,19},{4,0},{5,21},{6,2},{7,23},{8,12},{9,25},... | collective-permute-start | bytes 196616 | tf_op jit(solution)/shard_map/ppermute | solution.py:367
  4.4 4.7 %collective-permute-start = (bf16[128,256]{1,0:T(8,128)(2,1)}, bf16[128,256]{1,0:T(8,128)(2,1)S(1)}, u32[]{:S(2)}, u32[]{:S(2)}) collective-permute-start(bf16[128,256]{1,0:T(8,128)(2,1)} %param.12), channel_id=1, source_target_pairs={{0,6},{1,25},{2,0},{3,27},{4,2},{5,29},{6,4},{7,31},{8,14},{9,1},{... | collective-permute-start | bytes 196616 | tf_op jit(solution)/shard_map/ppermute | solution.py:367
  4.9 4.5 %collective-permute-start.2 = (bf16[128,256]{1,0:T(8,128)(2,1)}, bf16[128,256]{1,0:T(8,128)(2,1)S(1)}, u32[]{:S(2)}, u32[]{:S(2)}) collective-permute-start(bf16[128,256]{1,0:T(8,128)(2,1)} %param.12), channel_id=1, source_target_pairs={{0,2},{1,9},{2,4},{3,11},{4,6},{5,13},{6,0},{7,15},{8,10},{9,17},{... | collective-permute-start | bytes 196616 | tf_op jit(solution)/shard_map/ppermute | solution.py:367
  10.3 11.2 %collective-permute-start.5 = (bf16[512,256]{1,0:T(8,128)(2,1)S(1)}, bf16[512,256]{1,0:T(8,128)(2,1)S(1)}, u32[]{:S(2)}, u32[]{:S(2)}) collective-permute-start(bf16[512,256]{1,0:T(8,128)(2,1)S(1)} %pad_maximum_fusion.1), channel_id=1, source_target_pairs={{0,8},{1,33},{2,10},{3,35},{4,12},{5,37},{6,14},{7,39},{8,16},{9,4... | collective-permute-start | bytes 786440 | tf_op jit(solution)/shard_map/ppermute | solution.py:367
  11.5 9.9 %collective-permute-start.4 = (bf16[512,256]{1,0:T(8,128)(2,1)S(1)}, bf16[512,256]{1,0:T(8,128)(2,1)S(1)}, u32[]{:S(2)}, u32[]{:S(2)}) collective-permute-start(bf16[512,256]{1,0:T(8,128)(2,1)S(1)} %pad_maximum_fusion.1), channel_id=1, source_target_pairs={{0,16},{1,65},{2,18},{3,67},{4,20},{5,69},{6,22},{7,71},{8,24},{9,... | collective-permute-start | bytes 786440 | tf_op jit(solution)/shard_map/ppermute | solution.py:367
  14.0 7.5 %collective-permute-start.3 = (bf16[512,256]{1,0:T(8,128)(2,1)S(1)}, bf16[512,256]{1,0:T(8,128)(2,1)S(1)}, u32[]{:S(2)}, u32[]{:S(2)}) collective-permute-start(bf16[512,256]{1,0:T(8,128)(2,1)S(1)} %pad_maximum_fusion.1), channel_id=1, source_target_pairs={{0,24},{1,97},{2,26},{3,99},{4,28},{5,101},{6,30},{7,103},{8,0},{9... | collective-permute-start | bytes 786440 | tf_op jit(solution)/shard_map/ppermute | solution.py:367
  15.1 1.2 %copy-start = (bf16[2048,256]{1,0:T(8,128)(2,1)S(1)}, bf16[2048,256]{1,0:T(8,128)(2,1)}, u32[]{:S(2)}) copy-start(bf16[2048,256]{1,0:T(8,128)(2,1)} %refs_4_.1) | copy-start | bytes 3145732
  21.4 5.8 %copy-start.1 = (bf16[2048,256]{1,0:T(8,128)(2,1)S(1)}, bf16[2048,256]{1,0:T(8,128)(2,1)}, u32[]{:S(2)}) copy-start(bf16[2048,256]{1,0:T(8,128)(2,1)} %refs_4_.1) | copy-start | bytes 3145732
  21.5 35.3 %collective-permute-start.8 = (bf16[2048,256]{1,0:T(8,128)(2,1)S(1)}, bf16[2048,256]{1,0:T(8,128)(2,1)}, u32[]{:S(2)}, u32[]{:S(2)}) collective-permute-start(bf16[2048,256]{1,0:T(8,128)(2,1)S(1)} %pad_maximum_fusion.refs_2_), channel_id=1, source_target_pairs={{0,64},{1,5},{2,66},{3,7},{4,68},{5,1},{6,70},{7,3},{8,72},{9,13},... | collective-permute-start | bytes 3145736 | tf_op jit(solution)/shard_map/ppermute | solution.py:367
  24.5 32.3 %collective-permute-start.7 = (bf16[2048,256]{1,0:T(8,128)(2,1)S(1)}, bf16[2048,256]{1,0:T(8,128)(2,1)}, u32[]{:S(2)}, u32[]{:S(2)}) collective-permute-start(bf16[2048,256]{1,0:T(8,128)(2,1)S(1)} %pad_maximum_fusion.refs_2_), channel_id=1, source_target_pairs={{0,32},{1,3},{2,34},{3,5},{4,36},{5,7},{6,38},{7,1},{8,40},{9,11},... | collective-permute-start | bytes 3145736 | tf_op jit(solution)/shard_map/ppermute | solution.py:367
  24.9 32.1 %collective-permute-start.6 = (bf16[2048,256]{1,0:T(8,128)(2,1)S(1)}, bf16[2048,256]{1,0:T(8,128)(2,1)}, u32[]{:S(2)}, u32[]{:S(2)}) collective-permute-start(bf16[2048,256]{1,0:T(8,128)(2,1)S(1)} %pad_maximum_fusion.refs_2_), channel_id=1, source_target_pairs={{0,96},{1,7},{2,98},{3,1},{4,100},{5,3},{6,102},{7,5},{8,104},{9,1... | collective-permute-start | bytes 3145736 | tf_op jit(solution)/shard_map/ppermute | solution.py:367
  34.3 9.1 %copy-start.2 = (s32[2048,16]{0,1:T(8,128)S(1)}, s32[2048,16]{0,1:T(8,128)}, u32[]{:S(2)}) copy-start(s32[2048,16]{0,1:T(8,128)} %param.15) | copy-start | bytes 393220
  34.3 9.1 %copy-start.3 = (s32[2048]{0:T(1024)S(1)}, s32[2048]{0:T(1024)}, u32[]{:S(2)}) copy-start(s32[2048]{0:T(1024)} %param.16) | copy-start | bytes 24580
  34.4 64.3 %all-to-all-start = ((bf16[128,64,256]{2,1,0:T(8,128)(2,1)}), bf16[128,64,256]{2,1,0:T(8,128)(2,1)}, u32[]{:S(2)}, u32[]{:S(2)}) async-start(bf16[128,64,256]{2,1,0:T(8,128)(2,1)} %bitcast.23), calls=%async_computation | async-start | bytes 8388608 | tf_op jit(solution)/shard_map/all_to_all | solution.py:389
  58.3 14.9 %collective-permute-start.9 = (bf16[2048,256]{1,0:T(8,128)(2,1)S(1)}, bf16[2048,256]{1,0:T(8,128)(2,1)S(1)}, u32[]{:S(2)}, u32[]{:S(2)}) collective-permute-start(bf16[2048,256]{1,0:T(8,128)(2,1)S(1)} %pad_maximum_fusion.refs_2_), channel_id=1, source_target_pairs={{0,1},{1,0},{2,3},{3,2},{4,5},{5,4},{6,7},{7,6},{8,9},{9,8},{10,11... | collective-permute-start | bytes 3145736 | tf_op jit(solution)/shard_map/ppermute | solution.py:341
  69.5 4.0 %collective-permute-start.10 = (bf16[2048,256]{1,0:T(8,128)(2,1)}, bf16[2048,256]{1,0:T(8,128)(2,1)S(1)}, u32[]{:S(2)}, u32[]{:S(2)}) collective-permute-start(bf16[2048,256]{1,0:T(8,128)(2,1)} %collective-permute-done.6.refs_3_), channel_id=1, source_target_pairs={{0,1},{1,0},{2,3},{3,2},{4,5},{5,4},{6,7},{7,6},{8,9},{9,8},{10,11... | collective-permute-start | bytes 3145736 | tf_op jit(solution)/shard_map/ppermute | solution.py:341
  69.5 5.5 %collective-permute-start.11 = (bf16[2048,256]{1,0:T(8,128)(2,1)}, bf16[2048,256]{1,0:T(8,128)(2,1)S(1)}, u32[]{:S(2)}, u32[]{:S(2)}) collective-permute-start(bf16[2048,256]{1,0:T(8,128)(2,1)} %collective-permute-done.7.refs_4_), channel_id=1, source_target_pairs={{0,1},{1,0},{2,3},{3,2},{4,5},{5,4},{6,7},{7,6},{8,9},{9,8},{10,11... | collective-permute-start | bytes 3145736 | tf_op jit(solution)/shard_map/ppermute | solution.py:341
  70.0 6.5 %collective-permute-start.12 = (bf16[2048,256]{1,0:T(8,128)(2,1)}, bf16[2048,256]{1,0:T(8,128)(2,1)S(1)}, u32[]{:S(2)}, u32[]{:S(2)}) collective-permute-start(bf16[2048,256]{1,0:T(8,128)(2,1)} %collective-permute-done.8.refs_5_), channel_id=1, source_target_pairs={{0,1},{1,0},{2,3},{3,2},{4,5},{5,4},{6,7},{7,6},{8,9},{9,8},{10,11... | collective-permute-start | bytes 3145736 | tf_op jit(solution)/shard_map/ppermute | solution.py:341

commit v5 on v4

--- a/solution.py
+++ b/solution.py
@@ -198,9 +198,10 @@
     lax.fori_loop(0, out_ref.shape[0] // (2 * unroll), step, 0)
 
 
-def fetch(pairs, sem):
+def fetch(pairs, sem, first=0):
     copies = [
-        pltpu.make_async_copy(source, target, sem.at[i]) for i, (source, target) in enumerate(pairs)
+        pltpu.make_async_copy(source, target, sem.at[first + i])
+        for i, (source, target) in enumerate(pairs)
     ]
     for copy in copies:
         copy.start()
@@ -214,8 +215,9 @@
 def list_body(slots, pieces, index_hbm, loc_hbm, *refs):
     sources, (out_ref, index, loc, stage, table, sem, extra) = refs[:pieces], refs[pieces:]
     copies = start_table(sources, stage, sem)
-    ready, later = fetch([(index_hbm, index), (loc_hbm, loc)], extra)
+    (ready,) = fetch([(index_hbm, index)], extra)
     finish_table(copies, stage, table)
+    (later,) = fetch([(loc_hbm, loc)], extra, 1)
     ready.wait()
     add_rows(index, table, out_ref, slots, UNROLL)
     later.wait()
@@ -264,11 +266,12 @@
 
 def layer_body(slots, pieces, index_hbm, *refs):
     sources, refs = refs[:pieces], refs[pieces:]
-    outside, (bias_ref, out_ref), refs = refs[:4], refs[4:6], refs[6:]
-    index, inside, (stage, table, last, sem, extra) = refs[0], refs[1:5], refs[5:]
+    outside, (bias_ref, out_hbm), refs = refs[:4], refs[4:6], refs[6:]
+    index, inside, (out_ref, stage, table, last, sem, extra, out_sem) = refs[0], refs[1:5], refs[5:]
     copies = start_table(sources, stage, sem)
-    ready, *later = fetch([(index_hbm, index), *zip(outside, inside)], extra)
+    (ready,) = fetch([(index_hbm, index)], extra)
     finish_table(copies, stage, table)
+    later = fetch(list(zip(outside, inside)), extra, 1)
     ready.wait()
     add_rows(index, table, last, slots, UNROLL)
     for copy in later:
@@ -276,8 +279,9 @@
     partial, degree, feats, weight = inside
     rows, width = feats.shape
 
-    def finish(i, carry):
-        start = pl.multiple_of(i * WIDEN, WIDEN)
+    writes = []
+    for i in range(rows // WIDEN):
+        start = i * WIDEN
         span = pl.ds(start, WIDEN)
         divisor = degree[span, :]
         means = [
@@ -290,9 +294,9 @@
         )
         result += bias_ref[...]
         out_ref[span, :] = jnp.maximum(result, 0.0).astype(out_ref.dtype)
-        return carry
-
-    lax.fori_loop(0, rows // WIDEN, finish, 0)
+        writes += fetch([(out_ref.at[span], out_hbm.at[span])], out_sem, i)
+    for write in writes:
+        write.wait()
 
 
 def layer(index, slots, sources, partial, degree, feats, weight, bias):
@@ -304,16 +308,18 @@
     return pl.pallas_call(
         lambda *refs: layer_body(slots, len(sources), *refs),
         in_specs=[pl.BlockSpec(memory_space=pltpu.HBM)] * (1 + len(sources) + len(outside)) + [vmem],
-        out_specs=vmem,
-        out_shape=jax.ShapeDtypeStruct((rows, width), feats.dtype),
+        out_specs=pl.BlockSpec(memory_space=pltpu.HBM),
+        out_shape=pltpu.HBM((rows, width), feats.dtype),
         scratch_shapes=[pltpu.SMEM(index.shape, index.dtype)]
         + [pltpu.VMEM(array.shape, array.dtype) for array in outside]
         + [
+            pltpu.VMEM((rows, width), feats.dtype),
             pltpu.VMEM((count, width), feats.dtype),
             pltpu.VMEM((2 * count + 8, LANES), jnp.float32),
             pltpu.VMEM((2 * rows, LANES), jnp.float32),
             pltpu.SemaphoreType.DMA((chunk_count(sources),)),
             pltpu.SemaphoreType.DMA((1 + len(outside),)),
+            pltpu.SemaphoreType.DMA((rows // WIDEN,)),
         ],
         compiler_params=pltpu.CompilerParams(vmem_limit_bytes=62 * MIB),
         cost_estimate=pl.CostEstimate(

time: 120 us -> 118 us (0.983)
  Pallas kernels: 64 us -> 61.5 us
    pallas_call x1, Pallas kernels: 21 us -> 18.4 us  [layer(): pl.pallas_call(lambda *refs: layer_body(slots, len(sources), *refs), in_s...]
  transfers between devices with their start and end apart: 14 -> 14, of which waited for: 7 -> 7; matrix products, arithmetic and copies ran while one was open for 5% -> 5% of each run, Pallas kernels for 36% -> 37%
where the time goes in v5:
time: 118 us; the launch traced here: 117 us
  Pallas kernels  61.5 us (52%)
  starting transfers between devices  37.2 us (32%)
  waiting for transfers between devices  10.6 us (9%)
  other arithmetic  4.34 us (4%)
  local copies, waits for them, and re-layouts  3.31 us (3%)
    pallas_call x1, Pallas kernels, list_sums(): pl.pallas_call(lambda *refs: list_body(slots, len(sources), *refs), in_sp...  18.6 us
    pallas_call x1, Pallas kernels, layer(): pl.pallas_call(lambda *refs: layer_body(slots, len(sources), *refs), in_s...  18.4 us
    ppermute x9, starting transfers between devices, along(): lax.ppermute(block, 'dom', moved(stage, lambda i, shift=shift: (i - shift...  16.4 us
    pallas_call x1, Pallas kernels, local_sums(): pl.pallas_call(lambda *refs: local_body(part, *refs), grid=(rows // (grou...  12.4 us
    pallas_call x2, Pallas kernels, gather_to_send(): pl.pallas_call(lambda index_hbm, feats_ref, *refs: send_body(SEND_PEERS *...  12.2 us
    ppermute x4, starting transfers between devices, swapped(): lax.ppermute(block, 'dom', [(device, device ^ 1) for device in range(2 *...  11.6 us
    all_to_all x1, starting transfers between devices, per_device(): lax.all_to_all(outgoing.reshape(peers, slots, width), 'dom', split_axis=0...  9.1 us
    ppermute x4, waiting for transfers between devices, swapped(): lax.ppermute(block, 'dom', [(device, device ^ 1) for device in range(2 *...  6.48 us
  transfers between devices with their start and end apart: 14, of which 7 were waited for; matrix products, arithmetic and copies ran while one was open for 5% of the time, Pallas kernels for 37%

profile of v5, /device:TPU:1, one launch (start us, length us, event | category | flops | bytes accessed | tf_op | source)
XLA Modules:
  0.0 117.0 jit_solution(15163843216797248922)
XLA Ops:
  0.0 4.4 %collective-permute-start.1 = (bf16[128,256]{1,0:T(8,128)(2,1)}, bf16[128,256]{1,0:T(8,128)(2,1)S(1)}, u32[]{:S(2)}, u32[]{:S(2)}) collective-permute-start(bf16[128,256]{1,0:T(8,128)(2,1)} %param.12), channel_id=1, source_target_pairs={{0,4},{1,17},{2,6},{3,19},{4,0},{5,21},{6,2},{7,23},{8,12},{9,25},... | collective-permute-start | bytes 196616 | tf_op jit(solution)/shard_map/ppermute | solution.py:373
  4.4 0.4 collective-permute-start
  4.9 1.0 collective-permute-start.2
  5.9 0.8 multiply_bitcast_fusion.index_hbm
  6.7 0.7 add_convert_fusion
  7.4 1.8 %fusion.23 = (s32[16384]{0:T(1024)S(1)}, s32[16384]{0:T(1024)}) fusion(s32[2048,8]{0,1:T(8,128)} %param.17, s32[]{:T(128)S(6)} %and.118, s32[]{:T(128)S(6)} %select_n.108, s32[]{:T(128)S(6)} %select_n.104, s32[]{:T(128)S(6)} %select_n.100, s32[2048]{0:T(1024)} %param.18, s32[2048,8]{0,1:T(8,128)} %param.20, s32[2048]{0:T(1024)} %param.21), kind=kLoop, calls=%fused_computation.58 | loop fusion | flops 1949696 | bytes 278544 | tf_op jit(solution)/shard_map/reshape | solution.py:239
  9.2 0.0 collective-permute-done.1
  9.2 0.0 collective-permute-done
  9.2 0.2 collective-permute-done.2
  9.4 0.9 pad_maximum_fusion.1
  10.3 1.3 %collective-permute-start.5 = (bf16[512,256]{1,0:T(8,128)(2,1)S(1)}, bf16[512,256]{1,0:T(8,128)(2,1)S(1)}, u32[]{:S(2)}, u32[]{:S(2)}) collective-permute-start(bf16[512,256]{1,0:T(8,128)(2,1)S(1)} %pad_maximum_fusion.1), channel_id=1, source_target_pairs={{0,8},{1,33},{2,10},{3,35},{4,12},{5,37},{6,14},{7,39},{8,16},{9,4... | collective-permute-start | bytes 786440 | tf_op jit(solution)/shard_map/ppermute | solution.py:373
  11.5 2.5 %collective-permute-start.4 = (bf16[512,256]{1,0:T(8,128)(2,1)S(1)}, bf16[512,256]{1,0:T(8,128)(2,1)S(1)}, u32[]{:S(2)}, u32[]{:S(2)}) collective-permute-start(bf16[512,256]{1,0:T(8,128)(2,1)S(1)} %pad_maximum_fusion.1), channel_id=1, source_target_pairs={{0,16},{1,65},{2,18},{3,67},{4,20},{5,69},{6,22},{7,71},{8,24},{9,... | collective-permute-start | bytes 786440 | tf_op jit(solution)/shard_map/ppermute | solution.py:373
  14.0 1.2 collective-permute-start.3
  15.1 1.2 %copy-done = bf16[2048,256]{1,0:T(8,128)(2,1)S(1)} copy-done((bf16[2048,256]{1,0:T(8,128)(2,1)S(1)}, bf16[2048,256]{1,0:T(8,128)(2,1)}, u32[]{:S(2)}) %copy-start) | copy-done | bytes 1048600
  16.4 5.0 %gather_to_send.2.refs_0_ = bf16[8192,256]{1,0:T(8,128)(2,1)} custom-call(s32[8192]{0:T(1024)S(1)} %multiply_bitcast_fusion.index_hbm, bf16[2048,256]{1,0:T(8,128)(2,1)S(1)} %copy-done), custom_call_target="tpu_custom_call" | custom-call | flops 6442450944 | bytes 1572864 | tf_op jit(solution)/shard_map/gather_to_send/pallas_call | solution.py:85
  21.4 0.0 copy-start.1
  21.4 0.0 collective-permute-done.5
  21.4 0.0 collective-permute-done.4
  21.4 0.0 collective-permute-done.3
  21.5 0.1 pad_maximum_fusion.refs_2_
  21.5 3.0 %collective-permute-start.8 = (bf16[2048,256]{1,0:T(8,128)(2,1)S(1)}, bf16[2048,256]{1,0:T(8,128)(2,1)}, u32[]{:S(2)}, u32[]{:S(2)}) collective-permute-start(bf16[2048,256]{1,0:T(8,128)(2,1)S(1)} %pad_maximum_fusion.refs_2_), channel_id=1, source_target_pairs={{0,64},{1,5},{2,66},{3,7},{4,68},{5,1},{6,70},{7,3},{8,72},{9,13},... | collective-permute-start | bytes 3145736 | tf_op jit(solution)/shard_map/ppermute | solution.py:373
  24.5 0.4 collective-permute-start.7
  24.9 2.3 %collective-permute-start.6 = (bf16[2048,256]{1,0:T(8,128)(2,1)S(1)}, bf16[2048,256]{1,0:T(8,128)(2,1)}, u32[]{:S(2)}, u32[]{:S(2)}) collective-permute-start(bf16[2048,256]{1,0:T(8,128)(2,1)S(1)} %pad_maximum_fusion.refs_2_), channel_id=1, source_target_pairs={{0,96},{1,7},{2,98},{3,1},{4,100},{5,3},{6,102},{7,5},{8,104},{9,1... | collective-permute-start | bytes 3145736 | tf_op jit(solution)/shard_map/ppermute | solution.py:373
  27.2 0.0 copy-done.1
  27.2 7.1 %gather_to_send.3 = bf16[8192,256]{1,0:T(8,128)(2,1)} custom-call(s32[8192]{0:T(1024)S(1)} %multiply_bitcast_fusion.index_hbm, bf16[2048,256]{1,0:T(8,128)(2,1)S(1)} %copy-done.1, bf16[8192,256]{1,0:T(8,128)(2,1)} %gather_to_send.2.refs_0_), custom_call_target="tpu_custom_call", output_to_operand_aliasing={{}: (2, {})} | custom-call | flops 10737418240 | bytes 2621440 | tf_op jit(solution)/shard_map/gather_to_send/pallas_call | solution.py:85
  34.3 0.0 copy-start.2
  34.3 0.0 copy-start.3
  34.4 9.1 %all-to-all-start = ((bf16[128,64,256]{2,1,0:T(8,128)(2,1)}), bf16[128,64,256]{2,1,0:T(8,128)(2,1)}, u32[]{:S(2)}, u32[]{:S(2)}) async-start(bf16[128,64,256]{2,1,0:T(8,128)(2,1)} %bitcast.23), calls=%async_computation | async-start | bytes 8388608 | tf_op jit(solution)/shard_map/all_to_all | solution.py:395
  43.5 0.0 copy-done.2
  43.5 0.1 fusion.4
  43.6 0.3 copy.14
  44.0 0.4 reshape.37.refs_0_
  44.4 12.4 %local_sums.1.refs_1_ = f32[2048,256]{1,0:T(8,128)S(1)} custom-call(s32[128,256]{1,0:T(8,128)S(1)} %reshape.37.refs_0_, bf16[2048,256]{1,0:T(8,128)(2,1)S(1)} %copy-done.1), custom_call_target="tpu_custom_call" | custom-call | flops 4294967296 | bytes 2097152 | tf_op jit(solution)/shard_map/local_sums/pallas_call | solution.py:140
  56.8 0.0 collective-permute-done.8.refs_5_
  56.8 0.0 collective-permute-done.7.refs_4_
  56.9 0.2 collective-permute-done.6.refs_3_
  57.0 1.3 %broadcast_in_dim.15.refs_3_ = f32[2048,128]{1,0:T(8,128)} broadcast(f32[2048]{0:T(1024)S(1)} %add_convert_fusion), dimensions={0} | broadcast | bytes 1056768 | tf_op jit(solution)/shard_map/broadcast_in_dim | solution.py:401
  58.3 11.1 %collective-permute-start.9 = (bf16[2048,256]{1,0:T(8,128)(2,1)S(1)}, bf16[2048,256]{1,0:T(8,128)(2,1)S(1)}, u32[]{:S(2)}, u32[]{:S(2)}) collective-permute-start(bf16[2048,256]{1,0:T(8,128)(2,1)S(1)} %pad_maximum_fusion.refs_2_), channel_id=1, source_target_pairs={{0,1},{1,0},{2,3},{3,2},{4,5},{5,4},{6,7},{7,6},{8,9},{9,8},{10,11... | collective-permute-start | bytes 3145736 | tf_op jit(solution)/shard_map/ppermute | solution.py:347
  69.5 0.0 collective-permute-start.10
  69.5 0.5 collective-permute-start.11
  70.0 0.0 collective-permute-start.12
  70.0 3.2 %collective-permute-done.9.refs_6_ = bf16[2048,256]{1,0:T(8,128)(2,1)S(1)} collective-permute-done((bf16[2048,256]{1,0:T(8,128)(2,1)S(1)}, bf16[2048,256]{1,0:T(8,128)(2,1)S(1)}, u32[]{:S(2)}, u32[]{:S(2)}) %collective-permute-start.9) | collective-permute-done | bytes 1048608 | tf_op jit(solution)/shard_map/ppermute | solution.py:347
  73.2 0.2 collective-permute-done.10.refs_7_
  73.5 1.5 %collective-permute-done.11.refs_8_ = bf16[2048,256]{1,0:T(8,128)(2,1)S(1)} collective-permute-done((bf16[2048,256]{1,0:T(8,128)(2,1)}, bf16[2048,256]{1,0:T(8,128)(2,1)S(1)}, u32[]{:S(2)}, u32[]{:S(2)}) %collective-permute-start.11) | collective-permute-done | bytes 1048608 | tf_op jit(solution)/shard_map/ppermute | solution.py:347
  75.0 1.5 %collective-permute-done.12.refs_9_ = bf16[2048,256]{1,0:T(8,128)(2,1)S(1)} collective-permute-done((bf16[2048,256]{1,0:T(8,128)(2,1)}, bf16[2048,256]{1,0:T(8,128)(2,1)S(1)}, u32[]{:S(2)}, u32[]{:S(2)}) %collective-permute-start.12) | collective-permute-done | bytes 1048608 | tf_op jit(solution)/shard_map/ppermute | solution.py:347
  76.5 18.6 %list_sums.1.refs_2_ = f32[4096,128]{1,0:T(8,128)} custom-call(s32[16384]{0:T(1024)S(1)} %get-tuple-element.26.refs_0_, f32[2048,256]{1,0:T(8,128)S(1)} %local_sums.1.refs_1_, bf16[2048,256]{1,0:T(8,128)(2,1)S(1)} %pad_maximum_fusion.refs_2_, bf16[2048,256]{1,0:T(8,128)(2,1)} %collective-permute-done.6.refs_3_, ...), custom_call_target="tpu_custom_call" | custom-call | flops 27000000512 | bytes 8388608 | tf_op jit(solution)/shard_map/list_sums/pallas_call | solution.py:246
  95.0 3.7 %all-to-all-done = bf16[128,64,256]{2,1,0:T(8,128)(2,1)} async-done(((bf16[128,64,256]{2,1,0:T(8,128)(2,1)}), bf16[128,64,256]{2,1,0:T(8,128)(2,1)}, u32[]{:S(2)}, u32[]{:S(2)}) %all-to-all-start) | async-done | bytes 4194336 | tf_op jit(solution)/shard_map/all_to_all | solution.py:395
  98.7 18.4 %layer.1 = bf16[2048,256]{1,0:T(8,128)(2,1)} custom-call(s32[16384]{0:T(1024)} %get-tuple-element.24.refs_0_, bf16[8192,256]{1,0:T(8,128)(2,1)} %bitcast.11.refs_1_, f32[4096,128]{1,0:T(8,128)} %list_sums.1.refs_2_, f32[2048,128]{1,0:T(8,128)} %broadcast_in_dim.15.refs_3_, bf16[2048,256]{1,0:T(8,128)(2,1)} %refs_4_.1, bf16[512,256]{1,0:T(8,128)(2,1)} %refs_5_.1, ...), custom_call_target="tpu_custom_call" | custom-call | flops 27000000512 | bytes 4194304 | tf_op jit(solution)/shard_map/layer/pallas_call | solution.py:308
  (3 shorter events, 0.0 us)
Async XLA Ops:
  0.0 9.2 %collective-permute-start.1 = (bf16[128,256]{1,0:T(8,128)(2,1)}, bf16[128,256]{1,0:T(8,128)(2,1)S(1)}, u32[]{:S(2)}, u32[]{:S(2)}) collective-permute-start(bf16[128,256]{1,0:T(8,128)(2,1)} %param.12), channel_id=1, source_target_pairs={{0,4},{1,17},{2,6},{3,19},{4,0},{5,21},{6,2},{7,23},{8,12},{9,25},... | collective-permute-start | bytes 196616 | tf_op jit(solution)/shard_map/ppermute | solution.py:373
  4.4 4.7 %collective-permute-start = (bf16[128,256]{1,0:T(8,128)(2,1)}, bf16[128,256]{1,0:T(8,128)(2,1)S(1)}, u32[]{:S(2)}, u32[]{:S(2)}) collective-permute-start(bf16[128,256]{1,0:T(8,128)(2,1)} %param.12), channel_id=1, source_target_pairs={{0,6},{1,25},{2,0},{3,27},{4,2},{5,29},{6,4},{7,31},{8,14},{9,1},{... | collective-permute-start | bytes 196616 | tf_op jit(solution)/shard_map/ppermute | solution.py:373
  4.9 4.5 %collective-permute-start.2 = (bf16[128,256]{1,0:T(8,128)(2,1)}, bf16[128,256]{1,0:T(8,128)(2,1)S(1)}, u32[]{:S(2)}, u32[]{:S(2)}) collective-permute-start(bf16[128,256]{1,0:T(8,128)(2,1)} %param.12), channel_id=1, source_target_pairs={{0,2},{1,9},{2,4},{3,11},{4,6},{5,13},{6,0},{7,15},{8,10},{9,17},{... | collective-permute-start | bytes 196616 | tf_op jit(solution)/shard_map/ppermute | solution.py:373
  10.3 11.2 %collective-permute-start.5 = (bf16[512,256]{1,0:T(8,128)(2,1)S(1)}, bf16[512,256]{1,0:T(8,128)(2,1)S(1)}, u32[]{:S(2)}, u32[]{:S(2)}) collective-permute-start(bf16[512,256]{1,0:T(8,128)(2,1)S(1)} %pad_maximum_fusion.1), channel_id=1, source_target_pairs={{0,8},{1,33},{2,10},{3,35},{4,12},{5,37},{6,14},{7,39},{8,16},{9,4... | collective-permute-start | bytes 786440 | tf_op jit(solution)/shard_map/ppermute | solution.py:373
  11.5 9.9 %collective-permute-start.4 = (bf16[512,256]{1,0:T(8,128)(2,1)S(1)}, bf16[512,256]{1,0:T(8,128)(2,1)S(1)}, u32[]{:S(2)}, u32[]{:S(2)}) collective-permute-start(bf16[512,256]{1,0:T(8,128)(2,1)S(1)} %pad_maximum_fusion.1), channel_id=1, source_target_pairs={{0,16},{1,65},{2,18},{3,67},{4,20},{5,69},{6,22},{7,71},{8,24},{9,... | collective-permute-start | bytes 786440 | tf_op jit(solution)/shard_map/ppermute | solution.py:373
  14.0 7.5 %collective-permute-start.3 = (bf16[512,256]{1,0:T(8,128)(2,1)S(1)}, bf16[512,256]{1,0:T(8,128)(2,1)S(1)}, u32[]{:S(2)}, u32[]{:S(2)}) collective-permute-start(bf16[512,256]{1,0:T(8,128)(2,1)S(1)} %pad_maximum_fusion.1), channel_id=1, source_target_pairs={{0,24},{1,97},{2,26},{3,99},{4,28},{5,101},{6,30},{7,103},{8,0},{9... | collective-permute-start | bytes 786440 | tf_op jit(solution)/shard_map/ppermute | solution.py:373
  15.1 1.2 %copy-start = (bf16[2048,256]{1,0:T(8,128)(2,1)S(1)}, bf16[2048,256]{1,0:T(8,128)(2,1)}, u32[]{:S(2)}) copy-start(bf16[2048,256]{1,0:T(8,128)(2,1)} %refs_4_.1) | copy-start | bytes 3145732
  21.4 5.8 %copy-start.1 = (bf16[2048,256]{1,0:T(8,128)(2,1)S(1)}, bf16[2048,256]{1,0:T(8,128)(2,1)}, u32[]{:S(2)}) copy-start(bf16[2048,256]{1,0:T(8,128)(2,1)} %refs_4_.1) | copy-start | bytes 3145732
  21.5 35.3 %collective-permute-start.8 = (bf16[2048,256]{1,0:T(8,128)(2,1)S(1)}, bf16[2048,256]{1,0:T(8,128)(2,1)}, u32[]{:S(2)}, u32[]{:S(2)}) collective-permute-start(bf16[2048,256]{1,0:T(8,128)(2,1)S(1)} %pad_maximum_fusion.refs_2_), channel_id=1, source_target_pairs={{0,64},{1,5},{2,66},{3,7},{4,68},{5,1},{6,70},{7,3},{8,72},{9,13},... | collective-permute-start | bytes 3145736 | tf_op jit(solution)/shard_map/ppermute | solution.py:373
  24.5 32.3 %collective-permute-start.7 = (bf16[2048,256]{1,0:T(8,128)(2,1)S(1)}, bf16[2048,256]{1,0:T(8,128)(2,1)}, u32[]{:S(2)}, u32[]{:S(2)}) collective-permute-start(bf16[2048,256]{1,0:T(8,128)(2,1)S(1)} %pad_maximum_fusion.refs_2_), channel_id=1, source_target_pairs={{0,32},{1,3},{2,34},{3,5},{4,36},{5,7},{6,38},{7,1},{8,40},{9,11},... | collective-permute-start | bytes 3145736 | tf_op jit(solution)/shard_map/ppermute | solution.py:373
  24.9 32.1 %collective-permute-start.6 = (bf16[2048,256]{1,0:T(8,128)(2,1)S(1)}, bf16[2048,256]{1,0:T(8,128)(2,1)}, u32[]{:S(2)}, u32[]{:S(2)}) collective-permute-start(bf16[2048,256]{1,0:T(8,128)(2,1)S(1)} %pad_maximum_fusion.refs_2_), channel_id=1, source_target_pairs={{0,96},{1,7},{2,98},{3,1},{4,100},{5,3},{6,102},{7,5},{8,104},{9,1... | collective-permute-start | bytes 3145736 | tf_op jit(solution)/shard_map/ppermute | solution.py:373
  34.3 9.1 %copy-start.2 = (s32[2048,16]{0,1:T(8,128)S(1)}, s32[2048,16]{0,1:T(8,128)}, u32[]{:S(2)}) copy-start(s32[2048,16]{0,1:T(8,128)} %param.15) | copy-start | bytes 393220
  34.3 9.1 %copy-start.3 = (s32[2048]{0:T(1024)S(1)}, s32[2048]{0:T(1024)}, u32[]{:S(2)}) copy-start(s32[2048]{0:T(1024)} %param.16) | copy-start | bytes 24580
  34.4 64.3 %all-to-all-start = ((bf16[128,64,256]{2,1,0:T(8,128)(2,1)}), bf16[128,64,256]{2,1,0:T(8,128)(2,1)}, u32[]{:S(2)}, u32[]{:S(2)}) async-start(bf16[128,64,256]{2,1,0:T(8,128)(2,1)} %bitcast.23), calls=%async_computation | async-start | bytes 8388608 | tf_op jit(solution)/shard_map/all_to_all | solution.py:395
  58.3 14.9 %collective-permute-start.9 = (bf16[2048,256]{1,0:T(8,128)(2,1)S(1)}, bf16[2048,256]{1,0:T(8,128)(2,1)S(1)}, u32[]{:S(2)}, u32[]{:S(2)}) collective-permute-start(bf16[2048,256]{1,0:T(8,128)(2,1)S(1)} %pad_maximum_fusion.refs_2_), channel_id=1, source_target_pairs={{0,1},{1,0},{2,3},{3,2},{4,5},{5,4},{6,7},{7,6},{8,9},{9,8},{10,11... | collective-permute-start | bytes 3145736 | tf_op jit(solution)/shard_map/ppermute | solution.py:347
  69.5 4.0 %collective-permute-start.10 = (bf16[2048,256]{1,0:T(8,128)(2,1)}, bf16[2048,256]{1,0:T(8,128)(2,1)S(1)}, u32[]{:S(2)}, u32[]{:S(2)}) collective-permute-start(bf16[2048,256]{1,0:T(8,128)(2,1)} %collective-permute-done.6.refs_3_), channel_id=1, source_target_pairs={{0,1},{1,0},{2,3},{3,2},{4,5},{5,4},{6,7},{7,6},{8,9},{9,8},{10,11... | collective-permute-start | bytes 3145736 | tf_op jit(solution)/shard_map/ppermute | solution.py:347
  69.5 5.5 %collective-permute-start.11 = (bf16[2048,256]{1,0:T(8,128)(2,1)}, bf16[2048,256]{1,0:T(8,128)(2,1)S(1)}, u32[]{:S(2)}, u32[]{:S(2)}) collective-permute-start(bf16[2048,256]{1,0:T(8,128)(2,1)} %collective-permute-done.7.refs_4_), channel_id=1, source_target_pairs={{0,1},{1,0},{2,3},{3,2},{4,5},{5,4},{6,7},{7,6},{8,9},{9,8},{10,11... | collective-permute-start | bytes 3145736 | tf_op jit(solution)/shard_map/ppermute | solution.py:347
  70.0 6.5 %collective-permute-start.12 = (bf16[2048,256]{1,0:T(8,128)(2,1)}, bf16[2048,256]{1,0:T(8,128)(2,1)S(1)}, u32[]{:S(2)}, u32[]{:S(2)}) collective-permute-start(bf16[2048,256]{1,0:T(8,128)(2,1)} %collective-permute-done.8.refs_5_), channel_id=1, source_target_pairs={{0,1},{1,0},{2,3},{3,2},{4,5},{5,4},{6,7},{7,6},{8,9},{9,8},{10,11... | collective-permute-start | bytes 3145736 | tf_op jit(solution)/shard_map/ppermute | solution.py:347

commit v6 on v5

--- a/solution.py
+++ b/solution.py
@@ -9,7 +9,7 @@
 MIB = 2**20
 CHUNK = 1024
 WIDEN = 256
-UNROLL = 32
+UNROLL = 64
 SEND_PEERS = 16
 SEND_TURNS = ((0, 3), (3, 5))
 
@@ -266,7 +266,7 @@
 
 def layer_body(slots, pieces, index_hbm, *refs):
     sources, refs = refs[:pieces], refs[pieces:]
-    outside, (bias_ref, out_hbm), refs = refs[:4], refs[4:6], refs[6:]
+    outside, out_hbm, refs = refs[:4], refs[4], refs[5:]
     index, inside, (out_ref, stage, table, last, sem, extra, out_sem) = refs[0], refs[1:5], refs[5:]
     copies = start_table(sources, stage, sem)
     (ready,) = fetch([(index_hbm, index)], extra)
@@ -276,8 +276,8 @@
     add_rows(index, table, last, slots, UNROLL)
     for copy in later:
         copy.wait()
-    partial, degree, feats, weight = inside
-    rows, width = feats.shape
+    partial, degree, base, weight = inside
+    rows = base.shape[0]
 
     writes = []
     for i in range(rows // WIDEN):
@@ -288,33 +288,30 @@
             ((mine + theirs) / divisor).astype(jnp.bfloat16)
             for mine, theirs in zip(halves(partial, start, WIDEN), halves(last, start, WIDEN))
         ]
-        result = jnp.dot(feats[span, :], weight[:width, :], preferred_element_type=jnp.float32)
-        result += jnp.dot(
-            jnp.concatenate(means, axis=1), weight[width:, :], preferred_element_type=jnp.float32
+        result = base[span, :] + jnp.dot(
+            jnp.concatenate(means, axis=1), weight[...], preferred_element_type=jnp.float32
         )
-        result += bias_ref[...]
         out_ref[span, :] = jnp.maximum(result, 0.0).astype(out_ref.dtype)
         writes += fetch([(out_ref.at[span], out_hbm.at[span])], out_sem, i)
     for write in writes:
         write.wait()
 
 
-def layer(index, slots, sources, partial, degree, feats, weight, bias):
+def layer(index, slots, sources, partial, degree, base, weight):
     width = sources[0].shape[1]
     count = sum(source.shape[0] for source in sources)
-    rows = feats.shape[0]
-    outside = [partial, degree, feats, weight]
-    vmem = pl.BlockSpec(memory_space=pltpu.VMEM)
+    rows = base.shape[0]
+    outside = [partial, degree, base, weight]
     return pl.pallas_call(
         lambda *refs: layer_body(slots, len(sources), *refs),
-        in_specs=[pl.BlockSpec(memory_space=pltpu.HBM)] * (1 + len(sources) + len(outside)) + [vmem],
+        in_specs=[pl.BlockSpec(memory_space=pltpu.HBM)] * (1 + len(sources) + len(outside)),
         out_specs=pl.BlockSpec(memory_space=pltpu.HBM),
-        out_shape=pltpu.HBM((rows, width), feats.dtype),
+        out_shape=pltpu.HBM((rows, width), sources[0].dtype),
         scratch_shapes=[pltpu.SMEM(index.shape, index.dtype)]
         + [pltpu.VMEM(array.shape, array.dtype) for array in outside]
         + [
-            pltpu.VMEM((rows, width), feats.dtype),
-            pltpu.VMEM((count, width), feats.dtype),
+            pltpu.VMEM((rows, width), sources[0].dtype),
+            pltpu.VMEM((count, width), sources[0].dtype),
             pltpu.VMEM((2 * count + 8, LANES), jnp.float32),
             pltpu.VMEM((2 * rows, LANES), jnp.float32),
             pltpu.SemaphoreType.DMA((chunk_count(sources),)),
@@ -326,7 +323,7 @@
             flops=27_000_000_000, bytes_accessed=2 * count * width, transcendentals=0
         ),
         name="layer",
-    )(index, *sources, *outside, bias)
+    )(index, *sources, *outside)
 
 
 RING = 4
@@ -401,13 +398,14 @@
     degree = jnp.broadcast_to(
         (loc_len + hub_len + halo_len).astype(jnp.float32)[:, None], (rows, LANES)
     )
-    hubs, loc, hub_index, halo_index, degree = lax.optimization_barrier(
-        (hubs, loc, hub_index, halo_index, degree)
+    base = jnp.dot(feats, weight[:width], preferred_element_type=jnp.float32) + bias
+    hubs, loc, hub_index, halo_index, degree, base = lax.optimization_barrier(
+        (hubs, loc, hub_index, halo_index, degree, base)
     )
     hubs = hubs + [swapped(part) for part in hubs]
     partial = list_sums(hub_index, hub_nbr.shape[1], hubs, loc)
     return layer(
-        halo_index, halo_nbr.shape[1], [arrived], partial, degree, feats, weight, bias[None, :]
+        halo_index, halo_nbr.shape[1], [arrived], partial, degree, base, weight[width:]
     )
 
 

time: 118 us -> 119 us (level)
  starting transfers between devices: 37.2 us -> 29.5 us
  waiting for transfers between devices: 10.6 us -> 18.2 us
  matrix products: 0 us -> 3.13 us
  Pallas kernels: 61.5 us -> 59.4 us
  local copies, waits for them, and re-layouts: 3.31 us -> 4.99 us
  other arithmetic: 4.34 us -> 2.72 us
    all_to_all x1, waiting for transfers between devices: 3.66 us -> 11.5 us  [per_device(): lax.all_to_all(outgoing.reshape(peers, slots, width), 'dom', split_axis=0...]
    ppermute x4, starting transfers between devices: 11.6 us -> 4.79 us  [swapped(): lax.ppermute(block, 'dom', [(device, device ^ 1) for device in range(2 *...]
    dot_general x0 -> x1, matrix products: none -> 3.13 us  [per_device(): jnp.dot(feats, weight[:width], preferred_element_type=jnp.float32) + bias]
    pallas_call x1, Pallas kernels: 18.4 us -> 17.1 us  [layer(): pl.pallas_call(lambda *refs: layer_body(slots, len(sources), *refs), in_s...]
    unnamed x8 -> x18, local copies, waits for them, and re-layouts: 1.24 us -> 0.04 us
  transfers between devices with their start and end apart: 14 -> 14, of which waited for: 7 -> 7; matrix products, arithmetic and copies ran while one was open for 5% -> 9% of each run, Pallas kernels for 37% -> 36%
where the time goes in v6:
time: 119 us; the launch traced here: 118 us
  Pallas kernels  59.4 us (50%)
  starting transfers between devices  29.5 us (25%)
  waiting for transfers between devices  18.2 us (15%)
  local copies, waits for them, and re-layouts  4.99 us (4%)
  matrix products  3.13 us (3%)
  other arithmetic  2.72 us (2%)
    pallas_call x1, Pallas kernels, list_sums(): pl.pallas_call(lambda *refs: list_body(slots, len(sources), *refs), in_sp...  17.8 us
    pallas_call x1, Pallas kernels, layer(): pl.pallas_call(lambda *refs: layer_body(slots, len(sources), *refs), in_s...  17.1 us
    ppermute x9, starting transfers between devices, along(): lax.ppermute(block, 'dom', moved(stage, lambda i, shift=shift: (i - shift...  15.6 us
    pallas_call x1, Pallas kernels, local_sums(): pl.pallas_call(lambda *refs: local_body(part, *refs), grid=(rows // (grou...  12.4 us
    pallas_call x2, Pallas kernels, gather_to_send(): pl.pallas_call(lambda index_hbm, feats_ref, *refs: send_body(SEND_PEERS *...  12.1 us
    all_to_all x1, waiting for transfers between devices, per_device(): lax.all_to_all(outgoing.reshape(peers, slots, width), 'dom', split_axis=0...  11.5 us
    all_to_all x1, starting transfers between devices, per_device(): lax.all_to_all(outgoing.reshape(peers, slots, width), 'dom', split_axis=0...  9.12 us
    ppermute x4, waiting for transfers between devices, swapped(): lax.ppermute(block, 'dom', [(device, device ^ 1) for device in range(2 *...  5.83 us
  transfers between devices with their start and end apart: 14, of which 7 were waited for; matrix products, arithmetic and copies ran while one was open for 9% of the time, Pallas kernels for 36%

profile of v6, /device:TPU:1, one launch (start us, length us, event | category | flops | bytes accessed | tf_op | source)
XLA Modules:
  0.0 118.2 jit_solution(5359215790914710086)
XLA Ops:
  0.0 0.0 copy-start.3
  0.0 0.0 copy-start.4
  0.0 2.5 %collective-permute-start.2 = (bf16[128,256]{1,0:T(8,128)(2,1)}, bf16[128,256]{1,0:T(8,128)(2,1)S(1)}, u32[]{:S(2)}, u32[]{:S(2)}) collective-permute-start(bf16[128,256]{1,0:T(8,128)(2,1)} %param.12), channel_id=1, source_target_pairs={{0,2},{1,9},{2,4},{3,11},{4,6},{5,13},{6,0},{7,15},{8,10},{9,17},{... | collective-permute-start | bytes 196616 | tf_op jit(solution)/shard_map/ppermute | solution.py:370
  2.6 3.3 %collective-permute-start.1 = (bf16[128,256]{1,0:T(8,128)(2,1)}, bf16[128,256]{1,0:T(8,128)(2,1)S(1)}, u32[]{:S(2)}, u32[]{:S(2)}) collective-permute-start(bf16[128,256]{1,0:T(8,128)(2,1)} %param.12), channel_id=1, source_target_pairs={{0,4},{1,17},{2,6},{3,19},{4,0},{5,21},{6,2},{7,23},{8,12},{9,25},... | collective-permute-start | bytes 196616 | tf_op jit(solution)/shard_map/ppermute | solution.py:370
  5.9 0.7 collective-permute-start
  6.6 0.8 multiply_bitcast_fusion.index_hbm
  7.5 0.7 add_convert_fusion
  8.2 3.1 %convolution_add_fusion.refs_4_ = f32[2048,256]{1,0:T(8,128)} fusion(bf16[2048,256]{1,0:T(8,128)(2,1)} %refs_1_.1, f32[256]{0:T(256)} %param.14, bf16[512,256]{1,0:T(8,128)(2,1)} %param.13), kind=kOutput, calls=%fused_computation | convolution fusion | flops 268959744 | bytes 3277824 | tf_op jit(solution)/shard_map/dot_general | solution.py:401
  11.3 0.0 copy-done.6
  11.3 0.9 fusion.24
  12.2 0.0 collective-permute-done.2
  12.2 0.0 collective-permute-done.1
  12.3 0.0 collective-permute-done
  12.3 1.3 %collective-permute-start.5 = (bf16[512,256]{1,0:T(8,128)(2,1)S(1)}, bf16[512,256]{1,0:T(8,128)(2,1)S(1)}, u32[]{:S(2)}, u32[]{:S(2)}) collective-permute-start(bf16[512,256]{1,0:T(8,128)(2,1)S(1)} %pad_maximum_fusion.1), channel_id=1, source_target_pairs={{0,8},{1,33},{2,10},{3,35},{4,12},{5,37},{6,14},{7,39},{8,16},{9,4... | collective-permute-start | bytes 786440 | tf_op jit(solution)/shard_map/ppermute | solution.py:370
  13.6 2.5 %collective-permute-start.4 = (bf16[512,256]{1,0:T(8,128)(2,1)S(1)}, bf16[512,256]{1,0:T(8,128)(2,1)S(1)}, u32[]{:S(2)}, u32[]{:S(2)}) collective-permute-start(bf16[512,256]{1,0:T(8,128)(2,1)S(1)} %pad_maximum_fusion.1), channel_id=1, source_target_pairs={{0,16},{1,65},{2,18},{3,67},{4,20},{5,69},{6,22},{7,71},{8,24},{9,... | collective-permute-start | bytes 786440 | tf_op jit(solution)/shard_map/ppermute | solution.py:370
  16.0 1.2 collective-permute-start.3
  17.2 5.0 %gather_to_send.2.refs_0_ = bf16[8192,256]{1,0:T(8,128)(2,1)} custom-call(s32[8192]{0:T(1024)S(1)} %multiply_bitcast_fusion.index_hbm, bf16[2048,256]{1,0:T(8,128)(2,1)S(1)} %copy-done), custom_call_target="tpu_custom_call" | custom-call | flops 6442450944 | bytes 1572864 | tf_op jit(solution)/shard_map/gather_to_send/pallas_call | solution.py:85
  22.2 0.0 collective-permute-done.5
  22.2 0.7 collective-permute-done.4
  22.9 0.0 collective-permute-done.3
  22.9 0.1 pad_maximum_fusion.refs_2_
  23.0 2.5 %collective-permute-start.6 = (bf16[2048,256]{1,0:T(8,128)(2,1)S(1)}, bf16[2048,256]{1,0:T(8,128)(2,1)S(1)}, u32[]{:S(2)}, u32[]{:S(2)}) collective-permute-start(bf16[2048,256]{1,0:T(8,128)(2,1)S(1)} %pad_maximum_fusion.refs_2_), channel_id=1, source_target_pairs={{0,96},{1,7},{2,98},{3,1},{4,100},{5,3},{6,102},{7,5},{8,104},{9,1... | collective-permute-start | bytes 3145736 | tf_op jit(solution)/shard_map/ppermute | solution.py:370
  25.5 0.0 collective-permute-start.7
  25.5 1.6 %collective-permute-start.8 = (bf16[2048,256]{1,0:T(8,128)(2,1)S(1)}, bf16[2048,256]{1,0:T(8,128)(2,1)}, u32[]{:S(2)}, u32[]{:S(2)}) collective-permute-start(bf16[2048,256]{1,0:T(8,128)(2,1)S(1)} %pad_maximum_fusion.refs_2_), channel_id=1, source_target_pairs={{0,64},{1,5},{2,66},{3,7},{4,68},{5,1},{6,70},{7,3},{8,72},{9,13},... | collective-permute-start | bytes 3145736 | tf_op jit(solution)/shard_map/ppermute | solution.py:370
  27.1 7.1 %gather_to_send.3 = bf16[8192,256]{1,0:T(8,128)(2,1)} custom-call(s32[8192]{0:T(1024)S(1)} %multiply_bitcast_fusion.index_hbm, bf16[2048,256]{1,0:T(8,128)(2,1)S(1)} %copy-done, bf16[8192,256]{1,0:T(8,128)(2,1)} %gather_to_send.2.refs_0_), custom_call_target="tpu_custom_call", output_to_operand_aliasing={{}: (2, {})} | custom-call | flops 10737418240 | bytes 2621440 | tf_op jit(solution)/shard_map/gather_to_send/pallas_call | solution.py:85
  34.3 0.0 copy-start.2
  34.3 0.0 copy-start.8
  34.3 9.1 %all-to-all-start = ((bf16[128,64,256]{2,1,0:T(8,128)(2,1)}), bf16[128,64,256]{2,1,0:T(8,128)(2,1)}, u32[]{:S(2)}, u32[]{:S(2)}) async-start(bf16[128,64,256]{2,1,0:T(8,128)(2,1)} %bitcast.23), calls=%async_computation | async-start | bytes 8388608 | tf_op jit(solution)/shard_map/all_to_all | solution.py:392
  43.4 0.1 fusion.4
  43.6 1.3 %copy.14 = s32[2048,16]{1,0:T(8,128)} copy(s32[2048,16]{0,1:T(8,128)S(1)} %fusion.4) | data formatting | bytes 262144 | tf_op jit(solution)/shard_map/jit(_where)/select_n | solution.py:138
  44.9 1.6 %reshape.38.refs_0_ = s32[128,256]{1,0:T(8,128)S(1)} reshape(s32[2048,16]{1,0:T(8,128)} %copy.14) | data formatting | bytes 262144 | tf_op jit(solution)/shard_map/reshape | solution.py:138
  46.5 12.4 %local_sums.1.refs_1_ = f32[2048,256]{1,0:T(8,128)S(1)} custom-call(s32[128,256]{1,0:T(8,128)S(1)} %reshape.38.refs_0_, bf16[2048,256]{1,0:T(8,128)(2,1)S(1)} %copy-done), custom_call_target="tpu_custom_call" | custom-call | flops 4294967296 | bytes 2097152 | tf_op jit(solution)/shard_map/local_sums/pallas_call | solution.py:140
  58.9 0.0 collective-permute-done.6.refs_3_
  59.0 0.2 collective-permute-done.7.refs_4_
  59.2 0.0 collective-permute-done.8.refs_5_
  59.2 1.4 %broadcast_in_dim.13.refs_3_ = f32[2048,128]{1,0:T(8,128)} broadcast(f32[2048]{0:T(1024)S(1)} %add_convert_fusion), dimensions={0} | broadcast | bytes 1056768 | tf_op jit(solution)/shard_map/broadcast_in_dim | solution.py:398
  60.5 4.3 %collective-permute-start.9 = (bf16[2048,256]{1,0:T(8,128)(2,1)S(1)}, bf16[2048,256]{1,0:T(8,128)(2,1)S(1)}, u32[]{:S(2)}, u32[]{:S(2)}) collective-permute-start(bf16[2048,256]{1,0:T(8,128)(2,1)S(1)} %pad_maximum_fusion.refs_2_), channel_id=1, source_target_pairs={{0,1},{1,0},{2,3},{3,2},{4,5},{5,4},{6,7},{7,6},{8,9},{9,8},{10,11... | collective-permute-start | bytes 3145736 | tf_op jit(solution)/shard_map/ppermute | solution.py:344
  64.8 0.0 collective-permute-start.10
  64.8 0.5 collective-permute-start.11
  65.3 0.0 collective-permute-start.12
  65.3 0.7 slice.7.refs_5_
  66.0 1.1 collective-permute-done.9.refs_6_
  67.1 3.0 %collective-permute-done.10.refs_7_ = bf16[2048,256]{1,0:T(8,128)(2,1)S(1)} collective-permute-done((bf16[2048,256]{1,0:T(8,128)(2,1)S(1)}, bf16[2048,256]{1,0:T(8,128)(2,1)S(1)}, u32[]{:S(2)}, u32[]{:S(2)}) %collective-permute-start.10) | collective-permute-done | bytes 1048608 | tf_op jit(solution)/shard_map/ppermute | solution.py:344
  70.1 0.2 collective-permute-done.11.refs_8_
  70.3 1.5 %collective-permute-done.12.refs_9_ = bf16[2048,256]{1,0:T(8,128)(2,1)S(1)} collective-permute-done((bf16[2048,256]{1,0:T(8,128)(2,1)}, bf16[2048,256]{1,0:T(8,128)(2,1)S(1)}, u32[]{:S(2)}, u32[]{:S(2)}) %collective-permute-start.12) | collective-permute-done | bytes 1048608 | tf_op jit(solution)/shard_map/ppermute | solution.py:344
  71.8 17.8 %list_sums.1.refs_2_ = f32[4096,128]{1,0:T(8,128)} custom-call(s32[16384]{0:T(1024)S(1)} %get-tuple-element.27.refs_0_, f32[2048,256]{1,0:T(8,128)S(1)} %local_sums.1.refs_1_, bf16[2048,256]{1,0:T(8,128)(2,1)S(1)} %pad_maximum_fusion.refs_2_, bf16[2048,256]{1,0:T(8,128)(2,1)S(1)} %collective-permute-done.6.refs_3_, ...), custom_call_target="tpu_custom_call" | custom-call | flops 27000000512 | bytes 8388608 | tf_op jit(solution)/shard_map/list_sums/pallas_call | solution.py:246
  89.7 11.5 %all-to-all-done = bf16[128,64,256]{2,1,0:T(8,128)(2,1)} async-done(((bf16[128,64,256]{2,1,0:T(8,128)(2,1)}), bf16[128,64,256]{2,1,0:T(8,128)(2,1)}, u32[]{:S(2)}, u32[]{:S(2)}) %all-to-all-start) | async-done | bytes 4194336 | tf_op jit(solution)/shard_map/all_to_all | solution.py:392
  101.2 17.1 %layer.1 = bf16[2048,256]{1,0:T(8,128)(2,1)} custom-call(s32[16384]{0:T(1024)} %get-tuple-element.25.refs_0_, bf16[8192,256]{1,0:T(8,128)(2,1)} %bitcast.11.refs_1_, f32[4096,128]{1,0:T(8,128)} %list_sums.1.refs_2_, f32[2048,128]{1,0:T(8,128)} %broadcast_in_dim.13.refs_3_, f32[2048,256]{1,0:T(8,128)} %convolution_add_fusion.refs_4_, ...), custom_call_target="tpu_custom_call" | custom-call | flops 27000000512 | bytes 4194304 | tf_op jit(solution)/shard_map/layer/pallas_call | solution.py:305
  (15 shorter events, 0.0 us)
Async XLA Ops:
  0.0 12.3 %copy-start.5 = (bf16[128,256]{1,0:T(8,128)(2,1)S(1)}, bf16[128,256]{1,0:T(8,128)(2,1)}, u32[]{:S(2)}) copy-start(bf16[128,256]{1,0:T(8,128)(2,1)} %param.12) | copy-start | bytes 196612
  0.0 11.3 %copy-start.6 = (s32[2048]{0:T(1024)S(1)}, s32[2048]{0:T(1024)}, u32[]{:S(2)}) copy-start(s32[2048]{0:T(1024)} %param.18) | copy-start | bytes 24580
  0.0 11.3 %copy-start.7 = (s32[2048]{0:T(1024)S(1)}, s32[2048]{0:T(1024)}, u32[]{:S(2)}) copy-start(s32[2048]{0:T(1024)} %param.21) | copy-start | bytes 24580
  0.0 11.3 %copy-start.3 = (s32[2048,8]{0,1:T(8,128)S(1)}, s32[2048,8]{0,1:T(8,128)}, u32[]{:S(2)}) copy-start(s32[2048,8]{0,1:T(8,128)} %param.17) | copy-start | bytes 196612
  0.0 11.3 %copy-start.4 = (s32[2048,8]{0,1:T(8,128)S(1)}, s32[2048,8]{0,1:T(8,128)}, u32[]{:S(2)}) copy-start(s32[2048,8]{0,1:T(8,128)} %param.20) | copy-start | bytes 196612
  0.0 12.2 %collective-permute-start.2 = (bf16[128,256]{1,0:T(8,128)(2,1)}, bf16[128,256]{1,0:T(8,128)(2,1)S(1)}, u32[]{:S(2)}, u32[]{:S(2)}) collective-permute-start(bf16[128,256]{1,0:T(8,128)(2,1)} %param.12), channel_id=1, source_target_pairs={{0,2},{1,9},{2,4},{3,11},{4,6},{5,13},{6,0},{7,15},{8,10},{9,17},{... | collective-permute-start | bytes 196616 | tf_op jit(solution)/shard_map/ppermute | solution.py:370
  2.6 9.7 %collective-permute-start.1 = (bf16[128,256]{1,0:T(8,128)(2,1)}, bf16[128,256]{1,0:T(8,128)(2,1)S(1)}, u32[]{:S(2)}, u32[]{:S(2)}) collective-permute-start(bf16[128,256]{1,0:T(8,128)(2,1)} %param.12), channel_id=1, source_target_pairs={{0,4},{1,17},{2,6},{3,19},{4,0},{5,21},{6,2},{7,23},{8,12},{9,25},... | collective-permute-start | bytes 196616 | tf_op jit(solution)/shard_map/ppermute | solution.py:370
  5.9 6.4 %collective-permute-start = (bf16[128,256]{1,0:T(8,128)(2,1)}, bf16[128,256]{1,0:T(8,128)(2,1)S(1)}, u32[]{:S(2)}, u32[]{:S(2)}) collective-permute-start(bf16[128,256]{1,0:T(8,128)(2,1)} %param.12), channel_id=1, source_target_pairs={{0,6},{1,25},{2,0},{3,27},{4,2},{5,29},{6,4},{7,31},{8,14},{9,1},{... | collective-permute-start | bytes 196616 | tf_op jit(solution)/shard_map/ppermute | solution.py:370
  6.6 10.6 %copy-start = (bf16[2048,256]{1,0:T(8,128)(2,1)S(1)}, bf16[2048,256]{1,0:T(8,128)(2,1)}, u32[]{:S(2)}) copy-start(bf16[2048,256]{1,0:T(8,128)(2,1)} %refs_1_.1) | copy-start | bytes 3145732
  12.3 9.9 %collective-permute-start.5 = (bf16[512,256]{1,0:T(8,128)(2,1)S(1)}, bf16[512,256]{1,0:T(8,128)(2,1)S(1)}, u32[]{:S(2)}, u32[]{:S(2)}) collective-permute-start(bf16[512,256]{1,0:T(8,128)(2,1)S(1)} %pad_maximum_fusion.1), channel_id=1, source_target_pairs={{0,8},{1,33},{2,10},{3,35},{4,12},{5,37},{6,14},{7,39},{8,16},{9,4... | collective-permute-start | bytes 786440 | tf_op jit(solution)/shard_map/ppermute | solution.py:370
  13.6 9.3 %collective-permute-start.4 = (bf16[512,256]{1,0:T(8,128)(2,1)S(1)}, bf16[512,256]{1,0:T(8,128)(2,1)S(1)}, u32[]{:S(2)}, u32[]{:S(2)}) collective-permute-start(bf16[512,256]{1,0:T(8,128)(2,1)S(1)} %pad_maximum_fusion.1), channel_id=1, source_target_pairs={{0,16},{1,65},{2,18},{3,67},{4,20},{5,69},{6,22},{7,71},{8,24},{9,... | collective-permute-start | bytes 786440 | tf_op jit(solution)/shard_map/ppermute | solution.py:370
  16.0 6.9 %collective-permute-start.3 = (bf16[512,256]{1,0:T(8,128)(2,1)S(1)}, bf16[512,256]{1,0:T(8,128)(2,1)S(1)}, u32[]{:S(2)}, u32[]{:S(2)}) collective-permute-start(bf16[512,256]{1,0:T(8,128)(2,1)S(1)} %pad_maximum_fusion.1), channel_id=1, source_target_pairs={{0,24},{1,97},{2,26},{3,99},{4,28},{5,101},{6,30},{7,103},{8,0},{9... | collective-permute-start | bytes 786440 | tf_op jit(solution)/shard_map/ppermute | solution.py:370
  23.0 36.0 %collective-permute-start.6 = (bf16[2048,256]{1,0:T(8,128)(2,1)S(1)}, bf16[2048,256]{1,0:T(8,128)(2,1)S(1)}, u32[]{:S(2)}, u32[]{:S(2)}) collective-permute-start(bf16[2048,256]{1,0:T(8,128)(2,1)S(1)} %pad_maximum_fusion.refs_2_), channel_id=1, source_target_pairs={{0,96},{1,7},{2,98},{3,1},{4,100},{5,3},{6,102},{7,5},{8,104},{9,1... | collective-permute-start | bytes 3145736 | tf_op jit(solution)/shard_map/ppermute | solution.py:370
  25.5 33.7 %collective-permute-start.7 = (bf16[2048,256]{1,0:T(8,128)(2,1)S(1)}, bf16[2048,256]{1,0:T(8,128)(2,1)}, u32[]{:S(2)}, u32[]{:S(2)}) collective-permute-start(bf16[2048,256]{1,0:T(8,128)(2,1)S(1)} %pad_maximum_fusion.refs_2_), channel_id=1, source_target_pairs={{0,32},{1,3},{2,34},{3,5},{4,36},{5,7},{6,38},{7,1},{8,40},{9,11},... | collective-permute-start | bytes 3145736 | tf_op jit(solution)/shard_map/ppermute | solution.py:370
  25.5 33.7 %collective-permute-start.8 = (bf16[2048,256]{1,0:T(8,128)(2,1)S(1)}, bf16[2048,256]{1,0:T(8,128)(2,1)}, u32[]{:S(2)}, u32[]{:S(2)}) collective-permute-start(bf16[2048,256]{1,0:T(8,128)(2,1)S(1)} %pad_maximum_fusion.refs_2_), channel_id=1, source_target_pairs={{0,64},{1,5},{2,66},{3,7},{4,68},{5,1},{6,70},{7,3},{8,72},{9,13},... | collective-permute-start | bytes 3145736 | tf_op jit(solution)/shard_map/ppermute | solution.py:370
  34.3 9.2 %copy-start.2 = (s32[2048,16]{0,1:T(8,128)S(1)}, s32[2048,16]{0,1:T(8,128)}, u32[]{:S(2)}) copy-start(s32[2048,16]{0,1:T(8,128)} %param.15) | copy-start | bytes 393220
  34.3 9.2 %copy-start.8 = (s32[2048]{0:T(1024)S(1)}, s32[2048]{0:T(1024)}, u32[]{:S(2)}) copy-start(s32[2048]{0:T(1024)} %param.16) | copy-start | bytes 24580
  34.3 66.9 %all-to-all-start = ((bf16[128,64,256]{2,1,0:T(8,128)(2,1)}), bf16[128,64,256]{2,1,0:T(8,128)(2,1)}, u32[]{:S(2)}, u32[]{:S(2)}) async-start(bf16[128,64,256]{2,1,0:T(8,128)(2,1)} %bitcast.23), calls=%async_computation | async-start | bytes 8388608 | tf_op jit(solution)/shard_map/all_to_all | solution.py:392
  46.5 18.8 %copy-start.1 = (bf16[512,256]{1,0:T(8,128)(2,1)S(1)}, bf16[512,256]{1,0:T(8,128)(2,1)}, u32[]{:S(2)}) copy-start(bf16[512,256]{1,0:T(8,128)(2,1)} %param.13) | copy-start | bytes 786436
  60.5 6.6 %collective-permute-start.9 = (bf16[2048,256]{1,0:T(8,128)(2,1)S(1)}, bf16[2048,256]{1,0:T(8,128)(2,1)S(1)}, u32[]{:S(2)}, u32[]{:S(2)}) collective-permute-start(bf16[2048,256]{1,0:T(8,128)(2,1)S(1)} %pad_maximum_fusion.refs_2_), channel_id=1, source_target_pairs={{0,1},{1,0},{2,3},{3,2},{4,5},{5,4},{6,7},{7,6},{8,9},{9,8},{10,11... | collective-permute-start | bytes 3145736 | tf_op jit(solution)/shard_map/ppermute | solution.py:344
  64.8 5.3 %collective-permute-start.10 = (bf16[2048,256]{1,0:T(8,128)(2,1)S(1)}, bf16[2048,256]{1,0:T(8,128)(2,1)S(1)}, u32[]{:S(2)}, u32[]{:S(2)}) collective-permute-start(bf16[2048,256]{1,0:T(8,128)(2,1)S(1)} %collective-permute-done.6.refs_3_), channel_id=1, source_target_pairs={{0,1},{1,0},{2,3},{3,2},{4,5},{5,4},{6,7},{7,6},{8,9},{9,8},{10,11... | collective-permute-start | bytes 3145736 | tf_op jit(solution)/shard_map/ppermute | solution.py:344
  64.8 5.5 %collective-permute-start.11 = (bf16[2048,256]{1,0:T(8,128)(2,1)}, bf16[2048,256]{1,0:T(8,128)(2,1)S(1)}, u32[]{:S(2)}, u32[]{:S(2)}) collective-permute-start(bf16[2048,256]{1,0:T(8,128)(2,1)} %collective-permute-done.7.refs_4_), channel_id=1, source_target_pairs={{0,1},{1,0},{2,3},{3,2},{4,5},{5,4},{6,7},{7,6},{8,9},{9,8},{10,11... | collective-permute-start | bytes 3145736 | tf_op jit(solution)/shard_map/ppermute | solution.py:344
  65.3 6.5 %collective-permute-start.12 = (bf16[2048,256]{1,0:T(8,128)(2,1)}, bf16[2048,256]{1,0:T(8,128)(2,1)S(1)}, u32[]{:S(2)}, u32[]{:S(2)}) collective-permute-start(bf16[2048,256]{1,0:T(8,128)(2,1)} %collective-permute-done.8.refs_5_), channel_id=1, source_target_pairs={{0,1},{1,0},{2,3},{3,2},{4,5},{5,4},{6,7},{7,6},{8,9},{9,8},{10,11... | collective-permute-start | bytes 3145736 | tf_op jit(solution)/shard_map/ppermute | solution.py:344

commit v7 on v5

--- a/solution.py
+++ b/solution.py
@@ -331,7 +331,7 @@
 
 RING = 4
 STRIDES = {"x": 32, "z": 8, "y": 2}
-ORDERS = (("y", "z", "x"), ("z", "x", "y"))
+ORDERS = (("y", "z", "x"), ("x", "z", "y"))
 
 
 def moved(stage, step):

time: 118 us -> 122 us (1.034)
  waiting for transfers between devices: 10.6 us -> 26.3 us
  starting transfers between devices: 37.2 us -> 26.2 us
    ppermute x9, waiting for transfers between devices: 0.41 us -> 19.3 us  [along(): lax.ppermute(block, 'dom', moved(stage, lambda i, shift=shift: (i - shift...]
    ppermute x4, starting transfers between devices: 11.6 us -> 1.02 us  [swapped(): lax.ppermute(block, 'dom', [(device, device ^ 1) for device in range(2 *...]
    all_to_all x1, waiting for transfers between devices: 3.66 us -> 0.61 us  [per_device(): lax.all_to_all(outgoing.reshape(peers, slots, width), 'dom', split_axis=0...]
    all_to_all x1, starting transfers between devices: 9.1 us -> 6.2 us  [per_device(): lax.all_to_all(outgoing.reshape(peers, slots, width), 'dom', split_axis=0...]
    ppermute x9, starting transfers between devices: 16.4 us -> 19 us  [along(): lax.ppermute(block, 'dom', moved(stage, lambda i, shift=shift: (i - shift...]
  transfers between devices with their start and end apart: 14 -> 14, of which waited for: 7 -> 9; matrix products, arithmetic and copies ran while one was open for 5% -> 5% of each run, Pallas kernels for 37% -> 35%
where the time goes in v7:
time: 122 us
  Pallas kernels  61.5 us (50%)
  waiting for transfers between devices  26.3 us (22%)
  starting transfers between devices  26.2 us (21%)
  other arithmetic  4.34 us (4%)
  local copies, waits for them, and re-layouts  3.31 us (3%)
    ppermute x9, waiting for transfers between devices, along(): lax.ppermute(block, 'dom', moved(stage, lambda i, shift=shift: (i - shift...  19.3 us
    ppermute x9, starting transfers between devices, along(): lax.ppermute(block, 'dom', moved(stage, lambda i, shift=shift: (i - shift...  19 us
    pallas_call x1, Pallas kernels, list_sums(): pl.pallas_call(lambda *refs: list_body(slots, len(sources), *refs), in_sp...  18.6 us
    pallas_call x1, Pallas kernels, layer(): pl.pallas_call(lambda *refs: layer_body(slots, len(sources), *refs), in_s...  18.4 us
    pallas_call x1, Pallas kernels, local_sums(): pl.pallas_call(lambda *refs: local_body(part, *refs), grid=(rows // (grou...  12.4 us
    pallas_call x2, Pallas kernels, gather_to_send(): pl.pallas_call(lambda index_hbm, feats_ref, *refs: send_body(SEND_PEERS *...  12.2 us
    ppermute x4, waiting for transfers between devices, swapped(): lax.ppermute(block, 'dom', [(device, device ^ 1) for device in range(2 *...  6.35 us
    all_to_all x1, starting transfers between devices, per_device(): lax.all_to_all(outgoing.reshape(peers, slots, width), 'dom', split_axis=0...  6.2 us
  transfers between devices with their start and end apart: 14, of which 9 were waited for; matrix products, arithmetic and copies ran while one was open for 5% of the time, Pallas kernels for 35%

profile of v7, /device:TPU:1, one launch (start us, length us, event | category | flops | bytes accessed | tf_op | source)
XLA Modules:
  0.0 121.8 jit_solution(1889227328008338994)
XLA Ops:
  0.0 3.6 %collective-permute-start.1 = (bf16[128,256]{1,0:T(8,128)(2,1)}, bf16[128,256]{1,0:T(8,128)(2,1)S(1)}, u32[]{:S(2)}, u32[]{:S(2)}) collective-permute-start(bf16[128,256]{1,0:T(8,128)(2,1)} %param.12), channel_id=1, source_target_pairs={{0,4},{1,65},{2,6},{3,67},{4,0},{5,69},{6,2},{7,71},{8,12},{9,73},... | collective-permute-start | bytes 196616 | tf_op jit(solution)/shard_map/ppermute | solution.py:373
  3.6 0.9 collective-permute-start
  4.4 0.6 collective-permute-start.2
  5.0 0.8 multiply_bitcast_fusion.index_hbm
  5.8 0.7 add_convert_fusion
  6.5 1.8 %fusion.23 = (s32[16384]{0:T(1024)S(1)}, s32[16384]{0:T(1024)}) fusion(s32[2048,8]{0,1:T(8,128)} %param.17, s32[]{:T(128)S(6)} %and.118, s32[]{:T(128)S(6)} %select_n.108, s32[]{:T(128)S(6)} %select_n.104, s32[]{:T(128)S(6)} %select_n.100, s32[2048]{0:T(1024)} %param.18, s32[2048,8]{0,1:T(8,128)} %param.20, s32[2048]{0:T(1024)} %param.21), kind=kLoop, calls=%fused_computation.58 | loop fusion | flops 1949696 | bytes 278544 | tf_op jit(solution)/shard_map/reshape | solution.py:239
  8.3 0.0 collective-permute-done.1
  8.3 0.0 collective-permute-done
  8.3 0.6 collective-permute-done.2
  9.0 0.9 pad_maximum_fusion.1
  9.8 1.7 %collective-permute-start.5 = (bf16[512,256]{1,0:T(8,128)(2,1)S(1)}, bf16[512,256]{1,0:T(8,128)(2,1)S(1)}, u32[]{:S(2)}, u32[]{:S(2)}) collective-permute-start(bf16[512,256]{1,0:T(8,128)(2,1)S(1)} %pad_maximum_fusion.1), channel_id=1, source_target_pairs={{0,8},{1,9},{2,10},{3,11},{4,12},{5,13},{6,14},{7,15},{8,16},{9,17... | collective-permute-start | bytes 786440 | tf_op jit(solution)/shard_map/ppermute | solution.py:373
  11.5 3.3 %collective-permute-start.4 = (bf16[512,256]{1,0:T(8,128)(2,1)S(1)}, bf16[512,256]{1,0:T(8,128)(2,1)S(1)}, u32[]{:S(2)}, u32[]{:S(2)}) collective-permute-start(bf16[512,256]{1,0:T(8,128)(2,1)S(1)} %pad_maximum_fusion.1), channel_id=1, source_target_pairs={{0,16},{1,17},{2,18},{3,19},{4,20},{5,21},{6,22},{7,23},{8,24},{9,... | collective-permute-start | bytes 786440 | tf_op jit(solution)/shard_map/ppermute | solution.py:373
  14.8 0.7 collective-permute-start.3
  15.6 1.2 %copy-done = bf16[2048,256]{1,0:T(8,128)(2,1)S(1)} copy-done((bf16[2048,256]{1,0:T(8,128)(2,1)S(1)}, bf16[2048,256]{1,0:T(8,128)(2,1)}, u32[]{:S(2)}) %copy-start) | copy-done | bytes 1048600
  16.8 5.0 %gather_to_send.2.refs_0_ = bf16[8192,256]{1,0:T(8,128)(2,1)} custom-call(s32[8192]{0:T(1024)S(1)} %multiply_bitcast_fusion.index_hbm, bf16[2048,256]{1,0:T(8,128)(2,1)S(1)} %copy-done), custom_call_target="tpu_custom_call" | custom-call | flops 6442450944 | bytes 1572864 | tf_op jit(solution)/shard_map/gather_to_send/pallas_call | solution.py:85
  21.8 0.0 copy-start.1
  21.8 0.0 collective-permute-done.5
  21.9 2.2 %collective-permute-done.4 = bf16[512,256]{1,0:T(8,128)(2,1)S(1)} collective-permute-done((bf16[512,256]{1,0:T(8,128)(2,1)S(1)}, bf16[512,256]{1,0:T(8,128)(2,1)S(1)}, u32[]{:S(2)}, u32[]{:S(2)}) %collective-permute-start.4) | collective-permute-done | bytes 262176 | tf_op jit(solution)/shard_map/ppermute | solution.py:373
  24.0 0.5 collective-permute-done.3
  24.5 0.1 pad_maximum_fusion.refs_2_
  24.6 5.6 %collective-permute-start.8 = (bf16[2048,256]{1,0:T(8,128)(2,1)S(1)}, bf16[2048,256]{1,0:T(8,128)(2,1)}, u32[]{:S(2)}, u32[]{:S(2)}) collective-permute-start(bf16[2048,256]{1,0:T(8,128)(2,1)S(1)} %pad_maximum_fusion.refs_2_), channel_id=1, source_target_pairs={{0,64},{1,5},{2,66},{3,7},{4,68},{5,1},{6,70},{7,3},{8,72},{9,13},... | collective-permute-start | bytes 3145736 | tf_op jit(solution)/shard_map/ppermute | solution.py:373
  30.2 0.0 collective-permute-start.7
  30.2 2.7 %collective-permute-start.6 = (bf16[2048,256]{1,0:T(8,128)(2,1)S(1)}, bf16[2048,256]{1,0:T(8,128)(2,1)}, u32[]{:S(2)}, u32[]{:S(2)}) collective-permute-start(bf16[2048,256]{1,0:T(8,128)(2,1)S(1)} %pad_maximum_fusion.refs_2_), channel_id=1, source_target_pairs={{0,96},{1,7},{2,98},{3,1},{4,100},{5,3},{6,102},{7,5},{8,104},{9,1... | collective-permute-start | bytes 3145736 | tf_op jit(solution)/shard_map/ppermute | solution.py:373
  32.8 0.0 copy-done.1
  32.9 7.1 %gather_to_send.3 = bf16[8192,256]{1,0:T(8,128)(2,1)} custom-call(s32[8192]{0:T(1024)S(1)} %multiply_bitcast_fusion.index_hbm, bf16[2048,256]{1,0:T(8,128)(2,1)S(1)} %copy-done.1, bf16[8192,256]{1,0:T(8,128)(2,1)} %gather_to_send.2.refs_0_), custom_call_target="tpu_custom_call", output_to_operand_aliasing={{}: (2, {})} | custom-call | flops 10737418240 | bytes 2621440 | tf_op jit(solution)/shard_map/gather_to_send/pallas_call | solution.py:85
  40.0 0.0 copy-start.2
  40.0 0.0 copy-start.3
  40.0 6.2 %all-to-all-start = ((bf16[128,64,256]{2,1,0:T(8,128)(2,1)}), bf16[128,64,256]{2,1,0:T(8,128)(2,1)}, u32[]{:S(2)}, u32[]{:S(2)}) async-start(bf16[128,64,256]{2,1,0:T(8,128)(2,1)} %bitcast.23), calls=%async_computation | async-start | bytes 8388608 | tf_op jit(solution)/shard_map/all_to_all | solution.py:395
  46.2 0.0 copy-done.2
  46.2 0.1 fusion.4
  46.4 0.3 copy.14
  46.7 0.4 reshape.37.refs_0_
  47.2 12.4 %local_sums.1.refs_1_ = f32[2048,256]{1,0:T(8,128)S(1)} custom-call(s32[128,256]{1,0:T(8,128)S(1)} %reshape.37.refs_0_, bf16[2048,256]{1,0:T(8,128)(2,1)S(1)} %copy-done.1), custom_call_target="tpu_custom_call" | custom-call | flops 4294967296 | bytes 2097152 | tf_op jit(solution)/shard_map/local_sums/pallas_call | solution.py:140
  59.6 0.0 collective-permute-done.8.refs_5_
  59.6 16.0 %collective-permute-done.7.refs_4_ = bf16[2048,256]{1,0:T(8,128)(2,1)} collective-permute-done((bf16[2048,256]{1,0:T(8,128)(2,1)S(1)}, bf16[2048,256]{1,0:T(8,128)(2,1)}, u32[]{:S(2)}, u32[]{:S(2)}) %collective-permute-start.7) | collective-permute-done | bytes 1048608 | tf_op jit(solution)/shard_map/ppermute | solution.py:373
  75.6 0.0 collective-permute-done.6.refs_3_
  75.6 1.3 %broadcast_in_dim.15.refs_3_ = f32[2048,128]{1,0:T(8,128)} broadcast(f32[2048]{0:T(1024)S(1)} %add_convert_fusion), dimensions={0} | broadcast | bytes 1056768 | tf_op jit(solution)/shard_map/broadcast_in_dim | solution.py:401
  76.9 0.0 collective-permute-start.9
  76.9 0.5 collective-permute-start.10
  77.4 0.0 collective-permute-start.11
  77.4 0.5 collective-permute-start.12
  77.9 3.1 %collective-permute-done.9.refs_6_ = bf16[2048,256]{1,0:T(8,128)(2,1)S(1)} collective-permute-done((bf16[2048,256]{1,0:T(8,128)(2,1)S(1)}, bf16[2048,256]{1,0:T(8,128)(2,1)S(1)}, u32[]{:S(2)}, u32[]{:S(2)}) %collective-permute-start.9) | collective-permute-done | bytes 1048608 | tf_op jit(solution)/shard_map/ppermute | solution.py:347
  81.0 0.2 collective-permute-done.10.refs_7_
  81.3 1.5 %collective-permute-done.11.refs_8_ = bf16[2048,256]{1,0:T(8,128)(2,1)S(1)} collective-permute-done((bf16[2048,256]{1,0:T(8,128)(2,1)}, bf16[2048,256]{1,0:T(8,128)(2,1)S(1)}, u32[]{:S(2)}, u32[]{:S(2)}) %collective-permute-start.11) | collective-permute-done | bytes 1048608 | tf_op jit(solution)/shard_map/ppermute | solution.py:347
  82.8 1.5 %collective-permute-done.12.refs_9_ = bf16[2048,256]{1,0:T(8,128)(2,1)S(1)} collective-permute-done((bf16[2048,256]{1,0:T(8,128)(2,1)}, bf16[2048,256]{1,0:T(8,128)(2,1)S(1)}, u32[]{:S(2)}, u32[]{:S(2)}) %collective-permute-start.12) | collective-permute-done | bytes 1048608 | tf_op jit(solution)/shard_map/ppermute | solution.py:347
  84.3 18.6 %list_sums.1.refs_2_ = f32[4096,128]{1,0:T(8,128)} custom-call(s32[16384]{0:T(1024)S(1)} %get-tuple-element.26.refs_0_, f32[2048,256]{1,0:T(8,128)S(1)} %local_sums.1.refs_1_, bf16[2048,256]{1,0:T(8,128)(2,1)S(1)} %pad_maximum_fusion.refs_2_, bf16[2048,256]{1,0:T(8,128)(2,1)} %collective-permute-done.6.refs_3_, ...), custom_call_target="tpu_custom_call" | custom-call | flops 27000000512 | bytes 8388608 | tf_op jit(solution)/shard_map/list_sums/pallas_call | solution.py:246
  102.8 0.6 all-to-all-done
  103.5 18.4 %layer.1 = bf16[2048,256]{1,0:T(8,128)(2,1)} custom-call(s32[16384]{0:T(1024)} %get-tuple-element.24.refs_0_, bf16[8192,256]{1,0:T(8,128)(2,1)} %bitcast.11.refs_1_, f32[4096,128]{1,0:T(8,128)} %list_sums.1.refs_2_, f32[2048,128]{1,0:T(8,128)} %broadcast_in_dim.15.refs_3_, bf16[2048,256]{1,0:T(8,128)(2,1)} %refs_4_.1, bf16[512,256]{1,0:T(8,128)(2,1)} %refs_5_.1, ...), custom_call_target="tpu_custom_call" | custom-call | flops 27000000512 | bytes 4194304 | tf_op jit(solution)/shard_map/layer/pallas_call | solution.py:308
  (3 shorter events, 0.0 us)
Async XLA Ops:
  0.0 8.3 %collective-permute-start.1 = (bf16[128,256]{1,0:T(8,128)(2,1)}, bf16[128,256]{1,0:T(8,128)(2,1)S(1)}, u32[]{:S(2)}, u32[]{:S(2)}) collective-permute-start(bf16[128,256]{1,0:T(8,128)(2,1)} %param.12), channel_id=1, source_target_pairs={{0,4},{1,65},{2,6},{3,67},{4,0},{5,69},{6,2},{7,71},{8,12},{9,73},... | collective-permute-start | bytes 196616 | tf_op jit(solution)/shard_map/ppermute | solution.py:373
  3.6 4.7 %collective-permute-start = (bf16[128,256]{1,0:T(8,128)(2,1)}, bf16[128,256]{1,0:T(8,128)(2,1)S(1)}, u32[]{:S(2)}, u32[]{:S(2)}) collective-permute-start(bf16[128,256]{1,0:T(8,128)(2,1)} %param.12), channel_id=1, source_target_pairs={{0,6},{1,97},{2,0},{3,99},{4,2},{5,101},{6,4},{7,103},{8,14},{9,10... | collective-permute-start | bytes 196616 | tf_op jit(solution)/shard_map/ppermute | solution.py:373
  4.4 4.5 %collective-permute-start.2 = (bf16[128,256]{1,0:T(8,128)(2,1)}, bf16[128,256]{1,0:T(8,128)(2,1)S(1)}, u32[]{:S(2)}, u32[]{:S(2)}) collective-permute-start(bf16[128,256]{1,0:T(8,128)(2,1)} %param.12), channel_id=1, source_target_pairs={{0,2},{1,33},{2,4},{3,35},{4,6},{5,37},{6,0},{7,39},{8,10},{9,41},... | collective-permute-start | bytes 196616 | tf_op jit(solution)/shard_map/ppermute | solution.py:373
  9.8 12.0 %collective-permute-start.5 = (bf16[512,256]{1,0:T(8,128)(2,1)S(1)}, bf16[512,256]{1,0:T(8,128)(2,1)S(1)}, u32[]{:S(2)}, u32[]{:S(2)}) collective-permute-start(bf16[512,256]{1,0:T(8,128)(2,1)S(1)} %pad_maximum_fusion.1), channel_id=1, source_target_pairs={{0,8},{1,9},{2,10},{3,11},{4,12},{5,13},{6,14},{7,15},{8,16},{9,17... | collective-permute-start | bytes 786440 | tf_op jit(solution)/shard_map/ppermute | solution.py:373
  11.5 12.5 %collective-permute-start.4 = (bf16[512,256]{1,0:T(8,128)(2,1)S(1)}, bf16[512,256]{1,0:T(8,128)(2,1)S(1)}, u32[]{:S(2)}, u32[]{:S(2)}) collective-permute-start(bf16[512,256]{1,0:T(8,128)(2,1)S(1)} %pad_maximum_fusion.1), channel_id=1, source_target_pairs={{0,16},{1,17},{2,18},{3,19},{4,20},{5,21},{6,22},{7,23},{8,24},{9,... | collective-permute-start | bytes 786440 | tf_op jit(solution)/shard_map/ppermute | solution.py:373
  14.8 9.7 %collective-permute-start.3 = (bf16[512,256]{1,0:T(8,128)(2,1)S(1)}, bf16[512,256]{1,0:T(8,128)(2,1)S(1)}, u32[]{:S(2)}, u32[]{:S(2)}) collective-permute-start(bf16[512,256]{1,0:T(8,128)(2,1)S(1)} %pad_maximum_fusion.1), channel_id=1, source_target_pairs={{0,24},{1,25},{2,26},{3,27},{4,28},{5,29},{6,30},{7,31},{8,0},{9,1... | collective-permute-start | bytes 786440 | tf_op jit(solution)/shard_map/ppermute | solution.py:373
  15.6 1.2 %copy-start = (bf16[2048,256]{1,0:T(8,128)(2,1)S(1)}, bf16[2048,256]{1,0:T(8,128)(2,1)}, u32[]{:S(2)}) copy-start(bf16[2048,256]{1,0:T(8,128)(2,1)} %refs_4_.1) | copy-start | bytes 3145732
  21.8 11.0 %copy-start.1 = (bf16[2048,256]{1,0:T(8,128)(2,1)S(1)}, bf16[2048,256]{1,0:T(8,128)(2,1)}, u32[]{:S(2)}) copy-start(bf16[2048,256]{1,0:T(8,128)(2,1)} %refs_4_.1) | copy-start | bytes 3145732
  24.6 35.0 %collective-permute-start.8 = (bf16[2048,256]{1,0:T(8,128)(2,1)S(1)}, bf16[2048,256]{1,0:T(8,128)(2,1)}, u32[]{:S(2)}, u32[]{:S(2)}) collective-permute-start(bf16[2048,256]{1,0:T(8,128)(2,1)S(1)} %pad_maximum_fusion.refs_2_), channel_id=1, source_target_pairs={{0,64},{1,5},{2,66},{3,7},{4,68},{5,1},{6,70},{7,3},{8,72},{9,13},... | collective-permute-start | bytes 3145736 | tf_op jit(solution)/shard_map/ppermute | solution.py:373
  30.2 45.4 %collective-permute-start.7 = (bf16[2048,256]{1,0:T(8,128)(2,1)S(1)}, bf16[2048,256]{1,0:T(8,128)(2,1)}, u32[]{:S(2)}, u32[]{:S(2)}) collective-permute-start(bf16[2048,256]{1,0:T(8,128)(2,1)S(1)} %pad_maximum_fusion.refs_2_), channel_id=1, source_target_pairs={{0,32},{1,3},{2,34},{3,5},{4,36},{5,7},{6,38},{7,1},{8,40},{9,11},... | collective-permute-start | bytes 3145736 | tf_op jit(solution)/shard_map/ppermute | solution.py:373
  30.2 45.4 %collective-permute-start.6 = (bf16[2048,256]{1,0:T(8,128)(2,1)S(1)}, bf16[2048,256]{1,0:T(8,128)(2,1)}, u32[]{:S(2)}, u32[]{:S(2)}) collective-permute-start(bf16[2048,256]{1,0:T(8,128)(2,1)S(1)} %pad_maximum_fusion.refs_2_), channel_id=1, source_target_pairs={{0,96},{1,7},{2,98},{3,1},{4,100},{5,3},{6,102},{7,5},{8,104},{9,1... | collective-permute-start | bytes 3145736 | tf_op jit(solution)/shard_map/ppermute | solution.py:373
  40.0 6.2 %copy-start.2 = (s32[2048,16]{0,1:T(8,128)S(1)}, s32[2048,16]{0,1:T(8,128)}, u32[]{:S(2)}) copy-start(s32[2048,16]{0,1:T(8,128)} %param.15) | copy-start | bytes 393220
  40.0 6.2 %copy-start.3 = (s32[2048]{0:T(1024)S(1)}, s32[2048]{0:T(1024)}, u32[]{:S(2)}) copy-start(s32[2048]{0:T(1024)} %param.16) | copy-start | bytes 24580
  40.0 63.4 %all-to-all-start = ((bf16[128,64,256]{2,1,0:T(8,128)(2,1)}), bf16[128,64,256]{2,1,0:T(8,128)(2,1)}, u32[]{:S(2)}, u32[]{:S(2)}) async-start(bf16[128,64,256]{2,1,0:T(8,128)(2,1)} %bitcast.23), calls=%async_computation | async-start | bytes 8388608 | tf_op jit(solution)/shard_map/all_to_all | solution.py:395
  76.9 4.1 %collective-permute-start.9 = (bf16[2048,256]{1,0:T(8,128)(2,1)S(1)}, bf16[2048,256]{1,0:T(8,128)(2,1)S(1)}, u32[]{:S(2)}, u32[]{:S(2)}) collective-permute-start(bf16[2048,256]{1,0:T(8,128)(2,1)S(1)} %pad_maximum_fusion.refs_2_), channel_id=1, source_target_pairs={{0,1},{1,0},{2,3},{3,2},{4,5},{5,4},{6,7},{7,6},{8,9},{9,8},{10,11... | collective-permute-start | bytes 3145736 | tf_op jit(solution)/shard_map/ppermute | solution.py:347
  76.9 4.4 %collective-permute-start.10 = (bf16[2048,256]{1,0:T(8,128)(2,1)}, bf16[2048,256]{1,0:T(8,128)(2,1)S(1)}, u32[]{:S(2)}, u32[]{:S(2)}) collective-permute-start(bf16[2048,256]{1,0:T(8,128)(2,1)} %collective-permute-done.6.refs_3_), channel_id=1, source_target_pairs={{0,1},{1,0},{2,3},{3,2},{4,5},{5,4},{6,7},{7,6},{8,9},{9,8},{10,11... | collective-permute-start | bytes 3145736 | tf_op jit(solution)/shard_map/ppermute | solution.py:347
  77.4 5.4 %collective-permute-start.11 = (bf16[2048,256]{1,0:T(8,128)(2,1)}, bf16[2048,256]{1,0:T(8,128)(2,1)S(1)}, u32[]{:S(2)}, u32[]{:S(2)}) collective-permute-start(bf16[2048,256]{1,0:T(8,128)(2,1)} %collective-permute-done.7.refs_4_), channel_id=1, source_target_pairs={{0,1},{1,0},{2,3},{3,2},{4,5},{5,4},{6,7},{7,6},{8,9},{9,8},{10,11... | collective-permute-start | bytes 3145736 | tf_op jit(solution)/shard_map/ppermute | solution.py:347
  77.4 6.9 %collective-permute-start.12 = (bf16[2048,256]{1,0:T(8,128)(2,1)}, bf16[2048,256]{1,0:T(8,128)(2,1)S(1)}, u32[]{:S(2)}, u32[]{:S(2)}) collective-permute-start(bf16[2048,256]{1,0:T(8,128)(2,1)} %collective-permute-done.8.refs_5_), channel_id=1, source_target_pairs={{0,1},{1,0},{2,3},{3,2},{4,5},{5,4},{6,7},{7,6},{8,9},{9,8},{10,11... | collective-permute-start | bytes 3145736 | tf_op jit(solution)/shard_map/ppermute | solution.py:347
